TPU v7x, 32 devices: a whole 2x2x4 slice. The times are simulated.
32 devices in a mesh: genome: 8 (over z, x), people: 4 (over y, core).
Axes of the slice: x: 2, y: 2, z: 4, core: 2. Of those that a mesh axis runs over, the one named last changes fastest.
Arguments:
- dosages: float32 [6144, 8192], P('genome', 'people'), may hold values from 0 to 2
- annotations: int32 [6144, 128], P('genome'), may hold values from -1 to 1
Outputs:
- ld_scores: float32 [6144, 128], P(('genome', 'people'))
All inputs are finite; a program needn't handle non-finite values.
Results may differ from a plain program's by a relative error of at most 0.0003.
Values sent between devices are 32-bit elements; how exact they have to be, the bound alone decides.
No kernel may reach another device: no remote copies, remote signals or barrier semaphores. Data moves between devices by JAX's collectives and lax.ppermute only.
A program may use at most 64 MiB of HBM per device.

v0:
```python
import jax
import jax.numpy as jnp
from jax import lax
from jax.sharding import PartitionSpec as P


def shifted(block, axis, distance):
    devices = range(lax.axis_size(axis))
    route = [(i - distance, i) for i in devices if i - distance in devices]
    return lax.ppermute(block, axis, route)


def adjust(tile, people_count):
    square = tile * tile
    return square - (1.0 - square) / (people_count - 2.0)


def local(dosages, annotations):
    num_rows = dosages.shape[0]
    people_count = jnp.float32(dosages.shape[1] * lax.axis_size("people"))
    sum_dose, sum_square = lax.psum(
        (jnp.sum(dosages, axis=1), jnp.sum(dosages * dosages, axis=1)), "people"
    )
    centre = sum_dose / people_count
    spread = sum_square / people_count - centre * centre
    standard = (dosages - centre[:, None]) * lax.rsqrt(spread + 1e-06)[:, None]
    annot = annotations.astype(jnp.float32)
    blocks = [(standard, annot)]
    for step_ahead in (1, 2):
        blocks.append(shifted((standard, annot), "genome", -step_ahead))
    partial_value = [
        jnp.dot(standard, blocks[idx][0].T, precision=lax.Precision.HIGHEST) for idx in range(3)
    ]
    share_rows = num_rows // lax.axis_size("people")
    row_start = lax.axis_index("people") * share_rows
    summed = lax.psum((partial_value[0], partial_value[1], partial_value[2]), "people")
    adjusted = [adjust(tile / people_count, people_count) for tile in summed]
    forward = jnp.zeros((share_rows, annot.shape[1]), jnp.float32)
    for idx in range(3):
        mine = lax.dynamic_slice_in_dim(adjusted[idx], row_start, share_rows, 0)
        forward = forward + jnp.dot(mine, blocks[idx][1], precision=lax.Precision.HIGHEST)
    backs = []
    for idx in (1, 2):
        whole_back = jnp.dot(adjusted[idx].T, annot, precision=lax.Precision.HIGHEST)
        backs.append(lax.dynamic_slice_in_dim(whole_back, row_start, share_rows, 0))
    result = forward
    for step_back, returned in ((1, backs[0]), (2, backs[1])):
        result = result + shifted(returned, "genome", step_back)
    return result


def solution(mesh):
    in_specs = (P("genome", "people"), P("genome", None))
    out_specs = P(("genome", "people"), None)
    return jax.shard_map(local, mesh=mesh, in_specs=in_specs, out_specs=out_specs, check_vma=False)
```

profile of v0, /device:TPU:23, one launch (start us, length us, event | category | flops | bytes accessed | tf_op | source)
XLA Modules:
  0.0 471.0 jit_solution(2158784146336334676)
XLA Ops:
  6.5 0.0 all-reduce.4.cloned.1.call-start
  6.5 3.7 fusion.24
  10.2 5.8 %all-reduce = (f32[768]{0:T(1024)S(1)}, f32[768]{0:T(1024)S(1)}) all-reduce(f32[768]{0:T(1024)S(1)} %get-tuple-element.6, f32[768]{0:T(1024)S(1)} %get-tuple-element.5), channel_id=1, replica_groups=mesh['genome'=8,'people'=4] {'people'}, use_global_device_ids=true, to_apply=%region_3.0 | all-reduce | flops 1536 | bytes 12288 | tf_op jit(solution)/shard_map/psum | solution.py:21
  16.1 3.4 subtract_multiply_fusion
  19.5 2.2 collective-permute-start
  21.6 2.3 collective-permute-start.2
  23.9 16.2 %fusion.25 = f32[768,768]{1,0:T(8,128)} fusion(f32[768,2048]{1,0:T(8,128)S(1)} %subtract_multiply_fusion), kind=kOutput, calls=%fused_computation.35 | convolution fusion | flops 14495514624 | bytes 8650752 | tf_op jit(solution)/shard_map/dot_general | solution.py:32
  40.1 118.4 %collective-permute-done = f32[768,2048]{1,0:T(8,128)S(1)} collective-permute-done((f32[768,2048]{1,0:T(8,128)S(1)}, f32[768,2048]{1,0:T(8,128)S(1)}, u32[]{:S(2)}, u32[]{:S(2)}) %collective-permute-start) | collective-permute-done | bytes 6291488 | tf_op jit(solution)/shard_map/ppermute | solution.py:10
  158.5 16.2 %fusion.26 = f32[768,768]{1,0:T(8,128)} fusion(f32[768,2048]{1,0:T(8,128)S(1)} %subtract_multiply_fusion, f32[768,2048]{1,0:T(8,128)S(1)} %collective-permute-done), kind=kOutput, calls=%fused_computation.36 | convolution fusion | flops 14495514624 | bytes 14942208 | tf_op jit(solution)/shard_map/dot_general | solution.py:32
  174.7 0.0 collective-permute-done.2
  174.7 16.2 %fusion.27 = f32[768,768]{1,0:T(8,128)} fusion(f32[768,2048]{1,0:T(8,128)S(1)} %subtract_multiply_fusion, f32[768,2048]{1,0:T(8,128)S(1)} %collective-permute-done.2), kind=kOutput, calls=%fused_computation.37 | convolution fusion | flops 14495514624 | bytes 14942208 | tf_op jit(solution)/shard_map/dot_general | solution.py:32
  190.8 0.0 copy-start.1
  190.8 0.0 all-reduce.4.cloned.1.call-update
  190.9 1.0 copy-done.1
  191.9 120.8 %collective-permute-start.1 = (f32[768,128]{1,0:T(8,128)S(1)}, f32[768,128]{1,0:T(8,128)S(1)}, u32[]{:S(2)}, u32[]{:S(2)}) collective-permute-start(f32[768,128]{1,0:T(8,128)S(1)} %convert_element_type.3), channel_id=1, source_target_pairs={{4,0},{8,4},{12,8},{16,12},{20,16},{24,20},{28,24},{5,1},{9,5},{13... | collective-permute-start | bytes 1179656 | tf_op jit(solution)/shard_map/ppermute | solution.py:10
  312.7 2.1 collective-permute-start.3
  314.8 127.2 %all-reduce.4.cloned.1.call-done = (f32[768,768]{1,0:T(8,128)}, f32[768,768]{1,0:T(8,128)}, f32[768,768]{1,0:T(8,128)}) async-done(((f32[768,768]{1,0:T(8,128)}, f32[768,768]{1,0:T(8,128)}, f32[768,768]{1,0:T(8,128)}), (f32[768,768]{1,0:T(8,128)}, f32[768,768]{1,0:T(8,128)}, f32[768,768]{1,0:T(8,128)})) %all-reduce.4.cloned.1.call-update) | async-done | bytes 7077904 | tf_op jit(solution)/shard_map/psum | solution.py:36
  442.1 0.0 copy-start
  442.1 5.8 %fusion.18 = f32[768,128]{1,0:T(8,128)S(1)} fusion(s32[768,128]{1,0:T(8,128)S(1)} %copy-done.1, f32[768,768]{1,0:T(8,128)} %get-tuple-element.10), kind=kOutput, calls=%fused_computation.28 | convolution fusion | flops 909017088 | bytes 3145728 | tf_op jit(solution)/shard_map/dot_general | solution.py:44
  447.9 0.0 copy-done
  447.9 2.5 multiply_subtract_fusion
  450.3 4.0 fusion.16
  454.3 3.1 collective-permute-start.4
  457.5 1.9 collective-permute-start.5
  459.4 1.8 fusion.5
  461.2 0.0 collective-permute-done.1
  461.2 0.6 convolution_add_fusion.1
  461.8 0.0 collective-permute-done.3
  461.8 0.0 collective-permute-done.4
  461.9 1.0 collective-permute-done.5
  462.8 1.3 fusion.1
  (4 shorter events, 0.1 us)
Async XLA Ops:
  6.5 435.5 %all-reduce.4.cloned.1.call-start = ((), (), s32[]{:S(2)}) async-start(), calls=%async_computation | async-start | bytes 14155776 | tf_op jit(solution)/shard_map/psum | solution.py:36
  19.5 139.0 %collective-permute-start = (f32[768,2048]{1,0:T(8,128)S(1)}, f32[768,2048]{1,0:T(8,128)S(1)}, u32[]{:S(2)}, u32[]{:S(2)}) collective-permute-start(f32[768,2048]{1,0:T(8,128)S(1)} %subtract_multiply_fusion), channel_id=1, source_target_pairs={{4,0},{8,4},{12,8},{16,12},{20,16},{24,20},{28,24},{5,1},{9,5},{13... | collective-permute-start | bytes 18874376 | tf_op jit(solution)/shard_map/ppermute | solution.py:10
  21.6 153.0 %collective-permute-start.2 = (f32[768,2048]{1,0:T(8,128)S(1)}, f32[768,2048]{1,0:T(8,128)S(1)}, u32[]{:S(2)}, u32[]{:S(2)}) collective-permute-start(f32[768,2048]{1,0:T(8,128)S(1)} %subtract_multiply_fusion), channel_id=1, source_target_pairs={{8,0},{12,4},{16,8},{20,12},{24,16},{28,20},{9,1},{13,5},{17,9},{2... | collective-permute-start | bytes 18874376 | tf_op jit(solution)/shard_map/ppermute | solution.py:10
  190.8 1.0 copy-start.1
  191.9 269.3 %collective-permute-start.1 = (f32[768,128]{1,0:T(8,128)S(1)}, f32[768,128]{1,0:T(8,128)S(1)}, u32[]{:S(2)}, u32[]{:S(2)}) collective-permute-start(f32[768,128]{1,0:T(8,128)S(1)} %convert_element_type.3), channel_id=1, source_target_pairs={{4,0},{8,4},{12,8},{16,12},{20,16},{24,20},{28,24},{5,1},{9,5},{13... | collective-permute-start | bytes 1179656 | tf_op jit(solution)/shard_map/ppermute | solution.py:10
  312.7 149.1 %collective-permute-start.3 = (f32[768,128]{1,0:T(8,128)S(1)}, f32[768,128]{1,0:T(8,128)S(1)}, u32[]{:S(2)}, u32[]{:S(2)}) collective-permute-start(f32[768,128]{1,0:T(8,128)S(1)} %convert_element_type.3), channel_id=1, source_target_pairs={{8,0},{12,4},{16,8},{20,12},{24,16},{28,20},{9,1},{13,5},{17,9},{2... | collective-permute-start | bytes 1179656 | tf_op jit(solution)/shard_map/ppermute | solution.py:10
  442.1 5.8 %copy-start = (f32[768,768]{1,0:T(8,128)S(1)}, f32[768,768]{1,0:T(8,128)}, u32[]{:S(2)}) copy-start(f32[768,768]{1,0:T(8,128)} %get-tuple-element.9) | copy-start | bytes 7077892
  454.3 7.5 %collective-permute-start.4 = (f32[192,128]{1,0:T(8,128)S(1)}, f32[192,128]{1,0:T(8,128)S(1)}, u32[]{:S(2)}, u32[]{:S(2)}) collective-permute-start(f32[192,128]{1,0:T(8,128)S(1)} %constant_dynamic-slice_fusion.1), channel_id=1, source_target_pairs={{0,4},{4,8},{8,12},{12,16},{16,20},{20,24},{24,28},{1,5},{5,9},{9,... | collective-permute-start | bytes 294920 | tf_op jit(solution)/shard_map/ppermute | solution.py:10
  457.5 5.4 %collective-permute-start.5 = (f32[192,128]{1,0:T(8,128)S(1)}, f32[192,128]{1,0:T(8,128)S(1)}, u32[]{:S(2)}, u32[]{:S(2)}) collective-permute-start(f32[192,128]{1,0:T(8,128)S(1)} %constant_dynamic-slice_fusion), channel_id=1, source_target_pairs={{0,8},{4,12},{8,16},{12,20},{16,24},{20,28},{1,9},{5,13},{9,17},{1... | collective-permute-start | bytes 294920 | tf_op jit(solution)/shard_map/ppermute | solution.py:10
Sparse Core Ops, SparseCore 0:
  191.0 251.0 all-reduce.3
where the time goes:
time: 474 us; the launch traced here: 471 us
  waiting for transfers between devices  247 us (52%)
  starting transfers between devices  132 us (28%)
  matrix products  62 us (13%)
  between operations  13.6 us (3%)
  other arithmetic  9.56 us (2%)
  blocking collectives  5.84 us (1%)
    ppermute x6, starting transfers between devices, shifted(): return lax.ppermute(block, axis, route)  132 us
    psum x1, waiting for transfers between devices, local(): lax.psum((partial_value[0], partial_value[1], partial_value[2]), 'people')  127 us
    ppermute x6, waiting for transfers between devices, shifted(): return lax.ppermute(block, axis, route)  119 us
    dot_general x3, matrix products, local(): jnp.dot(standard, blocks[idx][0].T, precision=lax.Precision.HIGHEST)  48.6 us
    dot_general x2, matrix products, local(): jnp.dot(adjusted[idx].T, annot, precision=lax.Precision.HIGHEST)  9.75 us
  transfers between devices with their start and end apart: 7, of which 3 were waited for; matrix products, arithmetic and copies ran while one was open for 10% of the time, Pallas kernels for 0%

commit v1 on v0

v1 whole, which is shorter than its diff:
```python
import functools

import jax
import jax.numpy as jnp
from jax import lax
from jax.experimental import pallas as pl
from jax.experimental.pallas import tpu as pltpu
from jax.sharding import PartitionSpec as P

AXES = ("genome", "people")
WIDTHS = (128, 128, 64, 64)
PHASES = ((0, 1), (2, 3))
LANES = 128
F32 = jnp.float32
BF16 = jnp.bfloat16
MIB = 1024 * 1024


def adjust(tile, people_count):
    square = tile * tile
    return square - (1.0 - square) / (people_count - 2.0)


def dot(a, b, dims):
    return lax.dot_general(a, b, (dims, ((), ())), preferred_element_type=F32)


def gram(ah, al, bh, bl):
    last = ((1,), (1,))
    return dot(ah, bh, last) + (dot(ah, bl, last) + dot(al, bh, last))


def split_pair(value):
    high = value.astype(BF16)
    return high, (value - high.astype(F32)).astype(BF16)


VMEM, SMEM, HBM = pltpu.VMEM, pltpu.SMEM, pltpu.HBM


def call(kernel, ins, outs, scratch=(), room=8, flops=0, moved=0, aliases={}):
    arrays = [a if m in (None, SMEM) else pltpu.with_memory_space_constraint(a, m) for m, a in ins]
    return pl.pallas_call(
        kernel,
        out_shape=[m(s, d) if m else jax.ShapeDtypeStruct(s, d) for s, d, m in outs],
        in_specs=[pl.BlockSpec(memory_space=m or VMEM) for m, _ in ins],
        out_specs=[pl.BlockSpec(memory_space=m or VMEM) for _, _, m in outs],
        scratch_shapes=list(scratch),
        input_output_aliases=aliases,
        compiler_params=pltpu.CompilerParams(vmem_limit_bytes=room * MIB),
        cost_estimate=pl.CostEstimate(flops=flops, bytes_accessed=moved, transcendentals=0),
    )(*arrays)


class Copies:
    def __init__(self, sems):
        self.sems, self.count, self.open = sems, 0, {}

    def start(self, name, src, dst):
        copy = pltpu.make_async_copy(src, dst, self.sems.at[self.count])
        self.count += 1
        copy.start()
        self.open.setdefault(name, []).append(copy)

    def wait(self, name):
        for copy in self.open.pop(name):
            copy.wait()


class Part:
    def __init__(self, at, w):
        self.at, self.w, self.m = at, w, at // LANES
        self.last = (at + w) % LANES == 0
        self.earlier = range(self.m * LANES, at, w)
        n = self.m
        self.pieces = [(False, at, j * LANES) for j in range(n)] + [(True, at, j * LANES) for j in range(n)]
        if self.last:
            self.pieces += [(False, n * LANES + u, n * LANES) for u in range(0, LANES, w)]


def centre_rows(read, write, count, col, squares=False):
    width = read.width
    groups = width // LANES
    rows = slice(0, count)

    @pl.loop(0, count // 16)
    def _(i):
        at = pl.multiple_of(i * 16, 16)
        parts = [read(at, g) for g in range(groups)]
        while len(parts) > 1:
            parts = [a + b for a, b in zip(parts[::2], parts[1::2])]
        col[0, pl.ds(at, 16), :] = parts[0]

    spread = lambda value: jnp.broadcast_to(jnp.sum(value, axis=1, keepdims=True), (count, LANES))
    col[0, rows] = spread(col[0, rows]) * (1.0 / width)

    @pl.loop(0, count // 16)
    def _(i):
        at = pl.multiple_of(i * 16, 16)
        mean = col[0, pl.ds(at, 16), :]
        total = jnp.zeros((16, LANES), F32)
        for g in range(groups):
            value = read(at, g) - mean
            write(at, g, *split_pair(value))
            if squares:
                total += value * value
        if squares:
            col[1, pl.ds(at, 16), :] = total

    if squares:
        col[1, rows] = spread(col[1, rows])


class Rows:
    def __init__(self, ref, index, first):
        self.ref, self.index, self.first, self.width = ref, index, first, ref.shape[-1]

    def where(self, at, g):
        return *self.index, pl.ds(pl.multiple_of(self.first + at, 16), 16), slice(g * LANES, (g + 1) * LANES)

    def __call__(self, at, g):
        return self.ref[self.where(at, g)]

    def store(self, at, g, value):
        self.ref[self.where(at, g)] = value


def store_pair(high, low):
    def write(at, g, h, l):
        high.store(at, g, h)
        low.store(at, g, l)

    return write


X, Z = 0, 1


def own_kernel(parts, role, dose_hbm, *refs):
    refs = list(refs)
    take = lambda n: [refs.pop(0) for _ in range(n)]
    high_hbm, low_hbm, keep_hbm, send_hbm, moments = take(5)
    raw_hbm = take(len(parts) - 1)
    dose, high, low, tile, col, sems = refs
    c = role[1]
    blocks, size = high.shape[0], high.shape[1]
    half = blocks * LANES
    copies = Copies(sems)
    cut = lambda i: slice(i * size, (i + 1) * size)
    for i in range(blocks):
        copies.start(i, dose_hbm.at[cut(i)], dose.at[cut(i)])
    for i in range(blocks):
        copies.wait(i)
        for b in range(2):
            n = 2 * i + b
            target = [Rows(ref, (i,), b * LANES) for ref in (high, low)]
            centre_rows(Rows(dose, (), n * LANES), store_pair(*target), LANES, col, True)
            moments[n:n + 1] = col[0].T[0:1]
            moments[2 * blocks + n:2 * blocks + n + 1] = col[1].T[0:1]
        copies.start("out", high.at[i], high_hbm.at[i])
        copies.start("out", low.at[i], low_hbm.at[i])
    for part, there in zip(parts[1:], raw_hbm):
        for a in range(2):
            first = a * half + part.at
            copies.start("out", dose.at[first:first + part.w], there.at[a])

    @pl.loop(0, blocks)
    def _(i):
        at_i = pl.ds(pl.multiple_of(i * size, size), size)

        @pl.loop(0, i + 1)
        def _(j):
            at_j = pl.ds(pl.multiple_of(j * size, size), size)
            tile[at_i, at_j] = gram(high[i], low[i], high[j], low[j])

    for i in range(blocks):
        for j in range(i):
            tile[cut(j), cut(i)] = tile[cut(i), cut(j)].T
    quarter = half // 2
    for chip in range(2):
        for core, there in ((c, keep_hbm), (1 - c, send_hbm)):
            first = pl.multiple_of((2 * chip + core) * quarter, quarter)
            copies.start("out", tile.at[pl.ds(first, quarter)], there.at[chip])
    copies.wait("out")


def chunk_kernel(part, first, role, raw_z, raw_x, own_h_hbm, own_l_hbm, *refs):
    if not first:
        refs = refs[2:]
    outs, refs = refs[:4], refs[4:]
    high, low, strips, squares, left_h, left_l, col, own_h, own_l, keep_a, send_a, keep_db, send_db, sems = refs
    y, c = role[0], role[1]
    w, m = part.w, part.m
    off = part.at - m * LANES
    blocks = own_h.shape[0]
    half = blocks * LANES

    def own_copies(i):
        return [pltpu.make_async_copy(there.at[i], here.at[i], sems.at[i, n])
                for n, (there, here) in enumerate(((own_h_hbm, own_h), (own_l_hbm, own_l)))]

    for i in range(blocks):
        for copy in own_copies(i):
            copy.start()
    for name, raw in ((X, raw_x), (Z, raw_z)):
        for a in range(2):
            target = [Rows(ref, (name, m), a * LANES + off) for ref in (high, low)]
            also = [Rows(ref, (), (2 * name + a) * w) for ref in (left_h, left_l)]

            def write(at, g, h, l, target=target, also=also):
                store_pair(*target)(at, g, h, l)
                store_pair(*also)(at, g, h, l)

            centre_rows(Rows(raw, (a,), 0), write, w, col)

    @pl.loop(0, blocks)
    def _(i):
        for copy in own_copies(i):
            copy.wait()
        strips[i] = gram(left_h[...], left_l[...], own_h[i], own_l[i])

    if m:
        @pl.loop(0, 2 * m)
        def _(t):
            turned = t >= m
            at = pl.ds(pl.multiple_of(jnp.where(turned, X, Z) * 2 * w, 2 * w), 2 * w)
            right = jnp.where(turned, Z, X)
            j = jnp.where(turned, t - m, t)
            squares[t, 0:2 * w] = gram(left_h[at], left_l[at], high[right, j], low[right, j])
    if part.last:
        squares[2 * m] = gram(high[Z, m], low[Z, m], high[X, m], low[X, m])

    def rows(at, count):
        return pl.ds(pl.multiple_of(at, 16), count)

    def lanes(j):
        return pl.ds(pl.multiple_of(j * LANES, LANES), LANES)

    copies = Copies(sems.at[blocks])
    for which, out_a, out_db in ((1 - y, send_a, send_db), (y, keep_a, keep_db)):
        for t in range(2):
            s, f = jnp.where(c == 0, which, t), jnp.where(c == 0, t, which)
            for name, out in ((Z, out_a), (X, out_db)):
                for j in range(blocks):
                    group = f * blocks + j
                    at = rows((2 * name + s) * w, w)
                    out[t, :, j * LANES:(j + 1) * LANES] = strips[group // 2, at, lanes(group % 2)]
            at = half
            for b in range(2 * m):
                i, j = (f, s) if b >= m else (s, f)
                out_db[t, :, at:at + LANES] = squares[b, rows(i * w, w), lanes(j)]
                at += LANES
            if part.last:
                for u in range(0, LANES, w):
                    out_db[t, :, at:at + LANES] = squares[2 * m, rows(s * LANES + u, w), lanes(f)]
                    at += LANES
    for here, there in zip((keep_a, send_a, keep_db, send_db), outs):
        copies.start("out", here, there)
    copies.wait("out")


def load_sums(copies, t, parts, ins, held):
    for k, _ in enumerate(parts):
        for i in range(4):
            copies.start("sums", ins[k][i].at[t], held[k][i])


def sum_kernel(parts, role, *refs):
    refs = list(refs)
    take = lambda n: [refs.pop(0) for _ in range(n)]
    ins = [take(4) for _ in parts]
    out_a, out_d, out_b = take(3)
    held = [take(4) for _ in parts]
    y, c = role[0], role[1]
    copies = Copies(*refs)
    load_sums(copies, jnp.where(c == 0, 1 - y, y), parts, ins, held)
    copies.wait("sums")
    row, row_b = 0, 0
    for part, (keep_a, got_a, keep_db, got_db) in zip(parts, held):
        half, w = keep_a.shape[1], part.w
        out_a[row:row + w] = keep_a[...] + got_a[...]
        out_d[row:row + w] = keep_db[:, :half] + got_db[:, :half]
        for i in range(len(part.pieces)):
            cut = slice(half + i * LANES, half + (i + 1) * LANES)
            out_b[row_b + i * w:row_b + (i + 1) * w] = keep_db[:, cut] + got_db[:, cut]
        row += w
        row_b += w * len(part.pieces)


def correlation(tile, offsets_r, scale_r, offsets_c, scale_c, width, people_count):
    between = lax.dot_general(
        offsets_r, offsets_c, (((0,), (0,)), ((), ())), precision=lax.Precision.HIGHEST, preferred_element_type=F32
    )
    column = jnp.broadcast_to(scale_r, (8, scale_r.shape[1])).T[:, 0:1]
    return (tile + width * between) * column * scale_c / people_count


def annotated(tile, annot, dims):
    high, low = split_pair(tile)
    annot = annot.astype(BF16)
    return dot(high, annot, dims) + dot(low, annot, dims)


TO_F, TO_S = ((0,), (0,)), ((1,), (0,))


def diagonal_kernel(width, people_count, tile, tile_pair, stats_rows, stats, annot, out):
    corr = correlation(
        tile[...] + tile_pair[...], stats_rows[0:8], stats_rows[8:9], stats[0:8], stats[8:9], width, people_count
    )
    out[...] = annotated(adjust(corr, people_count), annot[...], TO_S)


def final_kernel(width, people_count, phases, role, *refs):
    refs = list(refs)
    take = lambda n: [refs.pop(0) for _ in range(n)]
    every = [part for parts in phases for part in parts]
    ins = [take(4) for _ in every]
    data = [(parts, take(3)) for parts in phases]
    own, x, z = take(2), take(2), take(2)
    res_own, res_x, res_b, res_z = take(4)
    quad, turned_quad = take(2)
    held = [take(4) for _ in every]
    y, c = role[0], role[1]
    half = quad.shape[0]
    s_keep = jnp.where(c == 0, y, 1 - y)
    copies = Copies(*refs)
    load_sums(copies, s_keep, every, ins, held)
    copies.wait("sums")

    def half_of(block, h):
        rows = pl.ds(pl.multiple_of(h * half, half), half)
        return block[0][rows, :], block[1][0:8, rows], block[1][8:9, rows]

    def fill(n, s_side, f_side):
        if n == 2:
            quad[...] = jnp.zeros_like(quad)
            turned_quad[...] = jnp.zeros_like(turned_quad)
        for part, (keep_a, got_a, keep_db, got_db) in zip(every, held):
            rows = slice(part.at, part.at + part.w)
            if n == 0:
                quad[rows] = keep_a[...] + got_a[...]
            elif n == 1:
                quad[rows] = keep_db[:, :half] + got_db[:, :half]
            else:
                for i, (turned, row, at) in enumerate(part.pieces):
                    cut = slice(half + i * LANES, half + (i + 1) * LANES)
                    mine = turned_quad if turned else quad
                    mine[row:row + part.w, at:at + LANES] += keep_db[:, cut] + got_db[:, cut]
        for parts, got in data:
            if n < 2:
                turned_quad[parts[0].at:parts[-1].at + parts[-1].w] = got[n][...]
                continue
            cut = 0
            for part in parts:
                for turned, row, at in part.pieces:
                    theirs = quad if turned else turned_quad
                    theirs[row:row + part.w, at:at + LANES] += got[2][cut:cut + part.w]
                    cut += part.w
        corr = correlation(quad[...] + turned_quad[...].T, *s_side[1:], *f_side[1:], width, people_count)
        return adjust(corr, people_count)

    own_f, x_f = half_of(own, y), half_of(x, y)
    x_s, z_s = half_of(x, s_keep), half_of(z, s_keep)
    adj = fill(0, z_s, own_f)
    res_own[...] = annotated(adj, z_s[0], TO_F)
    res_z[...] = annotated(adj, own_f[0], TO_S)
    adj = fill(1, x_s, own_f)
    res_own[...] += annotated(adj, x_s[0], TO_F)
    res_x[...] = annotated(adj, own_f[0], TO_S)
    adj = fill(2, z_s, x_f)
    back = annotated(adj, z_s[0], TO_F)
    res_b[...] = back
    res_x[...] += jnp.where(c == 0, back, 0.0)
    res_z[...] += annotated(adj, x_f[0], TO_S)


def route(groups, fn):
    pairs = []
    for g in range(groups):
        for y in range(2):
            for c in range(2):
                to = fn(g, y, c)
                if to is not None and 0 <= to[0] < groups:
                    pairs.append((g * 4 + y * 2 + c, to[0] * 4 + to[1] * 2 + to[2]))
    return pairs


def local(dosages, annotations):
    groups = lax.axis_size("genome")
    rows, width = dosages.shape
    half = rows // 2
    assert sum(WIDTHS) == half
    parts = [Part(sum(WIDTHS[:k]), w) for k, w in enumerate(WIDTHS)]
    cats = annotations.shape[1]
    total = width * lax.axis_size("people")
    people_count = jnp.float32(total)
    p = lax.axis_index("people")
    y, c = p // 2, p % 2
    role = jnp.stack([y, c]).astype(jnp.int32)

    def meets(g, c):
        return g % 2 == c

    step = lambda c: 1 - 2 * c
    kept = lambda y, c: y if c == 0 else 1 - y
    routes = dict(
        x=route(groups, lambda g, y, c: (g - step(c), y, c) if not meets(g, c) else None),
        z=route(groups, lambda g, y, c: (g - 2 * step(c), y, c)),
        y=route(groups, lambda g, y, c: (g, 1 - y, c)),
        y_meet=route(groups, lambda g, y, c: (g, 1 - y, c) if meets(g, c) else None),
        pair_d=route(groups, lambda g, y, c: (g + step(c), y, 1 - c) if meets(g, c) else None),
        pair_a=route(groups, lambda g, y, c: (g + 2 * step(c), y, 1 - c)),
        pair_b=route(groups, lambda g, y, c: (g + 3 * step(c), y, 1 - c) if meets(g, c) else None),
        core=route(groups, lambda g, y, c: (g, y, 1 - c)),
        res_x=route(groups, lambda g, y, c: (g + step(c), kept(y, c), c) if meets(g, c) else None),
        res_b=route(groups, lambda g, y, c: (g + step(c), y, 0) if meets(g, c) and c == 1 else None),
        res_z=route(groups, lambda g, y, c: (g + 2 * step(c), kept(y, c), c)),
    )

    def send(value, name):
        return lax.ppermute(value, AXES, routes[name])

    raw_0 = dosages.reshape(2, half, width)[:, :parts[0].w]
    raw = [raw_0]
    stage = lax.optimization_barrier

    def send_block(k):
        return send(raw[k], "x"), send(raw[k], "z")

    col = VMEM((2, LANES, LANES), F32)
    stack = (rows // (2 * LANES), 2 * LANES, width)
    wide = (2, *stack)
    dma = pltpu.SemaphoreType.DMA

    def run_chunk(k, got, own, old):
        part = parts[k]
        w, n_b = part.w, len(part.pieces) * LANES
        shapes = [(2, w, half)] * 2 + [(2, w, half + n_b)] * 2
        size = 2 * LANES
        *outs, high, low = call(
            functools.partial(chunk_kernel, part, k == 0),
            [(SMEM, role), (None, got[1]), (None, got[0])] + [(HBM, t) for t in own] + [(VMEM, t) for t in old],
            [(s, F32, HBM) for s in shapes] + [(wide, BF16, VMEM)] * 2,
            [VMEM((stack[0], 4 * w, size), F32), VMEM((2 * part.m + 1, size, size), F32)]
            + [VMEM((4 * w, width), BF16)] * 2 + [col] + [VMEM(stack, BF16)] * 2
            + [VMEM(s, F32) for s in shapes] + [dma((stack[0] + 1, 4))],
            room=24, flops=1, moved=1,
            aliases={5: 4, 6: 5} if k else {},
        )
        return outs, (high, low)

    def send_pair(outs):
        return outs[0], send(outs[1], "y"), outs[2], send(outs[3], "y_meet")

    def held(part):
        n_b = len(part.pieces) * LANES
        return [VMEM((part.w, half), F32)] * 2 + [VMEM((part.w, half + n_b), F32)] * 2

    def run_sum(chunk):
        phase = [parts[k] for k in chunk]
        n_rows = sum(part.w for part in phase)
        shapes = [(n_rows, half)] * 2 + [(sum(part.w * len(part.pieces) for part in phase), LANES)]
        outs = call(
            functools.partial(sum_kernel, phase), [(SMEM, role)] + [(HBM, t) for k in chunk for t in pairs[k]],
            [(s, F32, None) for s in shapes], [t for part in phase for t in held(part)] + [dma((4 * len(phase),))],
            room=10, flops=n_rows * half, moved=12 * n_rows * half,
        )
        return [send(v, n) for v, n in zip(outs, ("pair_a", "pair_d", "pair_b"))]

    got = send_block(0)
    shared = ((2, rows // 4, rows), F32, HBM)
    outs = call(
        functools.partial(own_kernel, parts), [(SMEM, role), (HBM, dosages)],
        [(stack, BF16, HBM)] * 2 + [shared] * 2 + [((2 * rows // LANES, LANES), F32, None)]
        + [((2, part.w, width), F32, HBM) for part in parts[1:]],
        [VMEM((rows, width), F32)] + [VMEM(stack, BF16)] * 2 + [VMEM((rows, rows), F32), col, dma((24,))],
        room=24, flops=4 * rows * rows * width, moved=4 * rows * width,
    )
    own, keep_0, send_0, moments, raw = outs[:2], outs[2], outs[3], outs[4], [raw_0, *outs[5:]]
    own, keep_0, send_0, moments, raw = stage((own, keep_0, send_0, moments, raw))

    both = keep_0 + send(send_0, "core")
    pick = lambda value, i: lax.dynamic_index_in_dim(value, i, 0, keepdims=False)
    tile0_own, tile0_send = pick(both, y), pick(both, 1 - y)

    moments = moments.reshape(1, 2, rows)
    moments = jnp.concatenate([moments, send(moments, "core")])
    moments = jnp.concatenate([moments, send(moments, "y")])
    centre = jnp.sum(moments[:, 0], axis=0) / moments.shape[0]
    offsets = moments[:, 0] - centre
    spread = (jnp.sum(moments[:, 1], axis=0) + width * jnp.sum(offsets * offsets, axis=0)) / people_count
    scale = lax.rsqrt(spread + 1e-06)
    annot = annotations.astype(F32)
    stats = jnp.concatenate([offsets, jnp.zeros((8 - offsets.shape[0], rows), F32), scale[None]], axis=0)
    side = jnp.concatenate([annot, stats.reshape(-1, LANES)], axis=0)
    got, own, raw, tile0_own, tile0_send, annot, stats, side = stage(
        (got, own, raw, tile0_own, tile0_send, annot, stats, side)
    )

    pairs, old = [], []
    n_parts = len(parts)
    tile0_came = send(tile0_send, "y")
    for k in range(n_parts):
        coming = send_block(k + 1) if k + 1 < n_parts else ()
        if k == n_parts - 1:
            side = [send(side, name) for name in "xz"]
        outs, old = run_chunk(k, got, own, old)
        pair = send_pair(outs)
        if k:
            last = pairs.pop()
            got, raw, old, last, own, side = stage((coming, raw, old, last, own, side))
            pairs.append(last)
        else:
            got, raw, old, own, side, tile0_came = stage((coming, raw, old, own, side, tile0_came))
        pairs.append(pair)
    tile0 = tile0_own, tile0_came
    came = side
    pairs[:3], _ = stage((pairs[:3], old))
    received = [run_sum(chunk) for chunk in PHASES]
    sides = [(annot, stats)] + [(t[:rows], t[rows:].reshape(stats.shape)) for t in came]

    phases = [[parts[k] for k in chunk] for chunk in PHASES]
    res = ((half, cats), F32, None)
    res_own, res_x, res_b, res_z = call(
        functools.partial(final_kernel, float(width), float(total), phases),
        [(SMEM, role)] + [(HBM, t) for pair in pairs for t in pair]
        + [(None, t) for group in received + sides for t in group],
        [res] * 4, [VMEM((half, half), F32)] * 2 + [t for part in parts for t in held(part)] + [dma((4 * n_parts,))],
        room=16, flops=24 * half * half * cats, moved=32 * half * half,
    )
    stats_rows = lax.dynamic_slice_in_dim(stats, p * (rows // 4), rows // 4, 1)
    (res_0,) = call(
        functools.partial(diagonal_kernel, float(width), float(total)),
        [(None, t) for t in (*tile0, stats_rows, stats, annot)], [((rows // 4, cats), F32, None)],
        flops=4 * rows * rows * cats, moved=rows * rows,
    )
    arrived = res_own + send(res_x, "res_x") + send(res_b, "res_b") + send(res_z, "res_z")
    arrived = arrived.reshape(2, half // 2, cats)
    choose = lambda index: lax.dynamic_index_in_dim(arrived, index, 0, keepdims=False)
    return choose(c) + send(choose(1 - c), "core") + res_0


def solution(mesh):
    in_specs = (P("genome", "people"), P("genome", None))
    out_specs = P(("genome", "people"), None)
    return jax.shard_map(local, mesh=mesh, in_specs=in_specs, out_specs=out_specs, check_vma=False)
```

time: 474 us -> 193 us (0.41)
  waiting for transfers between devices: 247 us -> 38.3 us
  Pallas kernels: 0 us -> 76.5 us
  starting transfers between devices: 132 us -> 62.8 us
  matrix products: 62 us -> 0 us
  between operations: 13.6 us -> 0.65 us
  local copies, waits for them, and re-layouts: 1.01 us -> 9.53 us
  blocking collectives: 5.84 us -> 0 us
  other arithmetic: 9.56 us -> 3.82 us
    psum x1 -> x0, waiting for transfers between devices: 127 us -> none  [local(): lax.psum((partial_value[0], partial_value[1], partial_value[2]), 'people')]
    ppermute x6 -> x32, waiting for transfers between devices: 119 us -> 38.3 us  [send(): return lax.ppermute(value, AXES, routes[name])]
    pallas_call x0 -> x9, Pallas kernels: none -> 76.5 us  [call(): pl.pallas_call(kernel, out_shape=[m(s, d) if m else jax.ShapeDtypeStruct(...]
    ppermute x6 -> x32, starting transfers between devices: 132 us -> 62.8 us  [send(): return lax.ppermute(value, AXES, routes[name])]
    dot_general x8 -> x0, matrix products: 62 us -> none  [the longest x3 48.6 us: local(): jnp.dot(standard, blocks[idx][0].T, precision=lax.Precision.HIGHEST)]
    psum x1 -> x0, blocking collectives: 5.84 us -> none  [local(): lax.psum((jnp.sum(dosages, axis=1), jnp.sum(dosages * dosages, axis=1)),...]
  transfers between devices with their start and end apart: 7 -> 32, of which waited for: 3 -> 16; matrix products, arithmetic and copies ran while one was open for 10% -> 2% of each run, Pallas kernels for 0% -> 36%
where the time goes in v1:
time: 193 us; the launch traced here: 192 us
  Pallas kernels  76.5 us (40%)
  starting transfers between devices  62.8 us (33%)
  waiting for transfers between devices  38.3 us (20%)
  local copies, waits for them, and re-layouts  9.53 us (5%)
  other arithmetic  3.82 us (2%)
    pallas_call x9, Pallas kernels, call(): pl.pallas_call(kernel, out_shape=[m(s, d) if m else jax.ShapeDtypeStruct(...  76.5 us
    ppermute x32, starting transfers between devices, send(): return lax.ppermute(value, AXES, routes[name])  62.8 us
    ppermute x32, waiting for transfers between devices, send(): return lax.ppermute(value, AXES, routes[name])  38.3 us
    unnamed x40, local copies, waits for them, and re-layouts  4.81 us
  transfers between devices with their start and end apart: 32, of which 16 were waited for; matrix products, arithmetic and copies ran while one was open for 2% of the time, Pallas kernels for 36%

profile of v1, /device:TPU:23, one launch (start us, length us, event | category | flops | bytes accessed | tf_op | source)
XLA Modules:
  0.0 191.6 jit_solution(8257090555918944893)
XLA Ops:
  0.0 3.1 %slice.29 = f32[2,128,2048]{2,1,0:T(8,128)} slice(f32[2,384,2048]{2,1,0:T(8,128)} %bitcast.19), slice={[0:2], [0:128], [0:2048]} | slice | bytes 4194304 | tf_op jit(solution)/shard_map/slice | solution.py:424
  3.1 1.3 collective-permute-start
  4.4 3.2 %collective-permute-start.1 = (f32[2,128,2048]{2,1,0:T(8,128)}, f32[2,128,2048]{2,1,0:T(8,128)}, u32[]{:S(2)}, u32[]{:S(2)}) collective-permute-start(f32[2,128,2048]{2,1,0:T(8,128)} %slice.29), channel_id=1, source_target_pairs={{1,9},{3,11},{5,13},{7,15},{8,0},{9,17},{10,2},{11,19},{12,4},{13,... | collective-permute-start | bytes 6291464 | tf_op jit(solution)/shard_map/ppermute | solution.py:422
  7.7 14.2 %shard_map.28 = (bf16[3,256,2048]{2,1,0:T(8,128)(2,1)}, bf16[3,256,2048]{2,1,0:T(8,128)(2,1)}, f32[2,192,768]{2,1,0:T(8,128)}, f32[2,192,768]{2,1,0:T(8,128)}, f...) custom-call(s32[2]{0:T(128)S(1)} %pad_add_fusion.role, ...), custom_call_target="tpu_custom_call" | custom-call | flops 4831838208 | bytes 6291456 | tf_op jit(solution)/shard_map/pallas_call | solution.py:43
  22.0 1.2 collective-permute-start.3
  23.1 0.8 collective-permute-done.3
  24.3 0.6 collective-permute-start.2
  25.0 2.0 %collective-permute-done.4 = f32[2,2,768]{2,0,1:T(2,128)S(1)} collective-permute-done((f32[2,2,768]{2,0,1:T(2,128)S(1)}, f32[2,2,768]{2,0,1:T(2,128)S(1)}, u32[]{:S(2)}, u32[]{:S(2)}) %collective-permute-start.4) | collective-permute-done | bytes 12320 | tf_op jit(solution)/shard_map/ppermute | solution.py:422
  27.2 0.5 collective-permute-done.2
  27.7 1.9 add.70
  29.7 0.8 collective-permute-done.raw_x
  30.5 1.3 collective-permute-done.1.raw_z
  31.8 1.4 collective-permute-start.5
  33.2 2.9 %collective-permute-start.6 = (f32[2,128,2048]{2,1,0:T(8,128)S(1)}, f32[2,128,2048]{2,1,0:T(8,128)S(1)}, u32[]{:S(2)}, u32[]{:S(2)}) collective-permute-start(f32[2,128,2048]{2,1,0:T(8,128)S(1)} %copy-done.16), channel_id=1, source_target_pairs={{1,9},{3,11},{5,13},{7,15},{8,0},{9,17},{10,2},{11,19},{12,4},{13,... | collective-permute-start | bytes 6291464 | tf_op jit(solution)/shard_map/ppermute | solution.py:422
  36.2 0.8 collective-permute-start.7
  36.9 11.5 %shard_map.29 = (f32[2,128,384]{2,1,0:T(8,128)}, f32[2,128,384]{2,1,0:T(8,128)}, f32[2,128,512]{2,1,0:T(8,128)}, f32[2,128,512]{2,1,0:T(8,128)}, bf16[2,3,256,20...) custom-call(s32[2]{0:T(128)S(1)} %pad_add_fusion.role, f32[2,128,2048]{2,1,0:T(8,128)} %collective-permute-done.1.raw_z, ...), custom_call_target="tpu_custom_call" | custom-call | flops 1 | bytes 1 | tf_op jit(solution)/shard_map/pallas_call | solution.py:43
  48.7 10.4 %collective-permute-done.5.raw_x = f32[2,128,2048]{2,1,0:T(8,128)S(1)} collective-permute-done((f32[2,128,2048]{2,1,0:T(8,128)S(1)}, f32[2,128,2048]{2,1,0:T(8,128)S(1)}, u32[]{:S(2)}, u32[]{:S(2)}) %collective-permute-start.5) | collective-permute-done | bytes 2097184 | tf_op jit(solution)/shard_map/ppermute | solution.py:422
  59.0 1.3 collective-permute-done.6.raw_z
  60.3 1.3 collective-permute-start.8
  61.6 2.6 %collective-permute-start.9 = (f32[2,64,2048]{2,1,0:T(8,128)S(1)}, f32[2,64,2048]{2,1,0:T(8,128)S(1)}, u32[]{:S(2)}, u32[]{:S(2)}) collective-permute-start(f32[2,64,2048]{2,1,0:T(8,128)S(1)} %copy-done.18), channel_id=1, source_target_pairs={{1,9},{3,11},{5,13},{7,15},{8,0},{9,17},{10,2},{11,19},{12,4},{13,... | collective-permute-start | bytes 3145736 | tf_op jit(solution)/shard_map/ppermute | solution.py:422
  64.2 2.6 %collective-permute-start.11 = (f32[2,128,512]{2,1,0:T(8,128)}, f32[2,128,512]{2,1,0:T(8,128)S(1)}, u32[]{:S(2)}, u32[]{:S(2)}) collective-permute-start(f32[2,128,512]{2,1,0:T(8,128)} %get-tuple-element.156), channel_id=1, source_target_pairs={{0,2},{2,0},{5,7},{7,5},{8,10},{10,8},{13,15},{15,13},{16,18},{18,... | collective-permute-start | bytes 1572872 | tf_op jit(solution)/shard_map/ppermute | solution.py:422
  66.9 0.8 collective-permute-start.10
  67.7 12.8 %shard_map.30 = (f32[2,128,384]{2,1,0:T(8,128)}, f32[2,128,384]{2,1,0:T(8,128)}, f32[2,128,768]{2,1,0:T(8,128)}, f32[2,128,768]{2,1,0:T(8,128)}, bf16[2,3,256,20...) custom-call(s32[2]{0:T(128)S(1)} %pad_add_fusion.role, ...), custom_call_target="tpu_custom_call", output_to_operand_aliasing={{4}: (5, {}), {5}: (6, {})} | custom-call | flops 1 | bytes 1 | tf_op jit(solution)/shard_map/pallas_call | solution.py:43
  80.5 2.3 %collective-permute-done.10.refs_1_ = f32[2,128,384]{2,1,0:T(8,128)S(1)} collective-permute-done((f32[2,128,384]{2,1,0:T(8,128)}, f32[2,128,384]{2,1,0:T(8,128)S(1)}, u32[]{:S(2)}, u32[]{:S(2)}) %collective-permute-start.10) | collective-permute-done | bytes 393248 | tf_op jit(solution)/shard_map/ppermute | solution.py:422
  82.8 1.3 collective-permute-start.12
  84.1 1.9 %collective-permute-start.13 = (f32[2,64,2048]{2,1,0:T(8,128)S(1)}, f32[2,64,2048]{2,1,0:T(8,128)S(1)}, u32[]{:S(2)}, u32[]{:S(2)}) collective-permute-start(f32[2,64,2048]{2,1,0:T(8,128)S(1)} %copy-done.17), channel_id=1, source_target_pairs={{1,9},{3,11},{5,13},{7,15},{8,0},{9,17},{10,2},{11,19},{12,4},{13,... | collective-permute-start | bytes 3145736 | tf_op jit(solution)/shard_map/ppermute | solution.py:422
  86.1 2.8 %collective-permute-start.15 = (f32[2,128,768]{2,1,0:T(8,128)}, f32[2,128,768]{2,1,0:T(8,128)S(1)}, u32[]{:S(2)}, u32[]{:S(2)}) collective-permute-start(f32[2,128,768]{2,1,0:T(8,128)} %get-tuple-element.174), channel_id=1, source_target_pairs={{0,2},{2,0},{5,7},{7,5},{8,10},{10,8},{13,15},{15,13},{16,18},{18,... | collective-permute-start | bytes 2359304 | tf_op jit(solution)/shard_map/ppermute | solution.py:422
  88.9 0.8 collective-permute-start.14
  89.7 11.2 %shard_map.31 = (f32[2,64,384]{2,1,0:T(8,128)}, f32[2,64,384]{2,1,0:T(8,128)}, f32[2,64,896]{2,1,0:T(8,128)}, f32[2,64,896]{2,1,0:T(8,128)}, bf16[2,3,256,2048]{...) custom-call(s32[2]{0:T(128)S(1)} %pad_add_fusion.role, ...), custom_call_target="tpu_custom_call", output_to_operand_aliasing={{4}: (5, {}), {5}: (6, {})} | custom-call | flops 1 | bytes 1 | tf_op jit(solution)/shard_map/pallas_call | solution.py:43
  100.9 2.6 %collective-permute-start.17 = (f32[2,64,896]{2,1,0:T(8,128)}, f32[2,64,896]{2,1,0:T(8,128)S(1)}, u32[]{:S(2)}, u32[]{:S(2)}) collective-permute-start(f32[2,64,896]{2,1,0:T(8,128)} %get-tuple-element.183), channel_id=1, source_target_pairs={{0,2},{2,0},{5,7},{7,5},{8,10},{10,8},{13,15},{15,13},{16,18},{18,... | collective-permute-start | bytes 1376264 | tf_op jit(solution)/shard_map/ppermute | solution.py:422
  103.6 3.9 %collective-permute-done.14.refs_5_ = f32[2,128,384]{2,1,0:T(8,128)S(1)} collective-permute-done((f32[2,128,384]{2,1,0:T(8,128)}, f32[2,128,384]{2,1,0:T(8,128)S(1)}, u32[]{:S(2)}, u32[]{:S(2)}) %collective-permute-start.14) | collective-permute-done | bytes 393248 | tf_op jit(solution)/shard_map/ppermute | solution.py:422
  107.5 12.2 %shard_map.32 = (f32[2,64,384]{2,1,0:T(8,128)}, f32[2,64,384]{2,1,0:T(8,128)}, f32[2,64,1152]{2,1,0:T(8,128)}, f32[2,64,1152]{2,1,0:T(8,128)}, bf16[2,3,256,2048...) custom-call(s32[2]{0:T(128)S(1)} %pad_add_fusion.role, ...), custom_call_target="tpu_custom_call", output_to_operand_aliasing={{4}: (5, {}), {5}: (6, {})} | custom-call | flops 1 | bytes 1 | tf_op jit(solution)/shard_map/pallas_call | solution.py:43
  119.7 2.6 %collective-permute-start.21 = (f32[2,64,1152]{2,1,0:T(8,128)}, f32[2,64,1152]{2,1,0:T(8,128)S(1)}, u32[]{:S(2)}, u32[]{:S(2)}) collective-permute-start(f32[2,64,1152]{2,1,0:T(8,128)} %get-tuple-element.210), channel_id=1, source_target_pairs={{0,2},{2,0},{5,7},{7,5},{8,10},{10,8},{13,15},{15,13},{16,18},{18,... | collective-permute-start | bytes 1769480 | tf_op jit(solution)/shard_map/ppermute | solution.py:422
  122.3 1.3 collective-permute-start.18
  123.6 1.9 %collective-permute-start.19 = (f32[822,128]{1,0:T(8,128)S(1)}, f32[822,128]{1,0:T(8,128)S(1)}, u32[]{:S(2)}, u32[]{:S(2)}) collective-permute-start(f32[822,128]{1,0:T(8,128)S(1)} %pad_maximum_fusion), channel_id=1, source_target_pairs={{1,9},{3,11},{5,13},{7,15},{8,0},{9,17},{10,2},{11,19},{12,4},{13,... | collective-permute-start | bytes 1262600 | tf_op jit(solution)/shard_map/ppermute | solution.py:422
  125.5 0.8 collective-permute-start.16
  126.3 6.6 %collective-permute-done.16.refs_1_.refs_9_ = f32[2,64,384]{2,1,0:T(8,128)S(1)} collective-permute-done((f32[2,64,384]{2,1,0:T(8,128)S(1)}, f32[2,64,384]{2,1,0:T(8,128)S(1)}, u32[]{:S(2)}, u32[]{:S(2)}) %collective-permute-start.16) | collective-permute-done | bytes 196640 | tf_op jit(solution)/shard_map/ppermute | solution.py:422
  132.9 0.7 collective-permute-start.20
  133.6 3.2 %shard_map.33 = (f32[256,384]{1,0:T(8,128)}, f32[256,384]{1,0:T(8,128)}, f32[512,128]{1,0:T(8,128)S(1)}) custom-call(s32[2]{0:T(128)S(1)} %pad_add_fusion.role, f32[2,128,384]{2,1,0:T(8,128)} %get-tuple-element.191.refs_0_, f32[2,128,384]{2,1,0:T(8,128)} %copy-done.11, f32[2,128,512]{2,1,0:T(8,128)} %get-tuple-element.193.refs_2_, f32[2,128,512]{2,1,0:T(8,128)} %copy-done.9, ...), custom_call_target="tpu_custom_call" | custom-call | flops 98304 | bytes 1179648 | tf_op jit(solution)/shard_map/pallas_call | solution.py:43
  136.8 8.1 %collective-permute-start.24 = (f32[512,128]{1,0:T(8,128)S(1)}, f32[512,128]{1,0:T(8,128)S(1)}, u32[]{:S(2)}, u32[]{:S(2)}) collective-permute-start(f32[512,128]{1,0:T(8,128)S(1)} %get-tuple-element.213), channel_id=1, source_target_pairs={{0,13},{2,15},{8,21},{10,23},{13,0},{15,2},{16,29},{18,31},{21,8},... | collective-permute-start | bytes 786440 | tf_op jit(solution)/shard_map/ppermute | solution.py:422
  144.9 1.9 %collective-permute-start.22 = (f32[256,384]{1,0:T(8,128)}, f32[256,384]{1,0:T(8,128)S(1)}, u32[]{:S(2)}, u32[]{:S(2)}) collective-permute-start(f32[256,384]{1,0:T(8,128)} %get-tuple-element.211), channel_id=1, source_target_pairs={{0,9},{2,11},{4,13},{6,15},{8,17},{9,0},{10,19},{11,2},{12,21},{13... | collective-permute-start | bytes 1179656 | tf_op jit(solution)/shard_map/ppermute | solution.py:422
  146.8 1.9 %collective-permute-start.23 = (f32[256,384]{1,0:T(8,128)}, f32[256,384]{1,0:T(8,128)S(1)}, u32[]{:S(2)}, u32[]{:S(2)}) collective-permute-start(f32[256,384]{1,0:T(8,128)} %get-tuple-element.212), channel_id=1, source_target_pairs={{0,5},{2,7},{5,0},{7,2},{8,13},{10,15},{13,8},{15,10},{16,21},{18,... | collective-permute-start | bytes 1179656 | tf_op jit(solution)/shard_map/ppermute | solution.py:422
  148.8 0.6 copy-done.14
  149.7 2.9 %shard_map.34 = (f32[128,384]{1,0:T(8,128)}, f32[128,384]{1,0:T(8,128)}, f32[640,128]{1,0:T(8,128)}) custom-call(s32[2]{0:T(128)S(1)} %pad_add_fusion.role, f32[2,64,384]{2,1,0:T(8,128)} %get-tuple-element.199.refs_0_.refs_8_, f32[2,64,384]{2,1,0:T(8,128)} %copy-done.13, f32[2,64,896]{2,1,0:T(8,128)} %get-tuple-element.201.refs_2_.refs_10_, ...), custom_call_target="tpu_custom_call" | custom-call | flops 49152 | bytes 589824 | tf_op jit(solution)/shard_map/pallas_call | solution.py:43
  152.6 2.9 %collective-permute-start.27 = (f32[640,128]{1,0:T(8,128)}, f32[640,128]{1,0:T(8,128)S(1)}, u32[]{:S(2)}, u32[]{:S(2)}) collective-permute-start(f32[640,128]{1,0:T(8,128)} %get-tuple-element.216), channel_id=1, source_target_pairs={{0,13},{2,15},{8,21},{10,23},{13,0},{15,2},{16,29},{18,31},{21,8},... | collective-permute-start | bytes 983048 | tf_op jit(solution)/shard_map/ppermute | solution.py:422
  155.5 1.9 %collective-permute-start.25 = (f32[128,384]{1,0:T(8,128)}, f32[128,384]{1,0:T(8,128)}, u32[]{:S(2)}, u32[]{:S(2)}) collective-permute-start(f32[128,384]{1,0:T(8,128)} %get-tuple-element.214), channel_id=1, source_target_pairs={{0,9},{2,11},{4,13},{6,15},{8,17},{9,0},{10,19},{11,2},{12,21},{13... | collective-permute-start | bytes 589832 | tf_op jit(solution)/shard_map/ppermute | solution.py:422
  157.5 0.7 copy-done.2
  158.2 2.7 %collective-permute-start.26 = (f32[128,384]{1,0:T(8,128)}, f32[128,384]{1,0:T(8,128)}, u32[]{:S(2)}, u32[]{:S(2)}) collective-permute-start(f32[128,384]{1,0:T(8,128)} %get-tuple-element.215), channel_id=1, source_target_pairs={{0,5},{2,7},{5,0},{7,2},{8,13},{10,15},{13,8},{15,10},{16,21},{18,... | collective-permute-start | bytes 589832 | tf_op jit(solution)/shard_map/ppermute | solution.py:422
  160.9 0.6 reshape.54.refs_25_
  161.5 0.6 reshape.55.refs_27_
  162.2 1.0 collective-permute-done.25.refs_19_
  163.1 2.3 %collective-permute-done.26.refs_20_ = f32[128,384]{1,0:T(8,128)} collective-permute-done((f32[128,384]{1,0:T(8,128)}, f32[128,384]{1,0:T(8,128)}, u32[]{:S(2)}, u32[]{:S(2)}) %collective-permute-start.26) | collective-permute-done | bytes 196640 | tf_op jit(solution)/shard_map/ppermute | solution.py:422
  165.5 0.9 copy-done.3
  166.4 0.8 copy-done.4
  167.2 0.8 copy-done.5
  168.0 7.3 %shard_map.35 = (f32[384,128]{1,0:T(8,128)S(1)}, f32[384,128]{1,0:T(8,128)}, f32[384,128]{1,0:T(8,128)}, f32[384,128]{1,0:T(8,128)}) custom-call(s32[2]{0:T(128)S(1)} %pad_add_fusion.role, f32[2,128,384]{2,1,0:T(8,128)} %get-tuple-element.191.refs_0_, f32[2,128,384]{2,1,0:T(8,128)} %copy-done.11, f32[2,128,512]{2,1,0:T(8,128)} %get-tuple-element.193.refs_2_, ...), custom_call_target="tpu_custom_call" | custom-call | flops 452984832 | bytes 4718592 | tf_op jit(solution)/shard_map/pallas_call | solution.py:43
  175.4 0.7 copy-done.6
  176.1 1.8 collective-permute-start.28
  177.9 3.2 %collective-permute-start.29 = (f32[384,128]{1,0:T(8,128)}, f32[384,128]{1,0:T(8,128)S(1)}, u32[]{:S(2)}, u32[]{:S(2)}) collective-permute-start(f32[384,128]{1,0:T(8,128)} %get-tuple-element.223), channel_id=1, source_target_pairs={{5,0},{7,2},{13,8},{15,10},{21,16},{23,18},{29,24},{31,26}} | collective-permute-start | bytes 589832 | tf_op jit(solution)/shard_map/ppermute | solution.py:422
  181.1 2.5 %collective-permute-start.30 = (f32[384,128]{1,0:T(8,128)}, f32[384,128]{1,0:T(8,128)S(1)}, u32[]{:S(2)}, u32[]{:S(2)}) collective-permute-start(f32[384,128]{1,0:T(8,128)} %get-tuple-element.224), channel_id=1, source_target_pairs={{0,8},{2,10},{4,12},{6,14},{8,16},{9,3},{10,18},{11,1},{12,20},{13... | collective-permute-start | bytes 589832 | tf_op jit(solution)/shard_map/ppermute | solution.py:422
  184.0 4.6 %collective-permute-done.30 = f32[384,128]{1,0:T(8,128)S(1)} collective-permute-done((f32[384,128]{1,0:T(8,128)}, f32[384,128]{1,0:T(8,128)S(1)}, u32[]{:S(2)}, u32[]{:S(2)}) %collective-permute-start.30) | collective-permute-done | bytes 196640 | tf_op jit(solution)/shard_map/ppermute | solution.py:422
  188.6 1.0 add_add_fusion
  189.8 1.1 shard_map.36
  191.0 0.7 fusion
  (77 shorter events, 1.9 us)
Async XLA Ops:
  3.1 27.4 %collective-permute-start = (f32[2,128,2048]{2,1,0:T(8,128)}, f32[2,128,2048]{2,1,0:T(8,128)S(1)}, u32[]{:S(2)}, u32[]{:S(2)}) collective-permute-start(f32[2,128,2048]{2,1,0:T(8,128)} %slice.29), channel_id=1, source_target_pairs={{1,5},{3,7},{4,0},{6,2},{9,13},{11,15},{12,8},{14,10},{17,21},{19,... | collective-permute-start | bytes 6291464 | tf_op jit(solution)/shard_map/ppermute | solution.py:422
  4.4 27.4 %collective-permute-start.1 = (f32[2,128,2048]{2,1,0:T(8,128)}, f32[2,128,2048]{2,1,0:T(8,128)}, u32[]{:S(2)}, u32[]{:S(2)}) collective-permute-start(f32[2,128,2048]{2,1,0:T(8,128)} %slice.29), channel_id=1, source_target_pairs={{1,9},{3,11},{5,13},{7,15},{8,0},{9,17},{10,2},{11,19},{12,4},{13,... | collective-permute-start | bytes 6291464 | tf_op jit(solution)/shard_map/ppermute | solution.py:422
  7.7 17.2 %copy-start.15 = (s32[768,128]{1,0:T(8,128)S(1)}, s32[768,128]{1,0:T(8,128)}, u32[]{:S(2)}) copy-start(s32[768,128]{1,0:T(8,128)} %param.3) | copy-start | bytes 1179652
  22.0 2.0 %collective-permute-start.3 = (f32[1,2,768]{2,0,1:T(1,128)S(1)}, f32[1,2,768]{2,0,1:T(1,128)S(1)}, u32[]{:S(2)}, u32[]{:S(2)}) collective-permute-start(f32[1,2,768]{2,0,1:T(1,128)S(1)} %reshape.52), channel_id=1, source_target_pairs={{0,1},{1,0},{2,3},{3,2},{4,5},{5,4},{6,7},{7,6},{8,9},{9,8},{10,11... | collective-permute-start | bytes 18440 | tf_op jit(solution)/shard_map/ppermute | solution.py:422
  24.0 3.0 %collective-permute-start.4 = (f32[2,2,768]{2,0,1:T(2,128)S(1)}, f32[2,2,768]{2,0,1:T(2,128)S(1)}, u32[]{:S(2)}, u32[]{:S(2)}) collective-permute-start(f32[2,2,768]{2,0,1:T(2,128)S(1)} %pad_maximum_fusion.3), channel_id=1, source_target_pairs={{0,2},{1,3},{2,0},{3,1},{4,6},{5,7},{6,4},{7,5},{8,10},{9,11},{10,... | collective-permute-start | bytes 36872 | tf_op jit(solution)/shard_map/ppermute | solution.py:422
  24.3 3.4 %collective-permute-start.2 = (f32[2,192,768]{2,1,0:T(8,128)}, f32[2,192,768]{2,1,0:T(8,128)}, u32[]{:S(2)}, u32[]{:S(2)}) collective-permute-start(f32[2,192,768]{2,1,0:T(8,128)} %get-tuple-element.130), channel_id=1, source_target_pairs={{0,1},{1,0},{2,3},{3,2},{4,5},{5,4},{6,7},{7,6},{8,9},{9,8},{10,11... | collective-permute-start | bytes 3538952 | tf_op jit(solution)/shard_map/ppermute | solution.py:422
  27.2 4.6 %copy-start.16 = (f32[2,128,2048]{2,1,0:T(8,128)S(1)}, f32[2,128,2048]{2,1,0:T(8,128)}, u32[]{:S(2)}) copy-start(f32[2,128,2048]{2,1,0:T(8,128)} %get-tuple-element.132) | copy-start | bytes 6291460
  31.8 28.5 %copy-start.18 = (f32[2,64,2048]{2,1,0:T(8,128)S(1)}, f32[2,64,2048]{2,1,0:T(8,128)}, u32[]{:S(2)}) copy-start(f32[2,64,2048]{2,1,0:T(8,128)} %get-tuple-element.143) | copy-start | bytes 3145732
  31.8 27.2 %collective-permute-start.5 = (f32[2,128,2048]{2,1,0:T(8,128)S(1)}, f32[2,128,2048]{2,1,0:T(8,128)S(1)}, u32[]{:S(2)}, u32[]{:S(2)}) collective-permute-start(f32[2,128,2048]{2,1,0:T(8,128)S(1)} %copy-done.16), channel_id=1, source_target_pairs={{1,5},{3,7},{4,0},{6,2},{9,13},{11,15},{12,8},{14,10},{17,21},{19,... | collective-permute-start | bytes 6291464 | tf_op jit(solution)/shard_map/ppermute | solution.py:422
  33.2 27.1 %collective-permute-start.6 = (f32[2,128,2048]{2,1,0:T(8,128)S(1)}, f32[2,128,2048]{2,1,0:T(8,128)S(1)}, u32[]{:S(2)}, u32[]{:S(2)}) collective-permute-start(f32[2,128,2048]{2,1,0:T(8,128)S(1)} %copy-done.16), channel_id=1, source_target_pairs={{1,9},{3,11},{5,13},{7,15},{8,0},{9,17},{10,2},{11,19},{12,4},{13,... | collective-permute-start | bytes 6291464 | tf_op jit(solution)/shard_map/ppermute | solution.py:422
  36.2 12.5 %collective-permute-start.7 = (f32[192,768]{1,0:T(8,128)S(1)}, f32[192,768]{1,0:T(8,128)S(1)}, u32[]{:S(2)}, u32[]{:S(2)}) collective-permute-start(f32[192,768]{1,0:T(8,128)S(1)} %get-tuple-element.142), channel_id=1, source_target_pairs={{0,2},{1,3},{2,0},{3,1},{4,6},{5,7},{6,4},{7,5},{8,10},{9,11},{10,... | collective-permute-start | bytes 1769480 | tf_op jit(solution)/shard_map/ppermute | solution.py:422
  48.7 31.8 %copy-start = (f32[192,768]{1,0:T(8,128)}, f32[192,768]{1,0:T(8,128)S(1)}, u32[]{:S(2)}) copy-start(f32[192,768]{1,0:T(8,128)S(1)} %collective-permute-done.7.tile_pair) | copy-start | bytes 1769476
  60.3 22.5 %collective-permute-start.8 = (f32[2,64,2048]{2,1,0:T(8,128)S(1)}, f32[2,64,2048]{2,1,0:T(8,128)S(1)}, u32[]{:S(2)}, u32[]{:S(2)}) collective-permute-start(f32[2,64,2048]{2,1,0:T(8,128)S(1)} %copy-done.18), channel_id=1, source_target_pairs={{1,5},{3,7},{4,0},{6,2},{9,13},{11,15},{12,8},{14,10},{17,21},{19,... | collective-permute-start | bytes 3145736 | tf_op jit(solution)/shard_map/ppermute | solution.py:422
  61.6 21.2 %collective-permute-start.9 = (f32[2,64,2048]{2,1,0:T(8,128)S(1)}, f32[2,64,2048]{2,1,0:T(8,128)S(1)}, u32[]{:S(2)}, u32[]{:S(2)}) collective-permute-start(f32[2,64,2048]{2,1,0:T(8,128)S(1)} %copy-done.18), channel_id=1, source_target_pairs={{1,9},{3,11},{5,13},{7,15},{8,0},{9,17},{10,2},{11,19},{12,4},{13,... | collective-permute-start | bytes 3145736 | tf_op jit(solution)/shard_map/ppermute | solution.py:422
  64.2 18.6 %collective-permute-start.11 = (f32[2,128,512]{2,1,0:T(8,128)}, f32[2,128,512]{2,1,0:T(8,128)S(1)}, u32[]{:S(2)}, u32[]{:S(2)}) collective-permute-start(f32[2,128,512]{2,1,0:T(8,128)} %get-tuple-element.156), channel_id=1, source_target_pairs={{0,2},{2,0},{5,7},{7,5},{8,10},{10,8},{13,15},{15,13},{16,18},{18,... | collective-permute-start | bytes 1572872 | tf_op jit(solution)/shard_map/ppermute | solution.py:422
  66.9 16.0 %copy-start.17 = (f32[2,64,2048]{2,1,0:T(8,128)S(1)}, f32[2,64,2048]{2,1,0:T(8,128)}, u32[]{:S(2)}) copy-start(f32[2,64,2048]{2,1,0:T(8,128)} %get-tuple-element.162) | copy-start | bytes 3145732
  66.9 15.9 %collective-permute-start.10 = (f32[2,128,384]{2,1,0:T(8,128)}, f32[2,128,384]{2,1,0:T(8,128)S(1)}, u32[]{:S(2)}, u32[]{:S(2)}) collective-permute-start(f32[2,128,384]{2,1,0:T(8,128)} %get-tuple-element.154), channel_id=1, source_target_pairs={{0,2},{1,3},{2,0},{3,1},{4,6},{5,7},{6,4},{7,5},{8,10},{9,11},{10,... | collective-permute-start | bytes 1179656 | tf_op jit(solution)/shard_map/ppermute | solution.py:422
  82.8 18.1 %copy-start.11 = (f32[2,128,384]{2,1,0:T(8,128)}, f32[2,128,384]{2,1,0:T(8,128)S(1)}, u32[]{:S(2)}) copy-start(f32[2,128,384]{2,1,0:T(8,128)S(1)} %collective-permute-done.10.refs_1_) | copy-start | bytes 1179652
  82.8 18.1 %copy-start.9 = (f32[2,128,512]{2,1,0:T(8,128)}, f32[2,128,512]{2,1,0:T(8,128)S(1)}, u32[]{:S(2)}) copy-start(f32[2,128,512]{2,1,0:T(8,128)S(1)} %collective-permute-done.11.refs_3_) | copy-start | bytes 1572868
  82.8 24.6 %collective-permute-start.12 = (f32[2,64,2048]{2,1,0:T(8,128)S(1)}, f32[2,64,2048]{2,1,0:T(8,128)S(1)}, u32[]{:S(2)}, u32[]{:S(2)}) collective-permute-start(f32[2,64,2048]{2,1,0:T(8,128)S(1)} %copy-done.17), channel_id=1, source_target_pairs={{1,5},{3,7},{4,0},{6,2},{9,13},{11,15},{12,8},{14,10},{17,21},{19,... | collective-permute-start | bytes 3145736 | tf_op jit(solution)/shard_map/ppermute | solution.py:422
  84.1 23.3 %collective-permute-start.13 = (f32[2,64,2048]{2,1,0:T(8,128)S(1)}, f32[2,64,2048]{2,1,0:T(8,128)S(1)}, u32[]{:S(2)}, u32[]{:S(2)}) collective-permute-start(f32[2,64,2048]{2,1,0:T(8,128)S(1)} %copy-done.17), channel_id=1, source_target_pairs={{1,9},{3,11},{5,13},{7,15},{8,0},{9,17},{10,2},{11,19},{12,4},{13,... | collective-permute-start | bytes 3145736 | tf_op jit(solution)/shard_map/ppermute | solution.py:422
  86.1 21.4 %collective-permute-start.15 = (f32[2,128,768]{2,1,0:T(8,128)}, f32[2,128,768]{2,1,0:T(8,128)S(1)}, u32[]{:S(2)}, u32[]{:S(2)}) collective-permute-start(f32[2,128,768]{2,1,0:T(8,128)} %get-tuple-element.174), channel_id=1, source_target_pairs={{0,2},{2,0},{5,7},{7,5},{8,10},{10,8},{13,15},{15,13},{16,18},{18,... | collective-permute-start | bytes 2359304 | tf_op jit(solution)/shard_map/ppermute | solution.py:422
  88.9 18.6 %collective-permute-start.14 = (f32[2,128,384]{2,1,0:T(8,128)}, f32[2,128,384]{2,1,0:T(8,128)S(1)}, u32[]{:S(2)}, u32[]{:S(2)}) collective-permute-start(f32[2,128,384]{2,1,0:T(8,128)} %get-tuple-element.172), channel_id=1, source_target_pairs={{0,2},{1,3},{2,0},{3,1},{4,6},{5,7},{6,4},{7,5},{8,10},{9,11},{10,... | collective-permute-start | bytes 1179656 | tf_op jit(solution)/shard_map/ppermute | solution.py:422
  100.9 32.7 %collective-permute-start.17 = (f32[2,64,896]{2,1,0:T(8,128)}, f32[2,64,896]{2,1,0:T(8,128)S(1)}, u32[]{:S(2)}, u32[]{:S(2)}) collective-permute-start(f32[2,64,896]{2,1,0:T(8,128)} %get-tuple-element.183), channel_id=1, source_target_pairs={{0,2},{2,0},{5,7},{7,5},{8,10},{10,8},{13,15},{15,13},{16,18},{18,... | collective-permute-start | bytes 1376264 | tf_op jit(solution)/shard_map/ppermute | solution.py:422
  107.4 12.2 %copy-start.12 = (f32[2,128,384]{2,1,0:T(8,128)}, f32[2,128,384]{2,1,0:T(8,128)S(1)}, u32[]{:S(2)}) copy-start(f32[2,128,384]{2,1,0:T(8,128)S(1)} %collective-permute-done.14.refs_5_) | copy-start | bytes 1179652
  107.4 12.2 %copy-start.7 = (f32[2,128,768]{2,1,0:T(8,128)}, f32[2,128,768]{2,1,0:T(8,128)S(1)}, u32[]{:S(2)}) copy-start(f32[2,128,768]{2,1,0:T(8,128)S(1)} %collective-permute-done.15.refs_7_) | copy-start | bytes 2359300
  107.4 18.0 %copy-start.19 = (f32[2,64,384]{2,1,0:T(8,128)S(1)}, f32[2,64,384]{2,1,0:T(8,128)}, u32[]{:S(2)}) copy-start(f32[2,64,384]{2,1,0:T(8,128)} %get-tuple-element.181) | copy-start | bytes 589828
  119.7 29.1 %collective-permute-start.21 = (f32[2,64,1152]{2,1,0:T(8,128)}, f32[2,64,1152]{2,1,0:T(8,128)S(1)}, u32[]{:S(2)}, u32[]{:S(2)}) collective-permute-start(f32[2,64,1152]{2,1,0:T(8,128)} %get-tuple-element.210), channel_id=1, source_target_pairs={{0,2},{2,0},{5,7},{7,5},{8,10},{10,8},{13,15},{15,13},{16,18},{18,... | collective-permute-start | bytes 1769480 | tf_op jit(solution)/shard_map/ppermute | solution.py:422
  122.3 11.3 %collective-permute-start.18 = (f32[822,128]{1,0:T(8,128)S(1)}, f32[822,128]{1,0:T(8,128)S(1)}, u32[]{:S(2)}, u32[]{:S(2)}) collective-permute-start(f32[822,128]{1,0:T(8,128)S(1)} %pad_maximum_fusion), channel_id=1, source_target_pairs={{1,5},{3,7},{4,0},{6,2},{9,13},{11,15},{12,8},{14,10},{17,21},{19,... | collective-permute-start | bytes 1262600 | tf_op jit(solution)/shard_map/ppermute | solution.py:422
  123.6 10.0 %collective-permute-start.19 = (f32[822,128]{1,0:T(8,128)S(1)}, f32[822,128]{1,0:T(8,128)S(1)}, u32[]{:S(2)}, u32[]{:S(2)}) collective-permute-start(f32[822,128]{1,0:T(8,128)S(1)} %pad_maximum_fusion), channel_id=1, source_target_pairs={{1,9},{3,11},{5,13},{7,15},{8,0},{9,17},{10,2},{11,19},{12,4},{13,... | collective-permute-start | bytes 1262600 | tf_op jit(solution)/shard_map/ppermute | solution.py:422
  125.5 7.4 %collective-permute-start.16 = (f32[2,64,384]{2,1,0:T(8,128)S(1)}, f32[2,64,384]{2,1,0:T(8,128)S(1)}, u32[]{:S(2)}, u32[]{:S(2)}) collective-permute-start(f32[2,64,384]{2,1,0:T(8,128)S(1)} %copy-done.19), channel_id=1, source_target_pairs={{0,2},{1,3},{2,0},{3,1},{4,6},{5,7},{6,4},{7,5},{8,10},{9,11},{10,... | collective-permute-start | bytes 589832 | tf_op jit(solution)/shard_map/ppermute | solution.py:422
  132.9 15.9 %copy-start.13 = (f32[2,64,384]{2,1,0:T(8,128)}, f32[2,64,384]{2,1,0:T(8,128)S(1)}, u32[]{:S(2)}) copy-start(f32[2,64,384]{2,1,0:T(8,128)S(1)} %collective-permute-done.16.refs_1_.refs_9_) | copy-start | bytes 589828
  132.9 15.9 %collective-permute-start.20 = (f32[2,64,384]{2,1,0:T(8,128)}, f32[2,64,384]{2,1,0:T(8,128)S(1)}, u32[]{:S(2)}, u32[]{:S(2)}) collective-permute-start(f32[2,64,384]{2,1,0:T(8,128)} %get-tuple-element.208), channel_id=1, source_target_pairs={{0,2},{1,3},{2,0},{3,1},{4,6},{5,7},{6,4},{7,5},{8,10},{9,11},{10,... | collective-permute-start | bytes 589832 | tf_op jit(solution)/shard_map/ppermute | solution.py:422
  133.6 15.2 %copy-start.10 = (f32[2,64,896]{2,1,0:T(8,128)}, f32[2,64,896]{2,1,0:T(8,128)S(1)}, u32[]{:S(2)}) copy-start(f32[2,64,896]{2,1,0:T(8,128)S(1)} %collective-permute-done.17.refs_3_.refs_11_) | copy-start | bytes 1376260
  136.8 20.7 %collective-permute-start.24 = (f32[512,128]{1,0:T(8,128)S(1)}, f32[512,128]{1,0:T(8,128)S(1)}, u32[]{:S(2)}, u32[]{:S(2)}) collective-permute-start(f32[512,128]{1,0:T(8,128)S(1)} %get-tuple-element.213), channel_id=1, source_target_pairs={{0,13},{2,15},{8,21},{10,23},{13,0},{15,2},{16,29},{18,31},{21,8},... | collective-permute-start | bytes 786440 | tf_op jit(solution)/shard_map/ppermute | solution.py:422
  144.9 20.6 %collective-permute-start.22 = (f32[256,384]{1,0:T(8,128)}, f32[256,384]{1,0:T(8,128)S(1)}, u32[]{:S(2)}, u32[]{:S(2)}) collective-permute-start(f32[256,384]{1,0:T(8,128)} %get-tuple-element.211), channel_id=1, source_target_pairs={{0,9},{2,11},{4,13},{6,15},{8,17},{9,0},{10,19},{11,2},{12,21},{13... | collective-permute-start | bytes 1179656 | tf_op jit(solution)/shard_map/ppermute | solution.py:422
  146.8 18.6 %collective-permute-start.23 = (f32[256,384]{1,0:T(8,128)}, f32[256,384]{1,0:T(8,128)S(1)}, u32[]{:S(2)}, u32[]{:S(2)}) collective-permute-start(f32[256,384]{1,0:T(8,128)} %get-tuple-element.212), channel_id=1, source_target_pairs={{0,5},{2,7},{5,0},{7,2},{8,13},{10,15},{13,8},{15,10},{16,21},{18,... | collective-permute-start | bytes 1179656 | tf_op jit(solution)/shard_map/ppermute | solution.py:422
  148.8 0.7 copy-start.14
  148.8 0.9 copy-start.8
  152.6 12.8 %collective-permute-start.27 = (f32[640,128]{1,0:T(8,128)}, f32[640,128]{1,0:T(8,128)S(1)}, u32[]{:S(2)}, u32[]{:S(2)}) collective-permute-start(f32[640,128]{1,0:T(8,128)} %get-tuple-element.216), channel_id=1, source_target_pairs={{0,13},{2,15},{8,21},{10,23},{13,0},{15,2},{16,29},{18,31},{21,8},... | collective-permute-start | bytes 983048 | tf_op jit(solution)/shard_map/ppermute | solution.py:422
  155.5 7.6 %collective-permute-start.25 = (f32[128,384]{1,0:T(8,128)}, f32[128,384]{1,0:T(8,128)}, u32[]{:S(2)}, u32[]{:S(2)}) collective-permute-start(f32[128,384]{1,0:T(8,128)} %get-tuple-element.214), channel_id=1, source_target_pairs={{0,9},{2,11},{4,13},{6,15},{8,17},{9,0},{10,19},{11,2},{12,21},{13... | collective-permute-start | bytes 589832 | tf_op jit(solution)/shard_map/ppermute | solution.py:422
  157.5 0.7 copy-start.2
  158.2 7.3 %collective-permute-start.26 = (f32[128,384]{1,0:T(8,128)}, f32[128,384]{1,0:T(8,128)}, u32[]{:S(2)}, u32[]{:S(2)}) collective-permute-start(f32[128,384]{1,0:T(8,128)} %get-tuple-element.215), channel_id=1, source_target_pairs={{0,5},{2,7},{5,0},{7,2},{8,13},{10,15},{13,8},{15,10},{16,21},{18,... | collective-permute-start | bytes 589832 | tf_op jit(solution)/shard_map/ppermute | solution.py:422
  162.2 27.6 %copy-start.1 = (f32[192,768]{1,0:T(8,128)S(1)}, f32[192,768]{1,0:T(8,128)}, u32[]{:S(2)}) copy-start(f32[192,768]{1,0:T(8,128)} %copy-done) | copy-start | bytes 1769476
  165.5 1.0 copy-start.3
  166.4 0.8 copy-start.4
  167.2 0.8 copy-start.5
  175.4 0.7 copy-start.6
  176.1 7.6 %collective-permute-start.28 = (f32[384,128]{1,0:T(8,128)}, f32[384,128]{1,0:T(8,128)S(1)}, u32[]{:S(2)}, u32[]{:S(2)}) collective-permute-start(f32[384,128]{1,0:T(8,128)} %get-tuple-element.222), channel_id=1, source_target_pairs={{0,4},{2,6},{5,3},{7,1},{8,12},{10,14},{13,11},{15,9},{16,20},{18,... | collective-permute-start | bytes 589832 | tf_op jit(solution)/shard_map/ppermute | solution.py:422
  177.9 6.1 %collective-permute-start.29 = (f32[384,128]{1,0:T(8,128)}, f32[384,128]{1,0:T(8,128)S(1)}, u32[]{:S(2)}, u32[]{:S(2)}) collective-permute-start(f32[384,128]{1,0:T(8,128)} %get-tuple-element.223), channel_id=1, source_target_pairs={{5,0},{7,2},{13,8},{15,10},{21,16},{23,18},{29,24},{31,26}} | collective-permute-start | bytes 589832 | tf_op jit(solution)/shard_map/ppermute | solution.py:422
  181.1 7.5 %collective-permute-start.30 = (f32[384,128]{1,0:T(8,128)}, f32[384,128]{1,0:T(8,128)S(1)}, u32[]{:S(2)}, u32[]{:S(2)}) collective-permute-start(f32[384,128]{1,0:T(8,128)} %get-tuple-element.224), channel_id=1, source_target_pairs={{0,8},{2,10},{4,12},{6,14},{8,16},{9,3},{10,18},{11,1},{12,20},{13... | collective-permute-start | bytes 589832 | tf_op jit(solution)/shard_map/ppermute | solution.py:422
  189.6 1.4 collective-permute-start.31

commit v2 on v1

--- a/solution.py
+++ b/solution.py
@@ -8,8 +8,8 @@
 from jax.sharding import PartitionSpec as P
 
 AXES = ("genome", "people")
-WIDTHS = (128, 128, 64, 64)
-PHASES = ((0, 1), (2, 3))
+WIDTHS = (128, 128, 128)
+EARLY = 2
 LANES = 128
 F32 = jnp.float32
 BF16 = jnp.bfloat16
@@ -184,105 +184,96 @@
     copies.wait("out")
 
 
-def chunk_kernel(part, first, role, raw_z, raw_x, own_h_hbm, own_l_hbm, *refs):
+def chunk_kernel(part, name, first, role, raw, own_h, own_l, *refs):
     if not first:
         refs = refs[2:]
-    outs, refs = refs[:4], refs[4:]
-    high, low, strips, squares, left_h, left_l, col, own_h, own_l, keep_a, send_a, keep_db, send_db, sems = refs
+    keep_hbm, send_hbm, high, low, *refs = refs
+    if first:
+        own_hbm, (own_h, own_l), refs = (own_h, own_l), refs[:2], refs[2:]
+    strips, squares, keep, send, col, sems = refs
     y, c = role[0], role[1]
     w, m = part.w, part.m
-    off = part.at - m * LANES
     blocks = own_h.shape[0]
     half = blocks * LANES
+    assert w == LANES and part.last
 
     def own_copies(i):
         return [pltpu.make_async_copy(there.at[i], here.at[i], sems.at[i, n])
-                for n, (there, here) in enumerate(((own_h_hbm, own_h), (own_l_hbm, own_l)))]
-
-    for i in range(blocks):
-        for copy in own_copies(i):
-            copy.start()
-    for name, raw in ((X, raw_x), (Z, raw_z)):
-        for a in range(2):
-            target = [Rows(ref, (name, m), a * LANES + off) for ref in (high, low)]
-            also = [Rows(ref, (), (2 * name + a) * w) for ref in (left_h, left_l)]
-
-            def write(at, g, h, l, target=target, also=also):
-                store_pair(*target)(at, g, h, l)
-                store_pair(*also)(at, g, h, l)
-
-            centre_rows(Rows(raw, (a,), 0), write, w, col)
+                for n, (there, here) in enumerate(zip(own_hbm, (own_h, own_l)))]
+
+    if first:
+        for i in range(blocks):
+            for copy in own_copies(i):
+                copy.start()
+    for a in range(2):
+        target = [Rows(ref, (name, m), a * LANES) for ref in (high, low)]
+        centre_rows(Rows(raw, (a,), 0), store_pair(*target), w, col)
 
     @pl.loop(0, blocks)
     def _(i):
-        for copy in own_copies(i):
-            copy.wait()
-        strips[i] = gram(left_h[...], left_l[...], own_h[i], own_l[i])
-
-    if m:
-        @pl.loop(0, 2 * m)
+        if first:
+            for copy in own_copies(i):
+                copy.wait()
+        strips[i] = gram(high[name, m], low[name, m], own_h[i], own_l[i])
+
+    n_b = len(part.pieces) if name == X else 0
+    if n_b:
+        @pl.loop(0, n_b)
         def _(t):
-            turned = t >= m
-            at = pl.ds(pl.multiple_of(jnp.where(turned, X, Z) * 2 * w, 2 * w), 2 * w)
-            right = jnp.where(turned, Z, X)
-            j = jnp.where(turned, t - m, t)
-            squares[t, 0:2 * w] = gram(left_h[at], left_l[at], high[right, j], low[right, j])
-    if part.last:
-        squares[2 * m] = gram(high[Z, m], low[Z, m], high[X, m], low[X, m])
-
-    def rows(at, count):
-        return pl.ds(pl.multiple_of(at, 16), count)
-
-    def lanes(j):
-        return pl.ds(pl.multiple_of(j * LANES, LANES), LANES)
+            turned = (t >= m) & (t < 2 * m)
+            left, right = jnp.where(turned, X, Z), jnp.where(turned, Z, X)
+            j = jnp.where(t == 2 * m, m, jnp.where(turned, t - m, t))
+            squares[t] = gram(high[left, m], low[left, m], high[right, j], low[right, j])
+
+    def rows(i):
+        return pl.ds(pl.multiple_of(i * LANES, LANES), LANES)
 
     copies = Copies(sems.at[blocks])
-    for which, out_a, out_db in ((1 - y, send_a, send_db), (y, keep_a, keep_db)):
+    for which, out, there in ((1 - y, send, send_hbm), (y, keep, keep_hbm)):
         for t in range(2):
             s, f = jnp.where(c == 0, which, t), jnp.where(c == 0, t, which)
-            for name, out in ((Z, out_a), (X, out_db)):
-                for j in range(blocks):
-                    group = f * blocks + j
-                    at = rows((2 * name + s) * w, w)
-                    out[t, :, j * LANES:(j + 1) * LANES] = strips[group // 2, at, lanes(group % 2)]
+            for j in range(blocks):
+                group = f * blocks + j
+                out[t, :, j * LANES:(j + 1) * LANES] = strips[group // 2, rows(s), rows(group % 2)]
             at = half
-            for b in range(2 * m):
-                i, j = (f, s) if b >= m else (s, f)
-                out_db[t, :, at:at + LANES] = squares[b, rows(i * w, w), lanes(j)]
+            for b in range(n_b):
+                i, j = (f, s) if m <= b < 2 * m else (s, f)
+                out[t, :, at:at + LANES] = squares[b, rows(i), rows(j)]
                 at += LANES
-            if part.last:
-                for u in range(0, LANES, w):
-                    out_db[t, :, at:at + LANES] = squares[2 * m, rows(s * LANES + u, w), lanes(f)]
-                    at += LANES
-    for here, there in zip((keep_a, send_a, keep_db, send_db), outs):
-        copies.start("out", here, there)
+        copies.start("out", out, there)
     copies.wait("out")
 
 
-def load_sums(copies, t, parts, ins, held):
-    for k, _ in enumerate(parts):
-        for i in range(4):
-            copies.start("sums", ins[k][i].at[t], held[k][i])
-
-
-def sum_kernel(parts, role, *refs):
+def load_sums(copies, t, ins, held):
+    for there, here in zip(ins, held):
+        copies.start("sums", there.at[t], here)
+
+
+def sum_kernel(names, parts, role, *refs):
     refs = list(refs)
     take = lambda n: [refs.pop(0) for _ in range(n)]
-    ins = [take(4) for _ in parts]
-    out_a, out_d, out_b = take(3)
-    held = [take(4) for _ in parts]
+    n = 2 * sum(strip in names for strip in "ad")
+    ins = take(n * len(parts))
+    outs = take(len(names))
+    held = take(n * len(parts))
     y, c = role[0], role[1]
     copies = Copies(*refs)
-    load_sums(copies, jnp.where(c == 0, 1 - y, y), parts, ins, held)
+    load_sums(copies, jnp.where(c == 0, 1 - y, y), ins, held)
     copies.wait("sums")
     row, row_b = 0, 0
-    for part, (keep_a, got_a, keep_db, got_db) in zip(parts, held):
-        half, w = keep_a.shape[1], part.w
-        out_a[row:row + w] = keep_a[...] + got_a[...]
-        out_d[row:row + w] = keep_db[:, :half] + got_db[:, :half]
-        for i in range(len(part.pieces)):
-            cut = slice(half + i * LANES, half + (i + 1) * LANES)
-            out_b[row_b + i * w:row_b + (i + 1) * w] = keep_db[:, cut] + got_db[:, cut]
+    for part in parts:
+        w = part.w
+        if "a" in names:
+            keep, got = held.pop(0), held.pop(0)
+            outs[0][row:row + w] = keep[...] + got[...]
+        if "d" in names:
+            keep, got = held.pop(0), held.pop(0)
+            out_d, out_b = outs[-2:]
+            half = out_d.shape[1]
+            out_d[row:row + w] = keep[:, :half] + got[:, :half]
+            for i in range(len(part.pieces)):
+                cut = slice(half + i * LANES, half + (i + 1) * LANES)
+                out_b[row_b + i * w:row_b + (i + 1) * w] = keep[:, cut] + got[:, cut]
         row += w
         row_b += w * len(part.pieces)
 
@@ -311,68 +302,77 @@
     out[...] = annotated(adjust(corr, people_count), annot[...], TO_S)
 
 
-def final_kernel(width, people_count, phases, role, *refs):
+def final_kernel(width, people_count, name, phases, role, *refs):
     refs = list(refs)
     take = lambda n: [refs.pop(0) for _ in range(n)]
     every = [part for parts in phases for part in parts]
-    ins = [take(4) for _ in every]
-    data = [(parts, take(3)) for parts in phases]
-    own, x, z = take(2), take(2), take(2)
-    res_own, res_x, res_b, res_z = take(4)
+    is_a = name == "a"
+    ins = take(2 * len(every))
+    came = [take(1 if is_a else 2) for _ in phases]
+    own, x, z = take(3)
+    before = [] if is_a else take(2)
+    res = take(2 if is_a else 4)
     quad, turned_quad = take(2)
-    held = [take(4) for _ in every]
+    held = take(2 * len(every))
     y, c = role[0], role[1]
     half = quad.shape[0]
     s_keep = jnp.where(c == 0, y, 1 - y)
     copies = Copies(*refs)
-    load_sums(copies, s_keep, every, ins, held)
-    copies.wait("sums")
+    load_sums(copies, s_keep, ins, held)
+    sums = list(zip(every, held[::2], held[1::2]))
 
     def half_of(block, h):
         rows = pl.ds(pl.multiple_of(h * half, half), half)
-        return block[0][rows, :], block[1][0:8, rows], block[1][8:9, rows]
-
-    def fill(n, s_side, f_side):
-        if n == 2:
-            quad[...] = jnp.zeros_like(quad)
-            turned_quad[...] = jnp.zeros_like(turned_quad)
-        for part, (keep_a, got_a, keep_db, got_db) in zip(every, held):
-            rows = slice(part.at, part.at + part.w)
-            if n == 0:
-                quad[rows] = keep_a[...] + got_a[...]
-            elif n == 1:
-                quad[rows] = keep_db[:, :half] + got_db[:, :half]
-            else:
-                for i, (turned, row, at) in enumerate(part.pieces):
-                    cut = slice(half + i * LANES, half + (i + 1) * LANES)
-                    mine = turned_quad if turned else quad
-                    mine[row:row + part.w, at:at + LANES] += keep_db[:, cut] + got_db[:, cut]
-        for parts, got in data:
-            if n < 2:
-                turned_quad[parts[0].at:parts[-1].at + parts[-1].w] = got[n][...]
-                continue
+        first = [2 * half + pl.multiple_of((h * (half // LANES) + j) * 16, 16) for j in range(half // LANES)]
+        part = lambda more: jnp.concatenate([block[pl.ds(at + more, 8), :] for at in first], axis=1)
+        return block[rows, :], part(0), part(8)[0:1]
+
+    def finish(s_side, f_side):
+        corr = correlation(quad[...] + turned_quad[...].T, *s_side[1:], *f_side[1:], width, people_count)
+        return adjust(corr, people_count)
+
+    def strips(s_side, f_side):
+        for part, keep, got in sums:
+            quad[part.at:part.at + part.w] = keep[:, :half] + got[:, :half]
+        for parts, got in zip(phases, came):
+            turned_quad[parts[0].at:parts[-1].at + parts[-1].w] = got[0][...]
+        return finish(s_side, f_side)
+
+    def squares(s_side, f_side):
+        quad[...] = jnp.zeros_like(quad)
+        turned_quad[...] = jnp.zeros_like(turned_quad)
+        for part, keep, got in sums:
+            for i, (turned, row, at) in enumerate(part.pieces):
+                cut = slice(half + i * LANES, half + (i + 1) * LANES)
+                mine = turned_quad if turned else quad
+                mine[row:row + part.w, at:at + LANES] += keep[:, cut] + got[:, cut]
+        for parts, got in zip(phases, came):
             cut = 0
             for part in parts:
                 for turned, row, at in part.pieces:
                     theirs = quad if turned else turned_quad
-                    theirs[row:row + part.w, at:at + LANES] += got[2][cut:cut + part.w]
+                    theirs[row:row + part.w, at:at + LANES] += got[1][cut:cut + part.w]
                     cut += part.w
-        corr = correlation(quad[...] + turned_quad[...].T, *s_side[1:], *f_side[1:], width, people_count)
-        return adjust(corr, people_count)
-
-    own_f, x_f = half_of(own, y), half_of(x, y)
-    x_s, z_s = half_of(x, s_keep), half_of(z, s_keep)
-    adj = fill(0, z_s, own_f)
-    res_own[...] = annotated(adj, z_s[0], TO_F)
-    res_z[...] = annotated(adj, own_f[0], TO_S)
-    adj = fill(1, x_s, own_f)
-    res_own[...] += annotated(adj, x_s[0], TO_F)
-    res_x[...] = annotated(adj, own_f[0], TO_S)
-    adj = fill(2, z_s, x_f)
+        return finish(s_side, f_side)
+
+    own_f = half_of(own, y)
+    copies.wait("sums")
+    if is_a:
+        z_s = half_of(z, s_keep)
+        adj = strips(z_s, own_f)
+        res[0][...] = annotated(adj, z_s[0], TO_F)
+        res[1][...] = annotated(adj, own_f[0], TO_S)
+        return
+    res_own, res_x, res_b, res_z = res
+    x_s, x_f, z_s = half_of(x, s_keep), half_of(x, y), half_of(z, s_keep)
+    adj = strips(x_s, own_f)
+    res_own[...] = before[0][...] + annotated(adj, x_s[0], TO_F)
+    back_x = annotated(adj, own_f[0], TO_S)
+    adj = squares(z_s, x_f)
     back = annotated(adj, z_s[0], TO_F)
     res_b[...] = back
-    res_x[...] += jnp.where(c == 0, back, 0.0)
-    res_z[...] += annotated(adj, x_f[0], TO_S)
+    res_x[...] = back_x + jnp.where(c == 0, back, 0.0)
+    res_z[...] = before[1][...] + annotated(adj, x_f[0], TO_S)
 
 
 def route(groups, fn):
@@ -433,40 +433,44 @@
     wide = (2, *stack)
     dma = pltpu.SemaphoreType.DMA
 
-    def run_chunk(k, got, own, old):
+    def run_chunk(k, name, raw, own, old):
         part = parts[k]
-        w, n_b = part.w, len(part.pieces) * LANES
-        shapes = [(2, w, half)] * 2 + [(2, w, half + n_b)] * 2
+        first = not old
+        n_b = len(part.pieces) * (name == X)
+        shape = (2, part.w, half + n_b * LANES)
         size = 2 * LANES
-        *outs, high, low = call(
-            functools.partial(chunk_kernel, part, k == 0),
-            [(SMEM, role), (None, got[1]), (None, got[0])] + [(HBM, t) for t in own] + [(VMEM, t) for t in old],
-            [(s, F32, HBM) for s in shapes] + [(wide, BF16, VMEM)] * 2,
-            [VMEM((stack[0], 4 * w, size), F32), VMEM((2 * part.m + 1, size, size), F32)]
-            + [VMEM((4 * w, width), BF16)] * 2 + [col] + [VMEM(stack, BF16)] * 2
-            + [VMEM(s, F32) for s in shapes] + [dma((stack[0] + 1, 4))],
-            room=24, flops=1, moved=1,
-            aliases={5: 4, 6: 5} if k else {},
+        keep, sent, *outs = call(
+            functools.partial(chunk_kernel, part, name, first),
+            [(SMEM, role), (None, raw)] + [(HBM if first else VMEM, t) for t in own] + [(VMEM, t) for t in old],
+            [(shape, F32, HBM)] * 2 + [(wide, BF16, VMEM)] * 2 + ([(stack, BF16, VMEM)] * 2 if first else []),
+            [VMEM((stack[0], size, size), F32), VMEM((max(n_b, 1), size, size), F32)]
+            + [VMEM(shape, F32)] * 2 + [col, dma((stack[0] + 1, 4))],
+            room=14, flops=12 * part.w * width * (rows + 2 * n_b * LANES), moved=12 * part.w * width,
+            aliases={} if first else {4: 2, 5: 3},
         )
-        return outs, (high, low)
-
-    def send_pair(outs):
-        return outs[0], send(outs[1], "y"), outs[2], send(outs[3], "y_meet")
-
-    def held(part):
-        n_b = len(part.pieces) * LANES
-        return [VMEM((part.w, half), F32)] * 2 + [VMEM((part.w, half + n_b), F32)] * 2
-
-    def run_sum(chunk):
+        return keep, sent, outs[2:] if first else own, outs[:2]
+
+    def sums_of(names, chunk):
+        arrays, room = [], []
+        for k in chunk:
+            n_b = len(parts[k].pieces) * LANES
+            for i, n in ((0, half), (2, half + n_b)):
+                if "ad"[i // 2] in names:
+                    arrays += [(HBM, t) for t in pairs[k][i:i + 2]]
+                    room += [VMEM((parts[k].w, n), F32)] * 2
+        return arrays, room
+
+    def run_sum(names, chunk, role):
         phase = [parts[k] for k in chunk]
         n_rows = sum(part.w for part in phase)
-        shapes = [(n_rows, half)] * 2 + [(sum(part.w * len(part.pieces) for part in phase), LANES)]
+        arrays, held = sums_of(names, chunk)
+        shapes = [(n_rows, half)] * (len(names) - ("b" in names))
+        shapes += [(sum(part.w * len(part.pieces) for part in phase), LANES)] * ("b" in names)
         outs = call(
-            functools.partial(sum_kernel, phase), [(SMEM, role)] + [(HBM, t) for k in chunk for t in pairs[k]],
-            [(s, F32, None) for s in shapes], [t for part in phase for t in held(part)] + [dma((4 * len(phase),))],
-            room=10, flops=n_rows * half, moved=12 * n_rows * half,
+            functools.partial(sum_kernel, names, phase), [(SMEM, role)] + arrays, [(s, F32, None) for s in shapes],
+            held + [dma((len(held),))], room=10, flops=n_rows * half, moved=12 * n_rows * half,
         )
-        return [send(v, n) for v, n in zip(outs, ("pair_a", "pair_d", "pair_b"))]
+        return [send(v, "pair_" + n) for v, n in zip(outs, names)]
 
     got = send_block(0)
     shared = ((2, rows // 4, rows), F32, HBM)
@@ -492,49 +496,59 @@
     spread = (jnp.sum(moments[:, 1], axis=0) + width * jnp.sum(offsets * offsets, axis=0)) / people_count
     scale = lax.rsqrt(spread + 1e-06)
     annot = annotations.astype(F32)
-    stats = jnp.concatenate([offsets, jnp.zeros((8 - offsets.shape[0], rows), F32), scale[None]], axis=0)
-    side = jnp.concatenate([annot, stats.reshape(-1, LANES)], axis=0)
+    fill = lambda n: jnp.zeros((n, rows), F32)
+    stats = jnp.concatenate([offsets, fill(8 - offsets.shape[0]), scale[None], fill(7)], axis=0)
+    by_block = stats.reshape(16, -1, LANES).transpose(1, 0, 2).reshape(-1, LANES)
+    side = jnp.concatenate([annot, by_block], axis=0)
     got, own, raw, tile0_own, tile0_send, annot, stats, side = stage(
         (got, own, raw, tile0_own, tile0_send, annot, stats, side)
     )
 
     pairs, old = [], []
     n_parts = len(parts)
+    last = n_parts - 1
     tile0_came = send(tile0_send, "y")
     for k in range(n_parts):
-        coming = send_block(k + 1) if k + 1 < n_parts else ()
-        if k == n_parts - 1:
-            side = [send(side, name) for name in "xz"]
-        outs, old = run_chunk(k, got, own, old)
-        pair = send_pair(outs)
-        if k:
-            last = pairs.pop()
-            got, raw, old, last, own, side = stage((coming, raw, old, last, own, side))
-            pairs.append(last)
+        coming = send_block(k + 1) if k < last else ()
+        if k == last:
+            came = [send(side, name) for name in "xz"]
+        keep_a, sent, own, old = run_chunk(k, Z, got[1], own, old)
+        if k == 0:
+            sent, tile0_came = stage((sent, tile0_came))
+        came_a = send(sent, "y")
+        keep_db, sent, own, old = run_chunk(k, X, got[0], own, old)
+        sent, came_a = stage((sent, came_a))
+        pairs.append((keep_a, came_a, keep_db, send(sent, "y_meet")))
+        if k < last:
+            *held, came_db = pairs.pop()
+            got, raw, old, own, pairs, held = stage((coming, raw, old, own, pairs, held))
+            pairs.append((*held, came_db))
         else:
-            got, raw, old, own, side, tile0_came = stage((coming, raw, old, own, side, tile0_came))
-        pairs.append(pair)
-    tile0 = tile0_own, tile0_came
-    came = side
-    pairs[:3], _ = stage((pairs[:3], old))
-    received = [run_sum(chunk) for chunk in PHASES]
-    sides = [(annot, stats)] + [(t[:rows], t[rows:].reshape(stats.shape)) for t in came]
-
-    phases = [[parts[k] for k in chunk] for chunk in PHASES]
-    res = ((half, cats), F32, None)
-    res_own, res_x, res_b, res_z = call(
-        functools.partial(final_kernel, float(width), float(total), phases),
-        [(SMEM, role)] + [(HBM, t) for pair in pairs for t in pair]
-        + [(None, t) for group in received + sides for t in group],
-        [res] * 4, [VMEM((half, half), F32)] * 2 + [t for part in parts for t in held(part)] + [dma((4 * n_parts,))],
-        room=16, flops=24 * half * half * cats, moved=32 * half * half,
-    )
+            came, old = stage((came, old))
+    sides = [side, *came]
+    early, late = range(EARLY), range(EARLY, n_parts)
+    phases = [[parts[k] for k in chunk] for chunk in (early, late)]
+    sent_early = run_sum("adb", early, role)
     stats_rows = lax.dynamic_slice_in_dim(stats, p * (rows // 4), rows // 4, 1)
     (res_0,) = call(
         functools.partial(diagonal_kernel, float(width), float(total)),
-        [(None, t) for t in (*tile0, stats_rows, stats, annot)], [((rows // 4, cats), F32, None)],
+        [(None, t) for t in (tile0_own, tile0_came, stats_rows, stats, annot)], [((rows // 4, cats), F32, None)],
         flops=4 * rows * rows * cats, moved=rows * rows,
     )
+    sent_late = run_sum("adb", late, stage((role, res_0))[0])
+
+    def run_final(name, received, before, role):
+        arrays, held = sums_of(name, range(n_parts))
+        return call(
+            functools.partial(final_kernel, float(width), float(total), name, phases),
+            [(SMEM, role)] + arrays + [(None, t) for t in (*received, *sides, *before)],
+            [((half, cats), F32, None)] * (2 if name == "a" else 4),
+            [VMEM((half, half), F32)] * 2 + held + [dma((len(held),))],
+            room=14, flops=12 * half * half * cats, moved=16 * half * half,
+        )
+
+    res_a = run_final("a", [sent_early[0], sent_late[0]], (), role)
+    res_own, res_x, res_b, res_z = run_final("db", [*sent_early[1:], *sent_late[1:]], res_a, role)
     arrived = res_own + send(res_x, "res_x") + send(res_b, "res_b") + send(res_z, "res_z")
     arrived = arrived.reshape(2, half // 2, cats)
     choose = lambda index: lax.dynamic_index_in_dim(arrived, index, 0, keepdims=False)

time: 193 us -> 171 us (0.89)
  waiting for transfers between devices: 38.3 us -> 28 us
  starting transfers between devices: 62.8 us -> 58.9 us
  local copies, waits for them, and re-layouts: 9.53 us -> 6.01 us
  Pallas kernels: 76.5 us -> 73.5 us
    ppermute x32 -> x28, waiting for transfers between devices: 38.3 us -> 28 us  [send(): return lax.ppermute(value, AXES, routes[name])]
    ppermute x32 -> x28, starting transfers between devices: 62.8 us -> 58.9 us  [send(): return lax.ppermute(value, AXES, routes[name])]
    pallas_call x9 -> x12, Pallas kernels: 76.5 us -> 73.5 us  [call(): pl.pallas_call(kernel, out_shape=[m(s, d) if m else jax.ShapeDtypeStruct(...]
    unnamed x40 -> x28, local copies, waits for them, and re-layouts: 4.81 us -> 2.39 us
  transfers between devices with their start and end apart: 32 -> 28, of which waited for: 16 -> 13; matrix products, arithmetic and copies ran while one was open for 2% -> 2% of each run, Pallas kernels for 36% -> 40%
where the time goes in v2:
time: 171 us
  Pallas kernels  73.5 us (43%)
  starting transfers between devices  58.9 us (34%)
  waiting for transfers between devices  28 us (16%)
  local copies, waits for them, and re-layouts  6.01 us (4%)
  other arithmetic  3.46 us (2%)
    pallas_call x12, Pallas kernels, call(): pl.pallas_call(kernel, out_shape=[m(s, d) if m else jax.ShapeDtypeStruct(...  73.5 us
    ppermute x28, starting transfers between devices, send(): return lax.ppermute(value, AXES, routes[name])  58.9 us
    ppermute x28, waiting for transfers between devices, send(): return lax.ppermute(value, AXES, routes[name])  28 us
  transfers between devices with their start and end apart: 28, of which 13 were waited for; matrix products, arithmetic and copies ran while one was open for 2% of the time, Pallas kernels for 40%

profile of v2, /device:TPU:23, one launch (start us, length us, event | category | flops | bytes accessed | tf_op | source)
XLA Modules:
  0.0 170.5 jit_solution(13344240879992126522)
XLA Ops:
  0.0 3.2 %slice.13 = f32[2,128,2048]{2,1,0:T(8,128)} slice(f32[2,384,2048]{2,1,0:T(8,128)} %bitcast.26), slice={[0:2], [0:128], [0:2048]} | slice | bytes 4194304 | tf_op jit(solution)/shard_map/slice | solution.py:424
  3.2 1.3 collective-permute-start
  4.5 3.2 %collective-permute-start.1 = (f32[2,128,2048]{2,1,0:T(8,128)}, f32[2,128,2048]{2,1,0:T(8,128)}, u32[]{:S(2)}, u32[]{:S(2)}) collective-permute-start(f32[2,128,2048]{2,1,0:T(8,128)} %slice.13), channel_id=1, source_target_pairs={{1,9},{3,11},{5,13},{7,15},{8,0},{9,17},{10,2},{11,19},{12,4},{13,... | collective-permute-start | bytes 6291464 | tf_op jit(solution)/shard_map/ppermute | solution.py:422
  7.8 14.2 %shard_map.28 = (bf16[3,256,2048]{2,1,0:T(8,128)(2,1)}, bf16[3,256,2048]{2,1,0:T(8,128)(2,1)}, f32[2,192,768]{2,1,0:T(8,128)}, f32[2,192,768]{2,1,0:T(8,128)}, f...) custom-call(s32[2]{0:T(128)S(1)} %pad_add_fusion.role, f32[768,2048]{1,0:T(8,128)} %dose_hbm.1), custom_call_target="tpu_custom_call" | custom-call | flops 4831838208 | bytes 6291456 | tf_op jit(solution)/shard_map/pallas_call | solution.py:43
  22.1 1.2 collective-permute-start.3
  23.2 0.8 collective-permute-done.3
  24.1 0.3 collective-permute-start.4
  24.4 0.6 collective-permute-start.2
  25.0 0.1 pad.7.clone
  25.1 0.1 pad.9.clone
  25.2 1.9 %collective-permute-done.4 = f32[2,2,768]{2,0,1:T(2,128)S(1)} collective-permute-done((f32[2,2,768]{2,0,1:T(2,128)S(1)}, f32[2,2,768]{2,0,1:T(2,128)S(1)}, u32[]{:S(2)}, u32[]{:S(2)}) %collective-permute-start.4) | collective-permute-done | bytes 12320 | tf_op jit(solution)/shard_map/ppermute | solution.py:422
  27.2 0.1 maximum_maximum_fusion.1
  27.4 0.7 maximum_maximum_fusion.stats
  28.1 1.8 %add.88 = f32[2,192,768]{2,1,0:T(8,128)S(1)} add(f32[2,192,768]{2,1,0:T(8,128)} %get-tuple-element.111, f32[2,192,768]{2,1,0:T(8,128)} %collective-permute-done.2) | non-fusion elementwise | flops 294912 | bytes 3538944 | tf_op jit(solution)/shard_map/add | solution.py:487
  29.8 0.1 dynamic-slice_bitcast_fusion
  29.9 0.7 collective-permute-done.raw
  30.6 1.3 collective-permute-done.1.raw
  31.9 1.3 collective-permute-start.5
  33.2 2.9 %collective-permute-start.6 = (f32[2,128,2048]{2,1,0:T(8,128)S(1)}, f32[2,128,2048]{2,1,0:T(8,128)S(1)}, u32[]{:S(2)}, u32[]{:S(2)}) collective-permute-start(f32[2,128,2048]{2,1,0:T(8,128)S(1)} %copy-done.13), channel_id=1, source_target_pairs={{1,9},{3,11},{5,13},{7,15},{8,0},{9,17},{10,2},{11,19},{12,4},{13,... | collective-permute-start | bytes 6291464 | tf_op jit(solution)/shard_map/ppermute | solution.py:422
  36.1 0.7 collective-permute-start.7
  36.8 7.3 %shard_map.29 = (f32[2,128,384]{2,1,0:T(8,128)}, f32[2,128,384]{2,1,0:T(8,128)}, bf16[2,3,256,2048]{3,2,1,0:T(8,128)(2,1)S(1)}, bf16[2,3,256,2048]{3,2,1,0:T(8,1...) custom-call(s32[2]{0:T(128)S(1)} %pad_add_fusion.role, ...), custom_call_target="tpu_custom_call" | custom-call | flops 2415919104 | bytes 3145728 | tf_op jit(solution)/shard_map/pallas_call | solution.py:43
  44.1 4.5 %collective-permute-done.7.tile_pair = f32[192,768]{1,0:T(8,128)S(1)} collective-permute-done((f32[192,768]{1,0:T(8,128)S(1)}, f32[192,768]{1,0:T(8,128)S(1)}, u32[]{:S(2)}, u32[]{:S(2)}) %collective-permute-start.7) | collective-permute-done | bytes 589856 | tf_op jit(solution)/shard_map/ppermute | solution.py:422
  48.6 1.0 collective-permute-start.8
  49.6 6.7 %shard_map.30 = (f32[2,128,512]{2,1,0:T(8,128)}, f32[2,128,512]{2,1,0:T(8,128)}, bf16[2,3,256,2048]{3,2,1,0:T(8,128)(2,1)S(1)}, bf16[2,3,256,2048]{3,2,1,0:T(8,128)(2,1)S(1)}) custom-call(s32[2]{0:T(128)S(1)} %pad_add_fusion.role, f32[2,128,2048]{2,1,0:T(8,128)S(1)} %collective-permute-done.raw, ...), custom_call_target="tpu_custom_call", output_to_operand_aliasing={{2}: (4, {}), {3}: (5, {})} | custom-call | flops 3221225472 | bytes 3145728 | tf_op jit(solution)/shard_map/pallas_call | solution.py:43
  56.3 2.6 %collective-permute-done.5.raw = f32[2,128,2048]{2,1,0:T(8,128)S(1)} collective-permute-done((f32[2,128,2048]{2,1,0:T(8,128)S(1)}, f32[2,128,2048]{2,1,0:T(8,128)S(1)}, u32[]{:S(2)}, u32[]{:S(2)}) %collective-permute-start.5) | collective-permute-done | bytes 2097184 | tf_op jit(solution)/shard_map/ppermute | solution.py:422
  59.0 1.3 collective-permute-done.6.raw
  60.3 2.6 %collective-permute-start.10 = (f32[2,128,2048]{2,1,0:T(8,128)S(1)}, f32[2,128,2048]{2,1,0:T(8,128)S(1)}, u32[]{:S(2)}, u32[]{:S(2)}) collective-permute-start(f32[2,128,2048]{2,1,0:T(8,128)S(1)} %copy-done.12), channel_id=1, source_target_pairs={{1,9},{3,11},{5,13},{7,15},{8,0},{9,17},{10,2},{11,19},{12,4},{13,... | collective-permute-start | bytes 6291464 | tf_op jit(solution)/shard_map/ppermute | solution.py:422
  62.9 1.3 collective-permute-start.9
  64.2 2.5 %collective-permute-start.11 = (f32[2,128,512]{2,1,0:T(8,128)}, f32[2,128,512]{2,1,0:T(8,128)S(1)}, u32[]{:S(2)}, u32[]{:S(2)}) collective-permute-start(f32[2,128,512]{2,1,0:T(8,128)} %get-tuple-element.147), channel_id=1, source_target_pairs={{0,2},{2,0},{5,7},{7,5},{8,10},{10,8},{13,15},{15,13},{16,18},{18,... | collective-permute-start | bytes 1572872 | tf_op jit(solution)/shard_map/ppermute | solution.py:422
  66.7 5.5 %shard_map.31 = (f32[2,128,384]{2,1,0:T(8,128)}, f32[2,128,384]{2,1,0:T(8,128)}, bf16[2,3,256,2048]{3,2,1,0:T(8,128)(2,1)S(1)}, bf16[2,3,256,2048]{3,2,1,0:T(8,128)(2,1)S(1)}) custom-call(s32[2]{0:T(128)S(1)} %pad_add_fusion.role, f32[2,128,2048]{2,1,0:T(8,128)S(1)} %collective-permute-done.6.raw, ...), custom_call_target="tpu_custom_call", output_to_operand_aliasing={{2}: (4, {}), {3}: (5, {})} | custom-call | flops 2415919104 | bytes 3145728 | tf_op jit(solution)/shard_map/pallas_call | solution.py:43
  72.3 0.9 collective-permute-start.12
  73.2 8.9 %shard_map.32 = (f32[2,128,768]{2,1,0:T(8,128)}, f32[2,128,768]{2,1,0:T(8,128)}, bf16[2,3,256,2048]{3,2,1,0:T(8,128)(2,1)S(1)}, bf16[2,3,256,2048]{3,2,1,0:T(8,128)(2,1)S(1)}) custom-call(s32[2]{0:T(128)S(1)} %pad_add_fusion.role, f32[2,128,2048]{2,1,0:T(8,128)S(1)} %collective-permute-done.5.raw, ...), custom_call_target="tpu_custom_call", output_to_operand_aliasing={{2}: (4, {}), {3}: (5, {})} | custom-call | flops 4831838208 | bytes 3145728 | tf_op jit(solution)/shard_map/pallas_call | solution.py:43
  82.1 2.7 %collective-permute-start.13 = (f32[2,128,768]{2,1,0:T(8,128)}, f32[2,128,768]{2,1,0:T(8,128)S(1)}, u32[]{:S(2)}, u32[]{:S(2)}) collective-permute-start(f32[2,128,768]{2,1,0:T(8,128)} %get-tuple-element.156), channel_id=1, source_target_pairs={{0,2},{2,0},{5,7},{7,5},{8,10},{10,8},{13,15},{15,13},{16,18},{18,... | collective-permute-start | bytes 2359304 | tf_op jit(solution)/shard_map/ppermute | solution.py:422
  84.8 2.5 %collective-permute-done.10.raw = f32[2,128,2048]{2,1,0:T(8,128)S(1)} collective-permute-done((f32[2,128,2048]{2,1,0:T(8,128)S(1)}, f32[2,128,2048]{2,1,0:T(8,128)S(1)}, u32[]{:S(2)}, u32[]{:S(2)}) %collective-permute-start.10) | collective-permute-done | bytes 2097184 | tf_op jit(solution)/shard_map/ppermute | solution.py:422
  87.3 3.9 %collective-permute-done.9.raw = f32[2,128,2048]{2,1,0:T(8,128)S(1)} collective-permute-done((f32[2,128,2048]{2,1,0:T(8,128)S(1)}, f32[2,128,2048]{2,1,0:T(8,128)S(1)}, u32[]{:S(2)}, u32[]{:S(2)}) %collective-permute-start.9) | collective-permute-done | bytes 2097184 | tf_op jit(solution)/shard_map/ppermute | solution.py:422
  91.3 5.6 %shard_map.33 = (f32[2,128,384]{2,1,0:T(8,128)}, f32[2,128,384]{2,1,0:T(8,128)}, bf16[2,3,256,2048]{3,2,1,0:T(8,128)(2,1)S(1)}, bf16[2,3,256,2048]{3,2,1,0:T(8,128)(2,1)S(1)}) custom-call(s32[2]{0:T(128)S(1)} %pad_add_fusion.role, f32[2,128,2048]{2,1,0:T(8,128)S(1)} %collective-permute-done.10.raw, ...), custom_call_target="tpu_custom_call", output_to_operand_aliasing={{2}: (4, {}), {3}: (5, {})} | custom-call | flops 2415919104 | bytes 3145728 | tf_op jit(solution)/shard_map/pallas_call | solution.py:43
  96.9 0.5 collective-permute-start.14
  97.3 11.2 %shard_map.34 = (f32[2,128,1024]{2,1,0:T(8,128)}, f32[2,128,1024]{2,1,0:T(8,128)}, bf16[2,3,256,2048]{3,2,1,0:T(8,128)(2,1)S(1)}, bf16[2,3,256,2048]{3,2,1,0:T(8,128)(2,1)S(1)}) custom-call(s32[2]{0:T(128)S(1)} %pad_add_fusion.role, f32[2,128,2048]{2,1,0:T(8,128)S(1)} %collective-permute-done.9.raw, ...), custom_call_target="tpu_custom_call", output_to_operand_aliasing={{2}: (4, {}), {3}: (5, {})} | custom-call | flops 6442450944 | bytes 3145728 | tf_op jit(solution)/shard_map/pallas_call | solution.py:43
  108.5 3.1 %collective-permute-start.15 = (f32[2,128,1024]{2,1,0:T(8,128)}, f32[2,128,1024]{2,1,0:T(8,128)}, u32[]{:S(2)}, u32[]{:S(2)}) collective-permute-start(f32[2,128,1024]{2,1,0:T(8,128)} %get-tuple-element.168), channel_id=1, source_target_pairs={{0,2},{2,0},{5,7},{7,5},{8,10},{10,8},{13,15},{15,13},{16,18},{18,... | collective-permute-start | bytes 3145736 | tf_op jit(solution)/shard_map/ppermute | solution.py:422
  111.7 1.3 collective-permute-start.20
  113.0 1.9 %collective-permute-start.21 = (f32[864,128]{1,0:T(8,128)S(1)}, f32[864,128]{1,0:T(8,128)S(1)}, u32[]{:S(2)}, u32[]{:S(2)}) collective-permute-start(f32[864,128]{1,0:T(8,128)S(1)} %pad_maximum_fusion.refs_8_.refs_10_), channel_id=1, source_target_pairs={{1,9},{3,11},{5,13},{7,15},{8,0},{9,17},{10,2},{11,19},{12,4},{13,... | collective-permute-start | bytes 1327112 | tf_op jit(solution)/shard_map/ppermute | solution.py:422
  114.9 0.9 copy-done.6
  115.8 3.0 %shard_map.35 = (f32[256,384]{1,0:T(8,128)}, f32[256,384]{1,0:T(8,128)S(1)}, f32[512,128]{1,0:T(8,128)S(1)}) custom-call(s32[2]{0:T(128)S(1)} %pad_add_fusion.role, f32[2,128,384]{2,1,0:T(8,128)} %get-tuple-element.169.refs_0_, f32[2,128,384]{2,1,0:T(8,128)} %copy-done.8, f32[2,128,512]{2,1,0:T(8,128)} %get-tuple-element.153.refs_2_.refs_0_, ...), custom_call_target="tpu_custom_call" | custom-call | flops 98304 | bytes 1179648 | tf_op jit(solution)/shard_map/pallas_call | solution.py:43
  118.8 0.7 copy-done.3
  119.6 0.7 copy-done.4
  120.3 7.0 %collective-permute-start.22 = (f32[256,384]{1,0:T(8,128)}, f32[256,384]{1,0:T(8,128)S(1)}, u32[]{:S(2)}, u32[]{:S(2)}) collective-permute-start(f32[256,384]{1,0:T(8,128)} %get-tuple-element.187), channel_id=1, source_target_pairs={{0,9},{2,11},{4,13},{6,15},{8,17},{9,0},{10,19},{11,2},{12,21},{13... | collective-permute-start | bytes 1179656 | tf_op jit(solution)/shard_map/ppermute | solution.py:422
  127.3 2.1 %collective-permute-start.16 = (f32[256,384]{1,0:T(8,128)}, f32[256,384]{1,0:T(8,128)S(1)}, u32[]{:S(2)}, u32[]{:S(2)}) collective-permute-start(f32[256,384]{1,0:T(8,128)} %copy-done.3), channel_id=1, source_target_pairs={{0,5},{2,7},{5,0},{7,2},{8,13},{10,15},{13,8},{15,10},{16,21},{18,... | collective-permute-start | bytes 1179656 | tf_op jit(solution)/shard_map/ppermute | solution.py:422
  129.4 0.1 constant_dynamic-slice_fusion.stats_rows
  129.4 1.1 shard_map.36
  130.6 2.1 %shard_map.37 = (f32[128,384]{1,0:T(8,128)S(1)}, f32[128,384]{1,0:T(8,128)S(1)}, f32[640,128]{1,0:T(8,128)S(1)}) custom-call(s32[2]{0:T(128)S(1)} %pad_add_fusion.role, f32[2,128,384]{2,1,0:T(8,128)} %get-tuple-element.180.refs_0_.refs_4_, f32[2,128,384]{2,1,0:T(8,128)} %copy-done.10, f32[2,128,1024]{2,1,0:T(8,128)} %get-tuple-element.165.refs_2_.refs_4_, ...), custom_call_target="tpu_custom_call" | custom-call | flops 49152 | bytes 589824 | tf_op jit(solution)/shard_map/pallas_call | solution.py:43
  132.7 1.9 %collective-permute-start.19 = (f32[640,128]{1,0:T(8,128)S(1)}, f32[640,128]{1,0:T(8,128)S(1)}, u32[]{:S(2)}, u32[]{:S(2)}) collective-permute-start(f32[640,128]{1,0:T(8,128)S(1)} %get-tuple-element.183), channel_id=1, source_target_pairs={{0,13},{2,15},{8,21},{10,23},{13,0},{15,2},{16,29},{18,31},{21,8},... | collective-permute-start | bytes 983048 | tf_op jit(solution)/shard_map/ppermute | solution.py:422
  134.6 4.5 %collective-permute-start.17 = (f32[512,128]{1,0:T(8,128)S(1)}, f32[512,128]{1,0:T(8,128)S(1)}, u32[]{:S(2)}, u32[]{:S(2)}) collective-permute-start(f32[512,128]{1,0:T(8,128)S(1)} %copy-done.5), channel_id=1, source_target_pairs={{0,13},{2,15},{8,21},{10,23},{13,0},{15,2},{16,29},{18,31},{21,8},... | collective-permute-start | bytes 786440 | tf_op jit(solution)/shard_map/ppermute | solution.py:422
  139.2 1.9 %collective-permute-start.23 = (f32[128,384]{1,0:T(8,128)S(1)}, f32[128,384]{1,0:T(8,128)S(1)}, u32[]{:S(2)}, u32[]{:S(2)}) collective-permute-start(f32[128,384]{1,0:T(8,128)S(1)} %get-tuple-element.188), channel_id=1, source_target_pairs={{0,9},{2,11},{4,13},{6,15},{8,17},{9,0},{10,19},{11,2},{12,21},{13... | collective-permute-start | bytes 589832 | tf_op jit(solution)/shard_map/ppermute | solution.py:422
  141.1 3.6 %collective-permute-start.18 = (f32[128,384]{1,0:T(8,128)S(1)}, f32[128,384]{1,0:T(8,128)S(1)}, u32[]{:S(2)}, u32[]{:S(2)}) collective-permute-start(f32[128,384]{1,0:T(8,128)S(1)} %get-tuple-element.182), channel_id=1, source_target_pairs={{0,5},{2,7},{5,0},{7,2},{8,13},{10,15},{13,8},{15,10},{16,21},{18,... | collective-permute-start | bytes 589832 | tf_op jit(solution)/shard_map/ppermute | solution.py:422
  144.8 1.7 collective-permute-done.23.refs_7_
  146.5 3.4 %shard_map.38 = (f32[384,128]{1,0:T(8,128)S(1)}, f32[384,128]{1,0:T(8,128)S(1)}) custom-call(s32[2]{0:T(128)S(1)} %pad_add_fusion.role, f32[2,128,384]{2,1,0:T(8,128)} %get-tuple-element.169.refs_0_, f32[2,128,384]{2,1,0:T(8,128)} %copy-done.8, f32[2,128,384]{2,1,0:T(8,128)} %get-tuple-element.171.refs_4_.refs_2_, f32[2,128,384]{2,1,0:T(8,128)} %copy-done.9, ...), custom_call_target="tpu_custom_call" | custom-call | flops 226492416 | bytes 2359296 | tf_op jit(solution)/shard_map/pallas_call | solution.py:43
  149.9 4.7 %shard_map.39 = (f32[384,128]{1,0:T(8,128)S(1)}, f32[384,128]{1,0:T(8,128)S(1)}, f32[384,128]{1,0:T(8,128)S(1)}, f32[384,128]{1,0:T(8,128)S(1)}) custom-call(s32[2]{0:T(128)S(1)} %pad_add_fusion.role, f32[2,128,512]{2,1,0:T(8,128)} %get-tuple-element.153.refs_2_.refs_0_, f32[2,128,512]{2,1,0:T(8,128)} %copy-done.7, ...), custom_call_target="tpu_custom_call" | custom-call | flops 226492416 | bytes 2359296 | tf_op jit(solution)/shard_map/pallas_call | solution.py:43
  154.6 2.8 %collective-permute-start.24 = (f32[384,128]{1,0:T(8,128)S(1)}, f32[384,128]{1,0:T(8,128)S(1)}, u32[]{:S(2)}, u32[]{:S(2)}) collective-permute-start(f32[384,128]{1,0:T(8,128)S(1)} %get-tuple-element.192), channel_id=1, source_target_pairs={{0,4},{2,6},{5,3},{7,1},{8,12},{10,14},{13,11},{15,9},{16,20},{18,... | collective-permute-start | bytes 589832 | tf_op jit(solution)/shard_map/ppermute | solution.py:422
  157.4 3.7 %collective-permute-start.25 = (f32[384,128]{1,0:T(8,128)S(1)}, f32[384,128]{1,0:T(8,128)S(1)}, u32[]{:S(2)}, u32[]{:S(2)}) collective-permute-start(f32[384,128]{1,0:T(8,128)S(1)} %get-tuple-element.193), channel_id=1, source_target_pairs={{5,0},{7,2},{13,8},{15,10},{21,16},{23,18},{29,24},{31,26}} | collective-permute-start | bytes 589832 | tf_op jit(solution)/shard_map/ppermute | solution.py:422
  161.1 1.9 %collective-permute-start.26 = (f32[384,128]{1,0:T(8,128)S(1)}, f32[384,128]{1,0:T(8,128)S(1)}, u32[]{:S(2)}, u32[]{:S(2)}) collective-permute-start(f32[384,128]{1,0:T(8,128)S(1)} %get-tuple-element.194), channel_id=1, source_target_pairs={{0,8},{2,10},{4,12},{6,14},{8,16},{9,3},{10,18},{11,1},{12,20},{13... | collective-permute-start | bytes 589832 | tf_op jit(solution)/shard_map/ppermute | solution.py:422
  163.1 0.6 collective-permute-done.25
  163.7 4.7 %collective-permute-done.26 = f32[384,128]{1,0:T(8,128)S(1)} collective-permute-done((f32[384,128]{1,0:T(8,128)S(1)}, f32[384,128]{1,0:T(8,128)S(1)}, u32[]{:S(2)}, u32[]{:S(2)}) %collective-permute-start.26) | collective-permute-done | bytes 196640 | tf_op jit(solution)/shard_map/ppermute | solution.py:422
  168.6 1.3 collective-permute-done.27
  169.9 0.7 fusion
  (60 shorter events, 0.5 us)
Async XLA Ops:
  3.2 27.4 %collective-permute-start = (f32[2,128,2048]{2,1,0:T(8,128)}, f32[2,128,2048]{2,1,0:T(8,128)S(1)}, u32[]{:S(2)}, u32[]{:S(2)}) collective-permute-start(f32[2,128,2048]{2,1,0:T(8,128)} %slice.13), channel_id=1, source_target_pairs={{1,5},{3,7},{4,0},{6,2},{9,13},{11,15},{12,8},{14,10},{17,21},{19,... | collective-permute-start | bytes 6291464 | tf_op jit(solution)/shard_map/ppermute | solution.py:422
  4.5 27.4 %collective-permute-start.1 = (f32[2,128,2048]{2,1,0:T(8,128)}, f32[2,128,2048]{2,1,0:T(8,128)}, u32[]{:S(2)}, u32[]{:S(2)}) collective-permute-start(f32[2,128,2048]{2,1,0:T(8,128)} %slice.13), channel_id=1, source_target_pairs={{1,9},{3,11},{5,13},{7,15},{8,0},{9,17},{10,2},{11,19},{12,4},{13,... | collective-permute-start | bytes 6291464 | tf_op jit(solution)/shard_map/ppermute | solution.py:422
  7.8 17.3 %copy-start.11 = (s32[768,128]{1,0:T(8,128)S(1)}, s32[768,128]{1,0:T(8,128)}, u32[]{:S(2)}) copy-start(s32[768,128]{1,0:T(8,128)} %param.3) | copy-start | bytes 1179652
  22.1 2.0 %collective-permute-start.3 = (f32[1,2,768]{2,0,1:T(1,128)S(1)}, f32[1,2,768]{2,0,1:T(1,128)S(1)}, u32[]{:S(2)}, u32[]{:S(2)}) collective-permute-start(f32[1,2,768]{2,0,1:T(1,128)S(1)} %reshape.96), channel_id=1, source_target_pairs={{0,1},{1,0},{2,3},{3,2},{4,5},{5,4},{6,7},{7,6},{8,9},{9,8},{10,11... | collective-permute-start | bytes 18440 | tf_op jit(solution)/shard_map/ppermute | solution.py:422
  24.1 3.0 %collective-permute-start.4 = (f32[2,2,768]{2,0,1:T(2,128)S(1)}, f32[2,2,768]{2,0,1:T(2,128)S(1)}, u32[]{:S(2)}, u32[]{:S(2)}) collective-permute-start(f32[2,2,768]{2,0,1:T(2,128)S(1)} %pad_maximum_fusion.2), channel_id=1, source_target_pairs={{0,2},{1,3},{2,0},{3,1},{4,6},{5,7},{6,4},{7,5},{8,10},{9,11},{10,... | collective-permute-start | bytes 36872 | tf_op jit(solution)/shard_map/ppermute | solution.py:422
  24.4 3.7 %collective-permute-start.2 = (f32[2,192,768]{2,1,0:T(8,128)}, f32[2,192,768]{2,1,0:T(8,128)}, u32[]{:S(2)}, u32[]{:S(2)}) collective-permute-start(f32[2,192,768]{2,1,0:T(8,128)} %get-tuple-element.112), channel_id=1, source_target_pairs={{0,1},{1,0},{2,3},{3,2},{4,5},{5,4},{6,7},{7,6},{8,9},{9,8},{10,11... | collective-permute-start | bytes 3538952 | tf_op jit(solution)/shard_map/ppermute | solution.py:422
  27.4 4.6 %copy-start.13 = (f32[2,128,2048]{2,1,0:T(8,128)S(1)}, f32[2,128,2048]{2,1,0:T(8,128)}, u32[]{:S(2)}) copy-start(f32[2,128,2048]{2,1,0:T(8,128)} %get-tuple-element.114) | copy-start | bytes 6291460
  31.9 27.1 %collective-permute-start.5 = (f32[2,128,2048]{2,1,0:T(8,128)S(1)}, f32[2,128,2048]{2,1,0:T(8,128)S(1)}, u32[]{:S(2)}, u32[]{:S(2)}) collective-permute-start(f32[2,128,2048]{2,1,0:T(8,128)S(1)} %copy-done.13), channel_id=1, source_target_pairs={{1,5},{3,7},{4,0},{6,2},{9,13},{11,15},{12,8},{14,10},{17,21},{19,... | collective-permute-start | bytes 6291464 | tf_op jit(solution)/shard_map/ppermute | solution.py:422
  33.2 27.1 %collective-permute-start.6 = (f32[2,128,2048]{2,1,0:T(8,128)S(1)}, f32[2,128,2048]{2,1,0:T(8,128)S(1)}, u32[]{:S(2)}, u32[]{:S(2)}) collective-permute-start(f32[2,128,2048]{2,1,0:T(8,128)S(1)} %copy-done.13), channel_id=1, source_target_pairs={{1,9},{3,11},{5,13},{7,15},{8,0},{9,17},{10,2},{11,19},{12,4},{13,... | collective-permute-start | bytes 6291464 | tf_op jit(solution)/shard_map/ppermute | solution.py:422
  36.1 12.5 %collective-permute-start.7 = (f32[192,768]{1,0:T(8,128)S(1)}, f32[192,768]{1,0:T(8,128)S(1)}, u32[]{:S(2)}, u32[]{:S(2)}) collective-permute-start(f32[192,768]{1,0:T(8,128)S(1)} %get-tuple-element.129), channel_id=1, source_target_pairs={{0,2},{1,3},{2,0},{3,1},{4,6},{5,7},{6,4},{7,5},{8,10},{9,11},{10,... | collective-permute-start | bytes 1769480 | tf_op jit(solution)/shard_map/ppermute | solution.py:422
  48.6 7.7 %copy-start = (f32[192,768]{1,0:T(8,128)}, f32[192,768]{1,0:T(8,128)S(1)}, u32[]{:S(2)}) copy-start(f32[192,768]{1,0:T(8,128)S(1)} %collective-permute-done.7.tile_pair) | copy-start | bytes 1769476
  48.6 7.7 %collective-permute-start.8 = (f32[2,128,384]{2,1,0:T(8,128)}, f32[2,128,384]{2,1,0:T(8,128)S(1)}, u32[]{:S(2)}, u32[]{:S(2)}) collective-permute-start(f32[2,128,384]{2,1,0:T(8,128)} %get-tuple-element.130), channel_id=1, source_target_pairs={{0,2},{1,3},{2,0},{3,1},{4,6},{5,7},{6,4},{7,5},{8,10},{9,11},{10,... | collective-permute-start | bytes 1179656 | tf_op jit(solution)/shard_map/ppermute | solution.py:422
  49.6 10.6 %copy-start.12 = (f32[2,128,2048]{2,1,0:T(8,128)S(1)}, f32[2,128,2048]{2,1,0:T(8,128)}, u32[]{:S(2)}) copy-start(f32[2,128,2048]{2,1,0:T(8,128)} %get-tuple-element.133) | copy-start | bytes 6291460
  56.3 16.0 %copy-start.8 = (f32[2,128,384]{2,1,0:T(8,128)}, f32[2,128,384]{2,1,0:T(8,128)S(1)}, u32[]{:S(2)}) copy-start(f32[2,128,384]{2,1,0:T(8,128)S(1)} %collective-permute-done.8.refs_1_) | copy-start | bytes 1179652
  60.3 27.1 %collective-permute-start.10 = (f32[2,128,2048]{2,1,0:T(8,128)S(1)}, f32[2,128,2048]{2,1,0:T(8,128)S(1)}, u32[]{:S(2)}, u32[]{:S(2)}) collective-permute-start(f32[2,128,2048]{2,1,0:T(8,128)S(1)} %copy-done.12), channel_id=1, source_target_pairs={{1,9},{3,11},{5,13},{7,15},{8,0},{9,17},{10,2},{11,19},{12,4},{13,... | collective-permute-start | bytes 6291464 | tf_op jit(solution)/shard_map/ppermute | solution.py:422
  62.9 28.4 %collective-permute-start.9 = (f32[2,128,2048]{2,1,0:T(8,128)S(1)}, f32[2,128,2048]{2,1,0:T(8,128)S(1)}, u32[]{:S(2)}, u32[]{:S(2)}) collective-permute-start(f32[2,128,2048]{2,1,0:T(8,128)S(1)} %copy-done.12), channel_id=1, source_target_pairs={{1,5},{3,7},{4,0},{6,2},{9,13},{11,15},{12,8},{14,10},{17,21},{19,... | collective-permute-start | bytes 6291464 | tf_op jit(solution)/shard_map/ppermute | solution.py:422
  64.2 20.6 %collective-permute-start.11 = (f32[2,128,512]{2,1,0:T(8,128)}, f32[2,128,512]{2,1,0:T(8,128)S(1)}, u32[]{:S(2)}, u32[]{:S(2)}) collective-permute-start(f32[2,128,512]{2,1,0:T(8,128)} %get-tuple-element.147), channel_id=1, source_target_pairs={{0,2},{2,0},{5,7},{7,5},{8,10},{10,8},{13,15},{15,13},{16,18},{18,... | collective-permute-start | bytes 1572872 | tf_op jit(solution)/shard_map/ppermute | solution.py:422
  72.3 9.8 %collective-permute-start.12 = (f32[2,128,384]{2,1,0:T(8,128)}, f32[2,128,384]{2,1,0:T(8,128)S(1)}, u32[]{:S(2)}, u32[]{:S(2)}) collective-permute-start(f32[2,128,384]{2,1,0:T(8,128)} %get-tuple-element.150), channel_id=1, source_target_pairs={{0,2},{1,3},{2,0},{3,1},{4,6},{5,7},{6,4},{7,5},{8,10},{9,11},{10,... | collective-permute-start | bytes 1179656 | tf_op jit(solution)/shard_map/ppermute | solution.py:422
  82.1 14.8 %copy-start.9 = (f32[2,128,384]{2,1,0:T(8,128)}, f32[2,128,384]{2,1,0:T(8,128)S(1)}, u32[]{:S(2)}) copy-start(f32[2,128,384]{2,1,0:T(8,128)S(1)} %collective-permute-done.12.refs_5_.refs_3_) | copy-start | bytes 1179652
  82.1 32.8 %collective-permute-start.13 = (f32[2,128,768]{2,1,0:T(8,128)}, f32[2,128,768]{2,1,0:T(8,128)S(1)}, u32[]{:S(2)}, u32[]{:S(2)}) collective-permute-start(f32[2,128,768]{2,1,0:T(8,128)} %get-tuple-element.156), channel_id=1, source_target_pairs={{0,2},{2,0},{5,7},{7,5},{8,10},{10,8},{13,15},{15,13},{16,18},{18,... | collective-permute-start | bytes 2359304 | tf_op jit(solution)/shard_map/ppermute | solution.py:422
  84.8 12.0 %copy-start.7 = (f32[2,128,512]{2,1,0:T(8,128)}, f32[2,128,512]{2,1,0:T(8,128)S(1)}, u32[]{:S(2)}) copy-start(f32[2,128,512]{2,1,0:T(8,128)S(1)} %collective-permute-done.11.refs_3_.refs_1_) | copy-start | bytes 1572868
  96.9 11.6 %collective-permute-start.14 = (f32[2,128,384]{2,1,0:T(8,128)}, f32[2,128,384]{2,1,0:T(8,128)S(1)}, u32[]{:S(2)}, u32[]{:S(2)}) collective-permute-start(f32[2,128,384]{2,1,0:T(8,128)} %get-tuple-element.167), channel_id=1, source_target_pairs={{0,2},{1,3},{2,0},{3,1},{4,6},{5,7},{6,4},{7,5},{8,10},{9,11},{10,... | collective-permute-start | bytes 1179656 | tf_op jit(solution)/shard_map/ppermute | solution.py:422
  108.5 20.9 %copy-start.2 = (f32[16,768]{1,0:T(8,128)S(1)}, f32[16,768]{1,0:T(8,128)}, u32[]{:S(2)}) copy-start(f32[16,768]{1,0:T(8,128)} %maximum_maximum_fusion.stats) | copy-start | bytes 147460
  108.5 20.9 %copy-start.1 = (f32[192,768]{1,0:T(8,128)S(1)}, f32[192,768]{1,0:T(8,128)}, u32[]{:S(2)}) copy-start(f32[192,768]{1,0:T(8,128)} %copy-done) | copy-start | bytes 1769476
  108.5 11.7 %copy-start.10 = (f32[2,128,384]{2,1,0:T(8,128)}, f32[2,128,384]{2,1,0:T(8,128)S(1)}, u32[]{:S(2)}) copy-start(f32[2,128,384]{2,1,0:T(8,128)S(1)} %collective-permute-done.14.refs_1_.refs_5_) | copy-start | bytes 1179652
  108.5 22.0 %collective-permute-start.15 = (f32[2,128,1024]{2,1,0:T(8,128)}, f32[2,128,1024]{2,1,0:T(8,128)}, u32[]{:S(2)}, u32[]{:S(2)}) collective-permute-start(f32[2,128,1024]{2,1,0:T(8,128)} %get-tuple-element.168), channel_id=1, source_target_pairs={{0,2},{2,0},{5,7},{7,5},{8,10},{10,8},{13,15},{15,13},{16,18},{18,... | collective-permute-start | bytes 3145736 | tf_op jit(solution)/shard_map/ppermute | solution.py:422
  111.7 22.9 %collective-permute-start.20 = (f32[864,128]{1,0:T(8,128)S(1)}, f32[864,128]{1,0:T(8,128)S(1)}, u32[]{:S(2)}, u32[]{:S(2)}) collective-permute-start(f32[864,128]{1,0:T(8,128)S(1)} %pad_maximum_fusion.refs_8_.refs_10_), channel_id=1, source_target_pairs={{1,5},{3,7},{4,0},{6,2},{9,13},{11,15},{12,8},{14,10},{17,21},{19,... | collective-permute-start | bytes 1327112 | tf_op jit(solution)/shard_map/ppermute | solution.py:422
  113.0 26.2 %collective-permute-start.21 = (f32[864,128]{1,0:T(8,128)S(1)}, f32[864,128]{1,0:T(8,128)S(1)}, u32[]{:S(2)}, u32[]{:S(2)}) collective-permute-start(f32[864,128]{1,0:T(8,128)S(1)} %pad_maximum_fusion.refs_8_.refs_10_), channel_id=1, source_target_pairs={{1,9},{3,11},{5,13},{7,15},{8,0},{9,17},{10,2},{11,19},{12,4},{13,... | collective-permute-start | bytes 1327112 | tf_op jit(solution)/shard_map/ppermute | solution.py:422
  114.9 0.9 copy-start.6
  118.8 0.7 copy-start.3
  119.6 0.7 copy-start.4
  120.3 20.8 %collective-permute-start.22 = (f32[256,384]{1,0:T(8,128)}, f32[256,384]{1,0:T(8,128)S(1)}, u32[]{:S(2)}, u32[]{:S(2)}) collective-permute-start(f32[256,384]{1,0:T(8,128)} %get-tuple-element.187), channel_id=1, source_target_pairs={{0,9},{2,11},{4,13},{6,15},{8,17},{9,0},{10,19},{11,2},{12,21},{13... | collective-permute-start | bytes 1179656 | tf_op jit(solution)/shard_map/ppermute | solution.py:422
  127.3 7.3 %copy-start.5 = (f32[512,128]{1,0:T(8,128)S(1)}, f32[512,128]{1,0:T(8,128)}, u32[]{:S(2)}) copy-start(f32[512,128]{1,0:T(8,128)} %copy-done.4) | copy-start | bytes 786436
  127.3 22.6 %collective-permute-start.16 = (f32[256,384]{1,0:T(8,128)}, f32[256,384]{1,0:T(8,128)S(1)}, u32[]{:S(2)}, u32[]{:S(2)}) collective-permute-start(f32[256,384]{1,0:T(8,128)} %copy-done.3), channel_id=1, source_target_pairs={{0,5},{2,7},{5,0},{7,2},{8,13},{10,15},{13,8},{15,10},{16,21},{18,... | collective-permute-start | bytes 1179656 | tf_op jit(solution)/shard_map/ppermute | solution.py:422
  132.7 17.2 %collective-permute-start.19 = (f32[640,128]{1,0:T(8,128)S(1)}, f32[640,128]{1,0:T(8,128)S(1)}, u32[]{:S(2)}, u32[]{:S(2)}) collective-permute-start(f32[640,128]{1,0:T(8,128)S(1)} %get-tuple-element.183), channel_id=1, source_target_pairs={{0,13},{2,15},{8,21},{10,23},{13,0},{15,2},{16,29},{18,31},{21,8},... | collective-permute-start | bytes 983048 | tf_op jit(solution)/shard_map/ppermute | solution.py:422
  134.6 15.3 %collective-permute-start.17 = (f32[512,128]{1,0:T(8,128)S(1)}, f32[512,128]{1,0:T(8,128)S(1)}, u32[]{:S(2)}, u32[]{:S(2)}) collective-permute-start(f32[512,128]{1,0:T(8,128)S(1)} %copy-done.5), channel_id=1, source_target_pairs={{0,13},{2,15},{8,21},{10,23},{13,0},{15,2},{16,29},{18,31},{21,8},... | collective-permute-start | bytes 786440 | tf_op jit(solution)/shard_map/ppermute | solution.py:422
  139.2 7.3 %collective-permute-start.23 = (f32[128,384]{1,0:T(8,128)S(1)}, f32[128,384]{1,0:T(8,128)S(1)}, u32[]{:S(2)}, u32[]{:S(2)}) collective-permute-start(f32[128,384]{1,0:T(8,128)S(1)} %get-tuple-element.188), channel_id=1, source_target_pairs={{0,9},{2,11},{4,13},{6,15},{8,17},{9,0},{10,19},{11,2},{12,21},{13... | collective-permute-start | bytes 589832 | tf_op jit(solution)/shard_map/ppermute | solution.py:422
  141.1 8.8 %collective-permute-start.18 = (f32[128,384]{1,0:T(8,128)S(1)}, f32[128,384]{1,0:T(8,128)S(1)}, u32[]{:S(2)}, u32[]{:S(2)}) collective-permute-start(f32[128,384]{1,0:T(8,128)S(1)} %get-tuple-element.182), channel_id=1, source_target_pairs={{0,5},{2,7},{5,0},{7,2},{8,13},{10,15},{13,8},{15,10},{16,21},{18,... | collective-permute-start | bytes 589832 | tf_op jit(solution)/shard_map/ppermute | solution.py:422
  154.6 8.5 %collective-permute-start.24 = (f32[384,128]{1,0:T(8,128)S(1)}, f32[384,128]{1,0:T(8,128)S(1)}, u32[]{:S(2)}, u32[]{:S(2)}) collective-permute-start(f32[384,128]{1,0:T(8,128)S(1)} %get-tuple-element.192), channel_id=1, source_target_pairs={{0,4},{2,6},{5,3},{7,1},{8,12},{10,14},{13,11},{15,9},{16,20},{18,... | collective-permute-start | bytes 589832 | tf_op jit(solution)/shard_map/ppermute | solution.py:422
  157.4 6.3 %collective-permute-start.25 = (f32[384,128]{1,0:T(8,128)S(1)}, f32[384,128]{1,0:T(8,128)S(1)}, u32[]{:S(2)}, u32[]{:S(2)}) collective-permute-start(f32[384,128]{1,0:T(8,128)S(1)} %get-tuple-element.193), channel_id=1, source_target_pairs={{5,0},{7,2},{13,8},{15,10},{21,16},{23,18},{29,24},{31,26}} | collective-permute-start | bytes 589832 | tf_op jit(solution)/shard_map/ppermute | solution.py:422
  161.1 7.3 %collective-permute-start.26 = (f32[384,128]{1,0:T(8,128)S(1)}, f32[384,128]{1,0:T(8,128)S(1)}, u32[]{:S(2)}, u32[]{:S(2)}) collective-permute-start(f32[384,128]{1,0:T(8,128)S(1)} %get-tuple-element.194), channel_id=1, source_target_pairs={{0,8},{2,10},{4,12},{6,14},{8,16},{9,3},{10,18},{11,1},{12,20},{13... | collective-permute-start | bytes 589832 | tf_op jit(solution)/shard_map/ppermute | solution.py:422
  168.5 1.4 collective-permute-start.27

commit v3 on v2

--- a/solution.py
+++ b/solution.py
@@ -136,13 +136,12 @@
 X, Z = 0, 1
 
 
-def own_kernel(parts, role, dose_hbm, *refs):
+def own_kernel(parts, dose_hbm, *refs):
     refs = list(refs)
     take = lambda n: [refs.pop(0) for _ in range(n)]
-    high_hbm, low_hbm, keep_hbm, send_hbm, moments = take(5)
+    high_hbm, low_hbm, tile_hbm, moments = take(4)
     raw_hbm = take(len(parts) - 1)
     dose, high, low, tile, col, sems = refs
-    c = role[1]
     blocks, size = high.shape[0], high.shape[1]
     half = blocks * LANES
     copies = Copies(sems)
@@ -176,11 +175,7 @@
     for i in range(blocks):
         for j in range(i):
             tile[cut(j), cut(i)] = tile[cut(i), cut(j)].T
-    quarter = half // 2
-    for chip in range(2):
-        for core, there in ((c, keep_hbm), (1 - c, send_hbm)):
-            first = pl.multiple_of((2 * chip + core) * quarter, quarter)
-            copies.start("out", tile.at[pl.ds(first, quarter)], there.at[chip])
+    copies.start("out", tile, tile_hbm)
     copies.wait("out")
 
 
@@ -295,9 +290,9 @@
 TO_F, TO_S = ((0,), (0,)), ((1,), (0,))
 
 
-def diagonal_kernel(width, people_count, tile, tile_pair, stats_rows, stats, annot, out):
+def diagonal_kernel(width, people_count, tile, stats_rows, stats, annot, out):
     corr = correlation(
-        tile[...] + tile_pair[...], stats_rows[0:8], stats_rows[8:9], stats[0:8], stats[8:9], width, people_count
+        tile[...], stats_rows[0:8], stats_rows[8:9], stats[0:8], stats[8:9], width, people_count
     )
     out[...] = annotated(adjust(corr, people_count), annot[...], TO_S)
 
@@ -423,6 +418,7 @@
 
     raw_0 = dosages.reshape(2, half, width)[:, :parts[0].w]
     raw = [raw_0]
+
     stage = lax.optimization_barrier
 
     def send_block(k):
@@ -473,20 +469,16 @@
         return [send(v, "pair_" + n) for v, n in zip(outs, names)]
 
     got = send_block(0)
-    shared = ((2, rows // 4, rows), F32, HBM)
     outs = call(
-        functools.partial(own_kernel, parts), [(SMEM, role), (HBM, dosages)],
-        [(stack, BF16, HBM)] * 2 + [shared] * 2 + [((2 * rows // LANES, LANES), F32, None)]
+        functools.partial(own_kernel, parts), [(HBM, dosages)],
+        [(stack, BF16, HBM)] * 2 + [((rows, rows), F32, HBM)] + [((2 * rows // LANES, LANES), F32, None)]
         + [((2, part.w, width), F32, HBM) for part in parts[1:]],
         [VMEM((rows, width), F32)] + [VMEM(stack, BF16)] * 2 + [VMEM((rows, rows), F32), col, dma((24,))],
         room=24, flops=4 * rows * rows * width, moved=4 * rows * width,
     )
-    own, keep_0, send_0, moments, raw = outs[:2], outs[2], outs[3], outs[4], [raw_0, *outs[5:]]
-    own, keep_0, send_0, moments, raw = stage((own, keep_0, send_0, moments, raw))
-
-    both = keep_0 + send(send_0, "core")
-    pick = lambda value, i: lax.dynamic_index_in_dim(value, i, 0, keepdims=False)
-    tile0_own, tile0_send = pick(both, y), pick(both, 1 - y)
+    own, tile0, moments, raw = outs[:2], outs[2], outs[3], [raw_0, *outs[4:]]
+    own, tile0, moments, raw = stage((own, tile0, moments, raw))
+    tile0 = lax.psum_scatter(tile0, "people", scatter_dimension=0, tiled=True)
 
     moments = moments.reshape(1, 2, rows)
     moments = jnp.concatenate([moments, send(moments, "core")])
@@ -500,31 +492,26 @@
     stats = jnp.concatenate([offsets, fill(8 - offsets.shape[0]), scale[None], fill(7)], axis=0)
     by_block = stats.reshape(16, -1, LANES).transpose(1, 0, 2).reshape(-1, LANES)
     side = jnp.concatenate([annot, by_block], axis=0)
-    got, own, raw, tile0_own, tile0_send, annot, stats, side = stage(
-        (got, own, raw, tile0_own, tile0_send, annot, stats, side)
-    )
+    got, own, annot, stats, side = stage((got, own, annot, stats, side))
 
     pairs, old = [], []
     n_parts = len(parts)
     last = n_parts - 1
-    tile0_came = send(tile0_send, "y")
     for k in range(n_parts):
         coming = send_block(k + 1) if k < last else ()
         if k == last:
             came = [send(side, name) for name in "xz"]
         keep_a, sent, own, old = run_chunk(k, Z, got[1], own, old)
-        if k == 0:
-            sent, tile0_came = stage((sent, tile0_came))
         came_a = send(sent, "y")
         keep_db, sent, own, old = run_chunk(k, X, got[0], own, old)
         sent, came_a = stage((sent, came_a))
+        if k == last:
+            sent, came, pairs = stage((sent, came, pairs))
         pairs.append((keep_a, came_a, keep_db, send(sent, "y_meet")))
         if k < last:
             *held, came_db = pairs.pop()
             got, raw, old, own, pairs, held = stage((coming, raw, old, own, pairs, held))
             pairs.append((*held, came_db))
-        else:
-            came, old = stage((came, old))
     sides = [side, *came]
     early, late = range(EARLY), range(EARLY, n_parts)
     phases = [[parts[k] for k in chunk] for chunk in (early, late)]
@@ -532,7 +519,7 @@
     stats_rows = lax.dynamic_slice_in_dim(stats, p * (rows // 4), rows // 4, 1)
     (res_0,) = call(
         functools.partial(diagonal_kernel, float(width), float(total)),
-        [(None, t) for t in (tile0_own, tile0_came, stats_rows, stats, annot)], [((rows // 4, cats), F32, None)],
+        [(None, t) for t in (tile0, stats_rows, stats, annot)], [((rows // 4, cats), F32, None)],
         flops=4 * rows * rows * cats, moved=rows * rows,
     )
     sent_late = run_sum("adb", late, stage((role, res_0))[0])

time: 171 us -> 178 us (1.041)
  between operations: 0.67 us -> 14 us
  waiting for transfers between devices: 28 us -> 14.7 us
  starting transfers between devices: 58.9 us -> 66.1 us
  other arithmetic: 3.46 us -> 1.09 us
  Pallas kernels: 73.5 us -> 75.5 us
    ppermute x28 -> x26, waiting for transfers between devices: 28 us -> 14.7 us  [send(): return lax.ppermute(value, AXES, routes[name])]
    ppermute x28 -> x26, starting transfers between devices: 58.9 us -> 66.1 us  [send(): return lax.ppermute(value, AXES, routes[name])]
    pallas_call x12, Pallas kernels: 73.5 us -> 75.5 us  [call(): pl.pallas_call(kernel, out_shape=[m(s, d) if m else jax.ShapeDtypeStruct(...]
  transfers between devices with their start and end apart: 28 -> 27, of which waited for: 13 -> 6; matrix products, arithmetic and copies ran while one was open for 2% -> 0% of each run, Pallas kernels for 40% -> 40%
where the time goes in v3:
time: 178 us; the launch traced here: 177 us
  Pallas kernels  75.5 us (42%)
  starting transfers between devices  66.1 us (37%)
  waiting for transfers between devices  14.7 us (8%)
  between operations  14 us (8%)
  local copies, waits for them, and re-layouts  5.27 us (3%)
    pallas_call x12, Pallas kernels, call(): pl.pallas_call(kernel, out_shape=[m(s, d) if m else jax.ShapeDtypeStruct(...  75.5 us
    ppermute x26, starting transfers between devices, send(): return lax.ppermute(value, AXES, routes[name])  66.1 us
    ppermute x26, waiting for transfers between devices, send(): return lax.ppermute(value, AXES, routes[name])  14.7 us
  transfers between devices with their start and end apart: 27, of which 6 were waited for; matrix products, arithmetic and copies ran while one was open for 0% of the time, Pallas kernels for 40%

profile of v3, /device:TPU:23, one launch (start us, length us, event | category | flops | bytes accessed | tf_op | source)
XLA Modules:
  0.0 176.7 jit_solution(9919708562622869444)
XLA Ops:
  6.5 3.2 %slice.13 = f32[2,128,2048]{2,1,0:T(8,128)} slice(f32[2,384,2048]{2,1,0:T(8,128)} %bitcast.22), slice={[0:2], [0:128], [0:2048]} | slice | bytes 4194304 | tf_op jit(solution)/shard_map/slice | solution.py:419
  9.7 1.4 collective-permute-start.2
  11.1 3.2 %collective-permute-start.3 = (f32[2,128,2048]{2,1,0:T(8,128)}, f32[2,128,2048]{2,1,0:T(8,128)}, u32[]{:S(2)}, u32[]{:S(2)}) collective-permute-start(f32[2,128,2048]{2,1,0:T(8,128)} %slice.13), channel_id=1, source_target_pairs={{1,9},{3,11},{5,13},{7,15},{8,0},{9,17},{10,2},{11,19},{12,4},{13,... | collective-permute-start | bytes 6291464 | tf_op jit(solution)/shard_map/ppermute | solution.py:417
  14.3 13.7 %shard_map.28 = (bf16[3,256,2048]{2,1,0:T(8,128)(2,1)}, bf16[3,256,2048]{2,1,0:T(8,128)(2,1)}, f32[768,768]{1,0:T(8,128)}, f32[12,128]{1,0:T(8,128)S(1)}, f32[2,...) custom-call(f32[768,2048]{1,0:T(8,128)} %dose_hbm.1), custom_call_target="tpu_custom_call" | custom-call | flops 4831838208 | bytes 6291456 | tf_op jit(solution)/shard_map/pallas_call | solution.py:43
  28.1 2.4 %collective-permute-start.4 = (f32[1,2,768]{2,0,1:T(1,128)S(1)}, f32[1,2,768]{2,0,1:T(1,128)S(1)}, u32[]{:S(2)}, u32[]{:S(2)}) collective-permute-start(f32[1,2,768]{2,0,1:T(1,128)S(1)} %reshape.96), channel_id=1, source_target_pairs={{0,1},{1,0},{2,3},{3,2},{4,5},{5,4},{6,7},{7,6},{8,9},{9,8},{10,11... | collective-permute-start | bytes 18440 | tf_op jit(solution)/shard_map/ppermute | solution.py:417
  30.5 1.3 collective-permute-start
  31.8 4.5 %collective-permute-start.1 = (f32[2,128,2048]{2,1,0:T(8,128)}, f32[2,128,2048]{2,1,0:T(8,128)}, u32[]{:S(2)}, u32[]{:S(2)}) collective-permute-start(f32[2,128,2048]{2,1,0:T(8,128)} %get-tuple-element.107), channel_id=1, source_target_pairs={{1,9},{3,11},{5,13},{7,15},{8,0},{9,17},{10,2},{11,19},{12,4},{13,... | collective-permute-start | bytes 6291464 | tf_op jit(solution)/shard_map/ppermute | solution.py:417
  36.3 0.0 reduce-scatter.2.cloned.1.call-update
  36.4 0.0 collective-permute-done.4
  36.4 0.3 collective-permute-start.5
  36.7 0.1 pad_add_fusion.role
  36.7 0.1 pad.7.clone
  36.8 0.1 pad.9.clone
  36.9 2.5 %collective-permute-done.5 = f32[2,2,768]{2,0,1:T(2,128)S(1)} collective-permute-done((f32[2,2,768]{2,0,1:T(2,128)S(1)}, f32[2,2,768]{2,0,1:T(2,128)S(1)}, u32[]{:S(2)}, u32[]{:S(2)}) %collective-permute-start.5) | collective-permute-done | bytes 12320 | tf_op jit(solution)/shard_map/ppermute | solution.py:417
  39.6 0.1 maximum_maximum_fusion.1
  39.6 0.1 maximum_maximum_fusion.stats
  39.8 0.0 collective-permute-done.2.raw
  39.8 0.0 collective-permute-done.3.raw
  39.8 7.3 %shard_map.29 = (f32[2,128,384]{2,1,0:T(8,128)}, f32[2,128,384]{2,1,0:T(8,128)}, bf16[2,3,256,2048]{3,2,1,0:T(8,128)(2,1)S(1)}, bf16[2,3,256,2048]{3,2,1,0:T(8,1...) custom-call(s32[2]{0:T(128)S(1)} %pad_add_fusion.role, ...), custom_call_target="tpu_custom_call" | custom-call | flops 2415919104 | bytes 3145728 | tf_op jit(solution)/shard_map/pallas_call | solution.py:43
  47.1 0.3 collective-permute-start.6
  47.4 8.0 %shard_map.30 = (f32[2,128,512]{2,1,0:T(8,128)}, f32[2,128,512]{2,1,0:T(8,128)}, bf16[2,3,256,2048]{3,2,1,0:T(8,128)(2,1)S(1)}, bf16[2,3,256,2048]{3,2,1,0:T(8,128)(2,1)S(1)}) custom-call(s32[2]{0:T(128)S(1)} %pad_add_fusion.role, f32[2,128,2048]{2,1,0:T(8,128)} %collective-permute-done.2.raw, ...), custom_call_target="tpu_custom_call", output_to_operand_aliasing={{2}: (4, {}), {3}: (5, {})} | custom-call | flops 3221225472 | bytes 3145728 | tf_op jit(solution)/shard_map/pallas_call | solution.py:43
  55.3 0.0 collective-permute-done.6.refs_1_
  55.3 4.4 %collective-permute-done.raw = f32[2,128,2048]{2,1,0:T(8,128)S(1)} collective-permute-done((f32[2,128,2048]{2,1,0:T(8,128)}, f32[2,128,2048]{2,1,0:T(8,128)S(1)}, u32[]{:S(2)}, u32[]{:S(2)}) %collective-permute-start) | collective-permute-done | bytes 2097184 | tf_op jit(solution)/shard_map/ppermute | solution.py:417
  59.7 1.3 collective-permute-done.1.raw
  61.0 1.3 collective-permute-start.7
  62.3 3.2 %collective-permute-start.8 = (f32[2,128,2048]{2,1,0:T(8,128)S(1)}, f32[2,128,2048]{2,1,0:T(8,128)S(1)}, u32[]{:S(2)}, u32[]{:S(2)}) collective-permute-start(f32[2,128,2048]{2,1,0:T(8,128)S(1)} %copy-done.8), channel_id=1, source_target_pairs={{1,9},{3,11},{5,13},{7,15},{8,0},{9,17},{10,2},{11,19},{12,4},{13,... | collective-permute-start | bytes 6291464 | tf_op jit(solution)/shard_map/ppermute | solution.py:417
  65.5 1.3 collective-permute-start.12
  66.8 2.1 %collective-permute-start.9 = (f32[2,128,512]{2,1,0:T(8,128)}, f32[2,128,512]{2,1,0:T(8,128)S(1)}, u32[]{:S(2)}, u32[]{:S(2)}) collective-permute-start(f32[2,128,512]{2,1,0:T(8,128)} %get-tuple-element.141), channel_id=1, source_target_pairs={{0,2},{2,0},{5,7},{7,5},{8,10},{10,8},{13,15},{15,13},{16,18},{18,... | collective-permute-start | bytes 1572872 | tf_op jit(solution)/shard_map/ppermute | solution.py:417
  68.9 6.6 %shard_map.31 = (f32[2,128,384]{2,1,0:T(8,128)}, f32[2,128,384]{2,1,0:T(8,128)}, bf16[2,3,256,2048]{3,2,1,0:T(8,128)(2,1)S(1)}, bf16[2,3,256,2048]{3,2,1,0:T(8,128)(2,1)S(1)}) custom-call(s32[2]{0:T(128)S(1)} %pad_add_fusion.role, f32[2,128,2048]{2,1,0:T(8,128)} %collective-permute-done.1.raw, ...), custom_call_target="tpu_custom_call", output_to_operand_aliasing={{2}: (4, {}), {3}: (5, {})} | custom-call | flops 2415919104 | bytes 3145728 | tf_op jit(solution)/shard_map/pallas_call | solution.py:43
  75.6 1.3 collective-permute-start.10
  76.9 8.9 %shard_map.32 = (f32[2,128,768]{2,1,0:T(8,128)}, f32[2,128,768]{2,1,0:T(8,128)}, bf16[2,3,256,2048]{3,2,1,0:T(8,128)(2,1)S(1)}, bf16[2,3,256,2048]{3,2,1,0:T(8,128)(2,1)S(1)}) custom-call(s32[2]{0:T(128)S(1)} %pad_add_fusion.role, f32[2,128,2048]{2,1,0:T(8,128)S(1)} %collective-permute-done.raw, ...), custom_call_target="tpu_custom_call", output_to_operand_aliasing={{2}: (4, {}), {3}: (5, {})} | custom-call | flops 4831838208 | bytes 3145728 | tf_op jit(solution)/shard_map/pallas_call | solution.py:43
  85.8 0.0 collective-permute-done.10.refs_5_.refs_3_
  85.8 1.9 %collective-permute-start.13 = (f32[864,128]{1,0:T(8,128)S(1)}, f32[864,128]{1,0:T(8,128)S(1)}, u32[]{:S(2)}, u32[]{:S(2)}) collective-permute-start(f32[864,128]{1,0:T(8,128)S(1)} %pad_maximum_fusion.refs_8_.refs_10_), channel_id=1, source_target_pairs={{1,9},{3,11},{5,13},{7,15},{8,0},{9,17},{10,2},{11,19},{12,4},{13,... | collective-permute-start | bytes 1327112 | tf_op jit(solution)/shard_map/ppermute | solution.py:417
  87.7 0.0 collective-permute-done.9.refs_3_.refs_1_
  87.7 3.2 %collective-permute-start.14 = (f32[2,128,768]{2,1,0:T(8,128)}, f32[2,128,768]{2,1,0:T(8,128)S(1)}, u32[]{:S(2)}, u32[]{:S(2)}) collective-permute-start(f32[2,128,768]{2,1,0:T(8,128)} %get-tuple-element.166), channel_id=1, source_target_pairs={{0,2},{2,0},{5,7},{7,5},{8,10},{10,8},{13,15},{15,13},{16,18},{18,... | collective-permute-start | bytes 2359304 | tf_op jit(solution)/shard_map/ppermute | solution.py:417
  90.9 0.0 collective-permute-done.7.raw
  90.9 0.0 collective-permute-done.8.raw
  90.9 5.6 %shard_map.33 = (f32[2,128,384]{2,1,0:T(8,128)}, f32[2,128,384]{2,1,0:T(8,128)}, bf16[2,3,256,2048]{3,2,1,0:T(8,128)(2,1)S(1)}, bf16[2,3,256,2048]{3,2,1,0:T(8,128)(2,1)S(1)}) custom-call(s32[2]{0:T(128)S(1)} %pad_add_fusion.role, f32[2,128,2048]{2,1,0:T(8,128)S(1)} %collective-permute-done.8.raw, ...), custom_call_target="tpu_custom_call", output_to_operand_aliasing={{2}: (4, {}), {3}: (5, {})} | custom-call | flops 2415919104 | bytes 3145728 | tf_op jit(solution)/shard_map/pallas_call | solution.py:43
  96.5 0.4 collective-permute-start.11
  97.0 11.1 %shard_map.34 = (f32[2,128,1024]{2,1,0:T(8,128)}, f32[2,128,1024]{2,1,0:T(8,128)}, bf16[2,3,256,2048]{3,2,1,0:T(8,128)(2,1)S(1)}, bf16[2,3,256,2048]{3,2,1,0:T(8,128)(2,1)S(1)}) custom-call(s32[2]{0:T(128)S(1)} %pad_add_fusion.role, f32[2,128,2048]{2,1,0:T(8,128)S(1)} %collective-permute-done.7.raw, ...), custom_call_target="tpu_custom_call", output_to_operand_aliasing={{2}: (4, {}), {3}: (5, {})} | custom-call | flops 6442450944 | bytes 3145728 | tf_op jit(solution)/shard_map/pallas_call | solution.py:43
  108.2 0.7 copy-done.6
  108.9 3.0 %collective-permute-start.15 = (f32[2,128,1024]{2,1,0:T(8,128)}, f32[2,128,1024]{2,1,0:T(8,128)}, u32[]{:S(2)}, u32[]{:S(2)}) collective-permute-start(f32[2,128,1024]{2,1,0:T(8,128)} %get-tuple-element.172), channel_id=1, source_target_pairs={{0,2},{2,0},{5,7},{7,5},{8,10},{10,8},{13,15},{15,13},{16,18},{18,... | collective-permute-start | bytes 3145736 | tf_op jit(solution)/shard_map/ppermute | solution.py:417
  111.9 3.0 %shard_map.35 = (f32[256,384]{1,0:T(8,128)}, f32[256,384]{1,0:T(8,128)S(1)}, f32[512,128]{1,0:T(8,128)S(1)}) custom-call(s32[2]{0:T(128)S(1)} %pad_add_fusion.role, f32[2,128,384]{2,1,0:T(8,128)} %get-tuple-element.173.refs_0_, f32[2,128,384]{2,1,0:T(8,128)} %copy-done.4, f32[2,128,512]{2,1,0:T(8,128)} %get-tuple-element.167.refs_2_.refs_0_, ...), custom_call_target="tpu_custom_call" | custom-call | flops 98304 | bytes 1179648 | tf_op jit(solution)/shard_map/pallas_call | solution.py:43
  114.9 4.1 %collective-permute-start.20 = (f32[256,384]{1,0:T(8,128)}, f32[256,384]{1,0:T(8,128)S(1)}, u32[]{:S(2)}, u32[]{:S(2)}) collective-permute-start(f32[256,384]{1,0:T(8,128)} %get-tuple-element.189), channel_id=1, source_target_pairs={{0,9},{2,11},{4,13},{6,15},{8,17},{9,0},{10,19},{11,2},{12,21},{13... | collective-permute-start | bytes 1179656 | tf_op jit(solution)/shard_map/ppermute | solution.py:417
  119.0 5.3 %collective-permute-start.16 = (f32[256,384]{1,0:T(8,128)S(1)}, f32[256,384]{1,0:T(8,128)S(1)}, u32[]{:S(2)}, u32[]{:S(2)}) collective-permute-start(f32[256,384]{1,0:T(8,128)S(1)} %get-tuple-element.177), channel_id=1, source_target_pairs={{0,5},{2,7},{5,0},{7,2},{8,13},{10,15},{13,8},{15,10},{16,21},{18,... | collective-permute-start | bytes 1179656 | tf_op jit(solution)/shard_map/ppermute | solution.py:417
  124.4 0.1 constant_dynamic-slice_fusion.stats_rows
  124.4 1.1 copy-done
  125.5 1.1 shard_map.36
  126.7 2.1 %shard_map.37 = (f32[128,384]{1,0:T(8,128)S(1)}, f32[128,384]{1,0:T(8,128)S(1)}, f32[640,128]{1,0:T(8,128)S(1)}) custom-call(s32[2]{0:T(128)S(1)} %pad_add_fusion.role, f32[2,128,384]{2,1,0:T(8,128)} %get-tuple-element.183.refs_0_.refs_4_, f32[2,128,384]{2,1,0:T(8,128)} %copy-done.6, f32[2,128,1024]{2,1,0:T(8,128)} %get-tuple-element.171.refs_2_.refs_4_, ...), custom_call_target="tpu_custom_call" | custom-call | flops 49152 | bytes 589824 | tf_op jit(solution)/shard_map/pallas_call | solution.py:43
  128.7 6.3 %collective-permute-start.19 = (f32[640,128]{1,0:T(8,128)S(1)}, f32[640,128]{1,0:T(8,128)S(1)}, u32[]{:S(2)}, u32[]{:S(2)}) collective-permute-start(f32[640,128]{1,0:T(8,128)S(1)} %get-tuple-element.186), channel_id=1, source_target_pairs={{0,13},{2,15},{8,21},{10,23},{13,0},{15,2},{16,29},{18,31},{21,8},... | collective-permute-start | bytes 983048 | tf_op jit(solution)/shard_map/ppermute | solution.py:417
  135.0 1.9 %collective-permute-start.17 = (f32[512,128]{1,0:T(8,128)}, f32[512,128]{1,0:T(8,128)S(1)}, u32[]{:S(2)}, u32[]{:S(2)}) collective-permute-start(f32[512,128]{1,0:T(8,128)} %copy-done.1), channel_id=1, source_target_pairs={{0,13},{2,15},{8,21},{10,23},{13,0},{15,2},{16,29},{18,31},{21,8},... | collective-permute-start | bytes 786440 | tf_op jit(solution)/shard_map/ppermute | solution.py:417
  136.9 1.9 %collective-permute-start.21 = (f32[128,384]{1,0:T(8,128)S(1)}, f32[128,384]{1,0:T(8,128)S(1)}, u32[]{:S(2)}, u32[]{:S(2)}) collective-permute-start(f32[128,384]{1,0:T(8,128)S(1)} %get-tuple-element.190), channel_id=1, source_target_pairs={{0,9},{2,11},{4,13},{6,15},{8,17},{9,0},{10,19},{11,2},{12,21},{13... | collective-permute-start | bytes 589832 | tf_op jit(solution)/shard_map/ppermute | solution.py:417
  138.9 5.1 %collective-permute-start.18 = (f32[128,384]{1,0:T(8,128)S(1)}, f32[128,384]{1,0:T(8,128)S(1)}, u32[]{:S(2)}, u32[]{:S(2)}) collective-permute-start(f32[128,384]{1,0:T(8,128)S(1)} %get-tuple-element.185), channel_id=1, source_target_pairs={{0,5},{2,7},{5,0},{7,2},{8,13},{10,15},{13,8},{15,10},{16,21},{18,... | collective-permute-start | bytes 589832 | tf_op jit(solution)/shard_map/ppermute | solution.py:417
  144.0 3.4 %shard_map.38 = (f32[384,128]{1,0:T(8,128)S(1)}, f32[384,128]{1,0:T(8,128)S(1)}) custom-call(s32[2]{0:T(128)S(1)} %pad_add_fusion.role, f32[2,128,384]{2,1,0:T(8,128)} %get-tuple-element.173.refs_0_, f32[2,128,384]{2,1,0:T(8,128)} %copy-done.4, f32[2,128,384]{2,1,0:T(8,128)} %get-tuple-element.175.refs_4_.refs_2_, f32[2,128,384]{2,1,0:T(8,128)} %copy-done.5, ...), custom_call_target="tpu_custom_call" | custom-call | flops 226492416 | bytes 2359296 | tf_op jit(solution)/shard_map/pallas_call | solution.py:43
  147.4 4.7 %shard_map.39 = (f32[384,128]{1,0:T(8,128)S(1)}, f32[384,128]{1,0:T(8,128)S(1)}, f32[384,128]{1,0:T(8,128)S(1)}, f32[384,128]{1,0:T(8,128)S(1)}) custom-call(s32[2]{0:T(128)S(1)} %pad_add_fusion.role, f32[2,128,512]{2,1,0:T(8,128)} %get-tuple-element.167.refs_2_.refs_0_, f32[2,128,512]{2,1,0:T(8,128)} %copy-done.3, ...), custom_call_target="tpu_custom_call" | custom-call | flops 226492416 | bytes 2359296 | tf_op jit(solution)/shard_map/pallas_call | solution.py:43
  152.1 4.8 %collective-permute-start.22 = (f32[384,128]{1,0:T(8,128)S(1)}, f32[384,128]{1,0:T(8,128)S(1)}, u32[]{:S(2)}, u32[]{:S(2)}) collective-permute-start(f32[384,128]{1,0:T(8,128)S(1)} %get-tuple-element.194), channel_id=1, source_target_pairs={{0,4},{2,6},{5,3},{7,1},{8,12},{10,14},{13,11},{15,9},{16,20},{18,... | collective-permute-start | bytes 589832 | tf_op jit(solution)/shard_map/ppermute | solution.py:417
  157.0 3.4 %collective-permute-start.23 = (f32[384,128]{1,0:T(8,128)S(1)}, f32[384,128]{1,0:T(8,128)S(1)}, u32[]{:S(2)}, u32[]{:S(2)}) collective-permute-start(f32[384,128]{1,0:T(8,128)S(1)} %get-tuple-element.195), channel_id=1, source_target_pairs={{5,0},{7,2},{13,8},{15,10},{21,16},{23,18},{29,24},{31,26}} | collective-permute-start | bytes 589832 | tf_op jit(solution)/shard_map/ppermute | solution.py:417
  160.4 2.1 %collective-permute-start.24 = (f32[384,128]{1,0:T(8,128)S(1)}, f32[384,128]{1,0:T(8,128)S(1)}, u32[]{:S(2)}, u32[]{:S(2)}) collective-permute-start(f32[384,128]{1,0:T(8,128)S(1)} %get-tuple-element.196), channel_id=1, source_target_pairs={{0,8},{2,10},{4,12},{6,14},{8,16},{9,3},{10,18},{11,1},{12,20},{13... | collective-permute-start | bytes 589832 | tf_op jit(solution)/shard_map/ppermute | solution.py:417
  162.5 0.5 collective-permute-done.23
  163.0 4.7 %collective-permute-done.24 = f32[384,128]{1,0:T(8,128)S(1)} collective-permute-done((f32[384,128]{1,0:T(8,128)S(1)}, f32[384,128]{1,0:T(8,128)S(1)}, u32[]{:S(2)}, u32[]{:S(2)}) %collective-permute-start.24) | collective-permute-done | bytes 196640 | tf_op jit(solution)/shard_map/ppermute | solution.py:417
  167.7 0.1 add_add_fusion
  167.8 0.1 collective-permute-start.25
  167.9 1.3 collective-permute-done.25
  169.2 0.7 fusion
  (47 shorter events, 0.3 us)
Async XLA Ops:
  6.5 117.9 %reduce-scatter.2.cloned.1.call-start = ((), (), s32[]{:S(2)}) async-start(), calls=%async_computation.1 | async-start | bytes 2949120 | tf_op jit(solution)/shard_map/reduce_scatter | solution.py:481
  9.7 27.2 %copy-start.7 = (s32[768,128]{1,0:T(8,128)S(1)}, s32[768,128]{1,0:T(8,128)}, u32[]{:S(2)}) copy-start(s32[768,128]{1,0:T(8,128)} %param.3) | copy-start | bytes 1179652
  9.7 30.1 %collective-permute-start.2 = (f32[2,128,2048]{2,1,0:T(8,128)}, f32[2,128,2048]{2,1,0:T(8,128)}, u32[]{:S(2)}, u32[]{:S(2)}) collective-permute-start(f32[2,128,2048]{2,1,0:T(8,128)} %slice.13), channel_id=1, source_target_pairs={{1,5},{3,7},{4,0},{6,2},{9,13},{11,15},{12,8},{14,10},{17,21},{19,... | collective-permute-start | bytes 6291464 | tf_op jit(solution)/shard_map/ppermute | solution.py:417
  11.1 28.6 %collective-permute-start.3 = (f32[2,128,2048]{2,1,0:T(8,128)}, f32[2,128,2048]{2,1,0:T(8,128)}, u32[]{:S(2)}, u32[]{:S(2)}) collective-permute-start(f32[2,128,2048]{2,1,0:T(8,128)} %slice.13), channel_id=1, source_target_pairs={{1,9},{3,11},{5,13},{7,15},{8,0},{9,17},{10,2},{11,19},{12,4},{13,... | collective-permute-start | bytes 6291464 | tf_op jit(solution)/shard_map/ppermute | solution.py:417
  28.1 8.3 %collective-permute-start.4 = (f32[1,2,768]{2,0,1:T(1,128)S(1)}, f32[1,2,768]{2,0,1:T(1,128)S(1)}, u32[]{:S(2)}, u32[]{:S(2)}) collective-permute-start(f32[1,2,768]{2,0,1:T(1,128)S(1)} %reshape.96), channel_id=1, source_target_pairs={{0,1},{1,0},{2,3},{3,2},{4,5},{5,4},{6,7},{7,6},{8,9},{9,8},{10,11... | collective-permute-start | bytes 18440 | tf_op jit(solution)/shard_map/ppermute | solution.py:417
  30.5 29.2 %collective-permute-start = (f32[2,128,2048]{2,1,0:T(8,128)}, f32[2,128,2048]{2,1,0:T(8,128)S(1)}, u32[]{:S(2)}, u32[]{:S(2)}) collective-permute-start(f32[2,128,2048]{2,1,0:T(8,128)} %get-tuple-element.107), channel_id=1, source_target_pairs={{1,5},{3,7},{4,0},{6,2},{9,13},{11,15},{12,8},{14,10},{17,21},{19,... | collective-permute-start | bytes 6291464 | tf_op jit(solution)/shard_map/ppermute | solution.py:417
  31.8 29.2 %collective-permute-start.1 = (f32[2,128,2048]{2,1,0:T(8,128)}, f32[2,128,2048]{2,1,0:T(8,128)}, u32[]{:S(2)}, u32[]{:S(2)}) collective-permute-start(f32[2,128,2048]{2,1,0:T(8,128)} %get-tuple-element.107), channel_id=1, source_target_pairs={{1,9},{3,11},{5,13},{7,15},{8,0},{9,17},{10,2},{11,19},{12,4},{13,... | collective-permute-start | bytes 6291464 | tf_op jit(solution)/shard_map/ppermute | solution.py:417
  36.4 3.0 %collective-permute-start.5 = (f32[2,2,768]{2,0,1:T(2,128)S(1)}, f32[2,2,768]{2,0,1:T(2,128)S(1)}, u32[]{:S(2)}, u32[]{:S(2)}) collective-permute-start(f32[2,2,768]{2,0,1:T(2,128)S(1)} %pad_maximum_fusion.2), channel_id=1, source_target_pairs={{0,2},{1,3},{2,0},{3,1},{4,6},{5,7},{6,4},{7,5},{8,10},{9,11},{10,... | collective-permute-start | bytes 36872 | tf_op jit(solution)/shard_map/ppermute | solution.py:417
  47.1 8.2 %collective-permute-start.6 = (f32[2,128,384]{2,1,0:T(8,128)}, f32[2,128,384]{2,1,0:T(8,128)S(1)}, u32[]{:S(2)}, u32[]{:S(2)}) collective-permute-start(f32[2,128,384]{2,1,0:T(8,128)} %get-tuple-element.124), channel_id=1, source_target_pairs={{0,2},{1,3},{2,0},{3,1},{4,6},{5,7},{6,4},{7,5},{8,10},{9,11},{10,... | collective-permute-start | bytes 1179656 | tf_op jit(solution)/shard_map/ppermute | solution.py:417
  47.3 13.6 %copy-start.8 = (f32[2,128,2048]{2,1,0:T(8,128)S(1)}, f32[2,128,2048]{2,1,0:T(8,128)}, u32[]{:S(2)}) copy-start(f32[2,128,2048]{2,1,0:T(8,128)} %get-tuple-element.127) | copy-start | bytes 6291460
  55.3 20.3 %copy-start.4 = (f32[2,128,384]{2,1,0:T(8,128)}, f32[2,128,384]{2,1,0:T(8,128)S(1)}, u32[]{:S(2)}) copy-start(f32[2,128,384]{2,1,0:T(8,128)S(1)} %collective-permute-done.6.refs_1_) | copy-start | bytes 1179652
  61.0 29.9 %collective-permute-start.7 = (f32[2,128,2048]{2,1,0:T(8,128)S(1)}, f32[2,128,2048]{2,1,0:T(8,128)S(1)}, u32[]{:S(2)}, u32[]{:S(2)}) collective-permute-start(f32[2,128,2048]{2,1,0:T(8,128)S(1)} %copy-done.8), channel_id=1, source_target_pairs={{1,5},{3,7},{4,0},{6,2},{9,13},{11,15},{12,8},{14,10},{17,21},{19,... | collective-permute-start | bytes 6291464 | tf_op jit(solution)/shard_map/ppermute | solution.py:417
  62.3 28.7 %collective-permute-start.8 = (f32[2,128,2048]{2,1,0:T(8,128)S(1)}, f32[2,128,2048]{2,1,0:T(8,128)S(1)}, u32[]{:S(2)}, u32[]{:S(2)}) collective-permute-start(f32[2,128,2048]{2,1,0:T(8,128)S(1)} %copy-done.8), channel_id=1, source_target_pairs={{1,9},{3,11},{5,13},{7,15},{8,0},{9,17},{10,2},{11,19},{12,4},{13,... | collective-permute-start | bytes 6291464 | tf_op jit(solution)/shard_map/ppermute | solution.py:417
  65.5 42.6 %collective-permute-start.12 = (f32[864,128]{1,0:T(8,128)S(1)}, f32[864,128]{1,0:T(8,128)S(1)}, u32[]{:S(2)}, u32[]{:S(2)}) collective-permute-start(f32[864,128]{1,0:T(8,128)S(1)} %pad_maximum_fusion.refs_8_.refs_10_), channel_id=1, source_target_pairs={{1,5},{3,7},{4,0},{6,2},{9,13},{11,15},{12,8},{14,10},{17,21},{19,... | collective-permute-start | bytes 1327112 | tf_op jit(solution)/shard_map/ppermute | solution.py:417
  66.8 20.9 %collective-permute-start.9 = (f32[2,128,512]{2,1,0:T(8,128)}, f32[2,128,512]{2,1,0:T(8,128)S(1)}, u32[]{:S(2)}, u32[]{:S(2)}) collective-permute-start(f32[2,128,512]{2,1,0:T(8,128)} %get-tuple-element.141), channel_id=1, source_target_pairs={{0,2},{2,0},{5,7},{7,5},{8,10},{10,8},{13,15},{15,13},{16,18},{18,... | collective-permute-start | bytes 1572872 | tf_op jit(solution)/shard_map/ppermute | solution.py:417
  75.6 10.2 %collective-permute-start.10 = (f32[2,128,384]{2,1,0:T(8,128)}, f32[2,128,384]{2,1,0:T(8,128)S(1)}, u32[]{:S(2)}, u32[]{:S(2)}) collective-permute-start(f32[2,128,384]{2,1,0:T(8,128)} %get-tuple-element.144), channel_id=1, source_target_pairs={{0,2},{1,3},{2,0},{3,1},{4,6},{5,7},{6,4},{7,5},{8,10},{9,11},{10,... | collective-permute-start | bytes 1179656 | tf_op jit(solution)/shard_map/ppermute | solution.py:417
  85.8 10.8 %copy-start.5 = (f32[2,128,384]{2,1,0:T(8,128)}, f32[2,128,384]{2,1,0:T(8,128)S(1)}, u32[]{:S(2)}) copy-start(f32[2,128,384]{2,1,0:T(8,128)S(1)} %collective-permute-done.10.refs_5_.refs_3_) | copy-start | bytes 1179652
  85.8 22.4 %collective-permute-start.13 = (f32[864,128]{1,0:T(8,128)S(1)}, f32[864,128]{1,0:T(8,128)S(1)}, u32[]{:S(2)}, u32[]{:S(2)}) collective-permute-start(f32[864,128]{1,0:T(8,128)S(1)} %pad_maximum_fusion.refs_8_.refs_10_), channel_id=1, source_target_pairs={{1,9},{3,11},{5,13},{7,15},{8,0},{9,17},{10,2},{11,19},{12,4},{13,... | collective-permute-start | bytes 1327112 | tf_op jit(solution)/shard_map/ppermute | solution.py:417
  87.7 8.8 %copy-start.3 = (f32[2,128,512]{2,1,0:T(8,128)}, f32[2,128,512]{2,1,0:T(8,128)S(1)}, u32[]{:S(2)}) copy-start(f32[2,128,512]{2,1,0:T(8,128)S(1)} %collective-permute-done.9.refs_3_.refs_1_) | copy-start | bytes 1572868
  87.7 20.4 %collective-permute-start.14 = (f32[2,128,768]{2,1,0:T(8,128)}, f32[2,128,768]{2,1,0:T(8,128)S(1)}, u32[]{:S(2)}, u32[]{:S(2)}) collective-permute-start(f32[2,128,768]{2,1,0:T(8,128)} %get-tuple-element.166), channel_id=1, source_target_pairs={{0,2},{2,0},{5,7},{7,5},{8,10},{10,8},{13,15},{15,13},{16,18},{18,... | collective-permute-start | bytes 2359304 | tf_op jit(solution)/shard_map/ppermute | solution.py:417
  96.5 11.6 %collective-permute-start.11 = (f32[2,128,384]{2,1,0:T(8,128)}, f32[2,128,384]{2,1,0:T(8,128)S(1)}, u32[]{:S(2)}, u32[]{:S(2)}) collective-permute-start(f32[2,128,384]{2,1,0:T(8,128)} %get-tuple-element.156), channel_id=1, source_target_pairs={{0,2},{1,3},{2,0},{3,1},{4,6},{5,7},{6,4},{7,5},{8,10},{9,11},{10,... | collective-permute-start | bytes 1179656 | tf_op jit(solution)/shard_map/ppermute | solution.py:417
  108.1 0.8 copy-start.6
  108.9 3.0 %copy-start.2 = (f32[2,128,768]{2,1,0:T(8,128)}, f32[2,128,768]{2,1,0:T(8,128)S(1)}, u32[]{:S(2)}) copy-start(f32[2,128,768]{2,1,0:T(8,128)S(1)} %collective-permute-done.14.refs_7_.refs_3_) | copy-start | bytes 2359300
  108.9 17.8 %collective-permute-start.15 = (f32[2,128,1024]{2,1,0:T(8,128)}, f32[2,128,1024]{2,1,0:T(8,128)}, u32[]{:S(2)}, u32[]{:S(2)}) collective-permute-start(f32[2,128,1024]{2,1,0:T(8,128)} %get-tuple-element.172), channel_id=1, source_target_pairs={{0,2},{2,0},{5,7},{7,5},{8,10},{10,8},{13,15},{15,13},{16,18},{18,... | collective-permute-start | bytes 3145736 | tf_op jit(solution)/shard_map/ppermute | solution.py:417
  114.9 11.7 %copy-start.1 = (f32[512,128]{1,0:T(8,128)}, f32[512,128]{1,0:T(8,128)S(1)}, u32[]{:S(2)}) copy-start(f32[512,128]{1,0:T(8,128)S(1)} %get-tuple-element.178) | copy-start | bytes 786436
  114.9 23.9 %collective-permute-start.20 = (f32[256,384]{1,0:T(8,128)}, f32[256,384]{1,0:T(8,128)S(1)}, u32[]{:S(2)}, u32[]{:S(2)}) collective-permute-start(f32[256,384]{1,0:T(8,128)} %get-tuple-element.189), channel_id=1, source_target_pairs={{0,9},{2,11},{4,13},{6,15},{8,17},{9,0},{10,19},{11,2},{12,21},{13... | collective-permute-start | bytes 1179656 | tf_op jit(solution)/shard_map/ppermute | solution.py:417
  119.0 28.4 %collective-permute-start.16 = (f32[256,384]{1,0:T(8,128)S(1)}, f32[256,384]{1,0:T(8,128)S(1)}, u32[]{:S(2)}, u32[]{:S(2)}) collective-permute-start(f32[256,384]{1,0:T(8,128)S(1)} %get-tuple-element.177), channel_id=1, source_target_pairs={{0,5},{2,7},{5,0},{7,2},{8,13},{10,15},{13,8},{15,10},{16,21},{18,... | collective-permute-start | bytes 1179656 | tf_op jit(solution)/shard_map/ppermute | solution.py:417
  124.4 1.1 copy-start
  128.7 18.7 %collective-permute-start.19 = (f32[640,128]{1,0:T(8,128)S(1)}, f32[640,128]{1,0:T(8,128)S(1)}, u32[]{:S(2)}, u32[]{:S(2)}) collective-permute-start(f32[640,128]{1,0:T(8,128)S(1)} %get-tuple-element.186), channel_id=1, source_target_pairs={{0,13},{2,15},{8,21},{10,23},{13,0},{15,2},{16,29},{18,31},{21,8},... | collective-permute-start | bytes 983048 | tf_op jit(solution)/shard_map/ppermute | solution.py:417
  135.0 12.4 %collective-permute-start.17 = (f32[512,128]{1,0:T(8,128)}, f32[512,128]{1,0:T(8,128)S(1)}, u32[]{:S(2)}, u32[]{:S(2)}) collective-permute-start(f32[512,128]{1,0:T(8,128)} %copy-done.1), channel_id=1, source_target_pairs={{0,13},{2,15},{8,21},{10,23},{13,0},{15,2},{16,29},{18,31},{21,8},... | collective-permute-start | bytes 786440 | tf_op jit(solution)/shard_map/ppermute | solution.py:417
  136.9 7.0 %collective-permute-start.21 = (f32[128,384]{1,0:T(8,128)S(1)}, f32[128,384]{1,0:T(8,128)S(1)}, u32[]{:S(2)}, u32[]{:S(2)}) collective-permute-start(f32[128,384]{1,0:T(8,128)S(1)} %get-tuple-element.190), channel_id=1, source_target_pairs={{0,9},{2,11},{4,13},{6,15},{8,17},{9,0},{10,19},{11,2},{12,21},{13... | collective-permute-start | bytes 589832 | tf_op jit(solution)/shard_map/ppermute | solution.py:417
  138.9 8.6 %collective-permute-start.18 = (f32[128,384]{1,0:T(8,128)S(1)}, f32[128,384]{1,0:T(8,128)S(1)}, u32[]{:S(2)}, u32[]{:S(2)}) collective-permute-start(f32[128,384]{1,0:T(8,128)S(1)} %get-tuple-element.185), channel_id=1, source_target_pairs={{0,5},{2,7},{5,0},{7,2},{8,13},{10,15},{13,8},{15,10},{16,21},{18,... | collective-permute-start | bytes 589832 | tf_op jit(solution)/shard_map/ppermute | solution.py:417
  152.1 10.4 %collective-permute-start.22 = (f32[384,128]{1,0:T(8,128)S(1)}, f32[384,128]{1,0:T(8,128)S(1)}, u32[]{:S(2)}, u32[]{:S(2)}) collective-permute-start(f32[384,128]{1,0:T(8,128)S(1)} %get-tuple-element.194), channel_id=1, source_target_pairs={{0,4},{2,6},{5,3},{7,1},{8,12},{10,14},{13,11},{15,9},{16,20},{18,... | collective-permute-start | bytes 589832 | tf_op jit(solution)/shard_map/ppermute | solution.py:417
  157.0 6.0 %collective-permute-start.23 = (f32[384,128]{1,0:T(8,128)S(1)}, f32[384,128]{1,0:T(8,128)S(1)}, u32[]{:S(2)}, u32[]{:S(2)}) collective-permute-start(f32[384,128]{1,0:T(8,128)S(1)} %get-tuple-element.195), channel_id=1, source_target_pairs={{5,0},{7,2},{13,8},{15,10},{21,16},{23,18},{29,24},{31,26}} | collective-permute-start | bytes 589832 | tf_op jit(solution)/shard_map/ppermute | solution.py:417
  160.4 7.3 %collective-permute-start.24 = (f32[384,128]{1,0:T(8,128)S(1)}, f32[384,128]{1,0:T(8,128)S(1)}, u32[]{:S(2)}, u32[]{:S(2)}) collective-permute-start(f32[384,128]{1,0:T(8,128)S(1)} %get-tuple-element.196), channel_id=1, source_target_pairs={{0,8},{2,10},{4,12},{6,14},{8,16},{9,3},{10,18},{11,1},{12,20},{13... | collective-permute-start | bytes 589832 | tf_op jit(solution)/shard_map/ppermute | solution.py:417
  167.8 1.4 collective-permute-start.25
Sparse Core Ops, SparseCore 0:
  36.5 35.7 reduce-scatter.1

commit v4 on v2

--- a/solution.py
+++ b/solution.py
@@ -490,6 +490,7 @@
 
     moments = moments.reshape(1, 2, rows)
     moments = jnp.concatenate([moments, send(moments, "core")])
+    moments, tile0_own, tile0_send = stage((moments, tile0_own, tile0_send))
     moments = jnp.concatenate([moments, send(moments, "y")])
     centre = jnp.sum(moments[:, 0], axis=0) / moments.shape[0]
     offsets = moments[:, 0] - centre
@@ -500,8 +501,8 @@
     stats = jnp.concatenate([offsets, fill(8 - offsets.shape[0]), scale[None], fill(7)], axis=0)
     by_block = stats.reshape(16, -1, LANES).transpose(1, 0, 2).reshape(-1, LANES)
     side = jnp.concatenate([annot, by_block], axis=0)
-    got, own, raw, tile0_own, tile0_send, annot, stats, side = stage(
-        (got, own, raw, tile0_own, tile0_send, annot, stats, side)
+    got, own, tile0_own, tile0_send, annot, stats, side = stage(
+        (got, own, tile0_own, tile0_send, annot, stats, side)
     )
 
     pairs, old = [], []
@@ -518,13 +519,13 @@
         came_a = send(sent, "y")
         keep_db, sent, own, old = run_chunk(k, X, got[0], own, old)
         sent, came_a = stage((sent, came_a))
+        if k == last:
+            sent, came, pairs = stage((sent, came, pairs))
         pairs.append((keep_a, came_a, keep_db, send(sent, "y_meet")))
         if k < last:
             *held, came_db = pairs.pop()
             got, raw, old, own, pairs, held = stage((coming, raw, old, own, pairs, held))
             pairs.append((*held, came_db))
-        else:
-            came, old = stage((came, old))
     sides = [side, *came]
     early, late = range(EARLY), range(EARLY, n_parts)
     phases = [[parts[k] for k in chunk] for chunk in (early, late)]

time: 171 us -> 183 us (1.070)
  starting transfers between devices: 58.9 us -> 65.9 us
  Pallas kernels: 73.5 us -> 75.8 us
  waiting for transfers between devices: 28 us -> 29.9 us
    ppermute x28, starting transfers between devices: 58.9 us -> 65.9 us  [send(): return lax.ppermute(value, AXES, routes[name])]
    pallas_call x12, Pallas kernels: 73.5 us -> 75.8 us  [call(): pl.pallas_call(kernel, out_shape=[m(s, d) if m else jax.ShapeDtypeStruct(...]
    ppermute x28, waiting for transfers between devices: 28 us -> 29.9 us  [send(): return lax.ppermute(value, AXES, routes[name])]
  transfers between devices with their start and end apart: 28 -> 28, of which waited for: 13 -> 12; matrix products, arithmetic and copies ran while one was open for 2% -> 2% of each run, Pallas kernels for 40% -> 31%
where the time goes in v4:
time: 183 us; the launch traced here: 182 us
  Pallas kernels  75.8 us (41%)
  starting transfers between devices  65.9 us (36%)
  waiting for transfers between devices  29.9 us (16%)
  local copies, waits for them, and re-layouts  6.69 us (4%)
  other arithmetic  3.11 us (2%)
    pallas_call x12, Pallas kernels, call(): pl.pallas_call(kernel, out_shape=[m(s, d) if m else jax.ShapeDtypeStruct(...  75.8 us
    ppermute x28, starting transfers between devices, send(): return lax.ppermute(value, AXES, routes[name])  65.9 us
    ppermute x28, waiting for transfers between devices, send(): return lax.ppermute(value, AXES, routes[name])  29.9 us
  transfers between devices with their start and end apart: 28, of which 12 were waited for; matrix products, arithmetic and copies ran while one was open for 2% of the time, Pallas kernels for 31%

profile of v4, /device:TPU:23, one launch (start us, length us, event | category | flops | bytes accessed | tf_op | source)
XLA Modules:
  0.0 182.0 jit_solution(3277088807638039199)
XLA Ops:
  0.0 0.1 pad_add_fusion.role
  0.1 14.3 %shard_map.28 = (bf16[3,256,2048]{2,1,0:T(8,128)(2,1)}, bf16[3,256,2048]{2,1,0:T(8,128)(2,1)}, f32[2,192,768]{2,1,0:T(8,128)}, f32[2,192,768]{2,1,0:T(8,128)}, f...) custom-call(s32[2]{0:T(128)S(1)} %pad_add_fusion.role, f32[768,2048]{1,0:T(8,128)} %dose_hbm.1), custom_call_target="tpu_custom_call" | custom-call | flops 4831838208 | bytes 6291456 | tf_op jit(solution)/shard_map/pallas_call | solution.py:43
  14.4 3.3 %slice.13 = f32[2,128,2048]{2,1,0:T(8,128)} slice(f32[2,384,2048]{2,1,0:T(8,128)} %bitcast.26), slice={[0:2], [0:128], [0:2048]} | slice | bytes 4194304 | tf_op jit(solution)/shard_map/slice | solution.py:424
  17.7 0.7 collective-permute-start.5
  18.3 1.3 collective-permute-start.2
  19.6 3.2 %collective-permute-start.3 = (f32[2,128,2048]{2,1,0:T(8,128)}, f32[2,128,2048]{2,1,0:T(8,128)}, u32[]{:S(2)}, u32[]{:S(2)}) collective-permute-start(f32[2,128,2048]{2,1,0:T(8,128)} %slice.13), channel_id=1, source_target_pairs={{1,9},{3,11},{5,13},{7,15},{8,0},{9,17},{10,2},{11,19},{12,4},{13,... | collective-permute-start | bytes 6291464 | tf_op jit(solution)/shard_map/ppermute | solution.py:422
  22.9 0.5 collective-permute-start.4
  23.4 0.8 collective-permute-done.4
  24.2 1.4 add.88
  25.7 0.9 dynamic-slice_bitcast_fusion
  26.6 0.2 collective-permute-start.6
  26.8 1.3 collective-permute-start
  28.1 4.4 %collective-permute-start.1 = (f32[2,128,2048]{2,1,0:T(8,128)}, f32[2,128,2048]{2,1,0:T(8,128)}, u32[]{:S(2)}, u32[]{:S(2)}) collective-permute-start(f32[2,128,2048]{2,1,0:T(8,128)} %get-tuple-element.117), channel_id=1, source_target_pairs={{1,9},{3,11},{5,13},{7,15},{8,0},{9,17},{10,2},{11,19},{12,4},{13,... | collective-permute-start | bytes 6291464 | tf_op jit(solution)/shard_map/ppermute | solution.py:422
  32.5 0.1 pad.7.clone
  32.6 0.1 pad.9.clone
  32.9 0.1 maximum_maximum_fusion.1
  33.0 0.7 maximum_maximum_fusion.stats
  33.7 12.0 %collective-permute-done.2.raw = f32[2,128,2048]{2,1,0:T(8,128)S(1)} collective-permute-done((f32[2,128,2048]{2,1,0:T(8,128)}, f32[2,128,2048]{2,1,0:T(8,128)S(1)}, u32[]{:S(2)}, u32[]{:S(2)}) %collective-permute-start.2) | collective-permute-done | bytes 2097184 | tf_op jit(solution)/shard_map/ppermute | solution.py:422
  45.7 1.3 collective-permute-done.3.raw
  47.0 0.2 collective-permute-start.7
  47.3 7.3 %shard_map.29 = (f32[2,128,384]{2,1,0:T(8,128)}, f32[2,128,384]{2,1,0:T(8,128)}, bf16[2,3,256,2048]{3,2,1,0:T(8,128)(2,1)S(1)}, bf16[2,3,256,2048]{3,2,1,0:T(8,1...) custom-call(s32[2]{0:T(128)S(1)} %pad_add_fusion.role, ...), custom_call_target="tpu_custom_call" | custom-call | flops 2415919104 | bytes 3145728 | tf_op jit(solution)/shard_map/pallas_call | solution.py:43
  54.5 5.5 %collective-permute-done.7.tile_pair = f32[192,768]{1,0:T(8,128)S(1)} collective-permute-done((f32[192,768]{1,0:T(8,128)}, f32[192,768]{1,0:T(8,128)S(1)}, u32[]{:S(2)}, u32[]{:S(2)}) %collective-permute-start.7) | collective-permute-done | bytes 589856 | tf_op jit(solution)/shard_map/ppermute | solution.py:422
  60.0 0.2 collective-permute-start.8
  60.3 6.6 %shard_map.30 = (f32[2,128,512]{2,1,0:T(8,128)}, f32[2,128,512]{2,1,0:T(8,128)}, bf16[2,3,256,2048]{3,2,1,0:T(8,128)(2,1)S(1)}, bf16[2,3,256,2048]{3,2,1,0:T(8,128)(2,1)S(1)}) custom-call(s32[2]{0:T(128)S(1)} %pad_add_fusion.role, f32[2,128,2048]{2,1,0:T(8,128)S(1)} %collective-permute-done.2.raw, ...), custom_call_target="tpu_custom_call", output_to_operand_aliasing={{2}: (4, {}), {3}: (5, {})} | custom-call | flops 3221225472 | bytes 3145728 | tf_op jit(solution)/shard_map/pallas_call | solution.py:43
  66.9 1.1 collective-permute-done.8.refs_1_
  68.0 0.2 collective-permute-done.raw
  68.2 1.3 collective-permute-done.1.raw
  69.5 4.8 %collective-permute-start.10 = (f32[2,128,2048]{2,1,0:T(8,128)S(1)}, f32[2,128,2048]{2,1,0:T(8,128)S(1)}, u32[]{:S(2)}, u32[]{:S(2)}) collective-permute-start(f32[2,128,2048]{2,1,0:T(8,128)S(1)} %copy-done.13), channel_id=1, source_target_pairs={{1,9},{3,11},{5,13},{7,15},{8,0},{9,17},{10,2},{11,19},{12,4},{13,... | collective-permute-start | bytes 6291464 | tf_op jit(solution)/shard_map/ppermute | solution.py:422
  74.3 1.3 collective-permute-start.9
  75.6 1.3 collective-permute-start.14
  76.9 2.1 %collective-permute-start.11 = (f32[2,128,512]{2,1,0:T(8,128)}, f32[2,128,512]{2,1,0:T(8,128)S(1)}, u32[]{:S(2)}, u32[]{:S(2)}) collective-permute-start(f32[2,128,512]{2,1,0:T(8,128)} %get-tuple-element.158), channel_id=1, source_target_pairs={{0,2},{2,0},{5,7},{7,5},{8,10},{10,8},{13,15},{15,13},{16,18},{18,... | collective-permute-start | bytes 1572872 | tf_op jit(solution)/shard_map/ppermute | solution.py:422
  79.0 6.6 %shard_map.31 = (f32[2,128,384]{2,1,0:T(8,128)}, f32[2,128,384]{2,1,0:T(8,128)}, bf16[2,3,256,2048]{3,2,1,0:T(8,128)(2,1)S(1)}, bf16[2,3,256,2048]{3,2,1,0:T(8,128)(2,1)S(1)}) custom-call(s32[2]{0:T(128)S(1)} %pad_add_fusion.role, f32[2,128,2048]{2,1,0:T(8,128)} %collective-permute-done.1.raw, ...), custom_call_target="tpu_custom_call", output_to_operand_aliasing={{2}: (4, {}), {3}: (5, {})} | custom-call | flops 2415919104 | bytes 3145728 | tf_op jit(solution)/shard_map/pallas_call | solution.py:43
  85.6 1.3 collective-permute-start.12
  86.9 10.0 %shard_map.32 = (f32[2,128,768]{2,1,0:T(8,128)}, f32[2,128,768]{2,1,0:T(8,128)}, bf16[2,3,256,2048]{3,2,1,0:T(8,128)(2,1)S(1)}, bf16[2,3,256,2048]{3,2,1,0:T(8,128)(2,1)S(1)}) custom-call(s32[2]{0:T(128)S(1)} %pad_add_fusion.role, f32[2,128,2048]{2,1,0:T(8,128)} %collective-permute-done.raw, ...), custom_call_target="tpu_custom_call", output_to_operand_aliasing={{2}: (4, {}), {3}: (5, {})} | custom-call | flops 4831838208 | bytes 3145728 | tf_op jit(solution)/shard_map/pallas_call | solution.py:43
  96.9 1.9 %collective-permute-start.15 = (f32[864,128]{1,0:T(8,128)S(1)}, f32[864,128]{1,0:T(8,128)S(1)}, u32[]{:S(2)}, u32[]{:S(2)}) collective-permute-start(f32[864,128]{1,0:T(8,128)S(1)} %pad_maximum_fusion.refs_8_.refs_10_), channel_id=1, source_target_pairs={{1,9},{3,11},{5,13},{7,15},{8,0},{9,17},{10,2},{11,19},{12,4},{13,... | collective-permute-start | bytes 1327112 | tf_op jit(solution)/shard_map/ppermute | solution.py:422
  98.9 2.3 %collective-permute-start.16 = (f32[2,128,768]{2,1,0:T(8,128)}, f32[2,128,768]{2,1,0:T(8,128)S(1)}, u32[]{:S(2)}, u32[]{:S(2)}) collective-permute-start(f32[2,128,768]{2,1,0:T(8,128)} %get-tuple-element.183), channel_id=1, source_target_pairs={{0,2},{2,0},{5,7},{7,5},{8,10},{10,8},{13,15},{15,13},{16,18},{18,... | collective-permute-start | bytes 2359304 | tf_op jit(solution)/shard_map/ppermute | solution.py:422
  101.2 0.9 collective-permute-done.9.raw
  102.1 5.6 %shard_map.33 = (f32[2,128,384]{2,1,0:T(8,128)}, f32[2,128,384]{2,1,0:T(8,128)}, bf16[2,3,256,2048]{3,2,1,0:T(8,128)(2,1)S(1)}, bf16[2,3,256,2048]{3,2,1,0:T(8,128)(2,1)S(1)}) custom-call(s32[2]{0:T(128)S(1)} %pad_add_fusion.role, f32[2,128,2048]{2,1,0:T(8,128)S(1)} %collective-permute-done.10.raw, ...), custom_call_target="tpu_custom_call", output_to_operand_aliasing={{2}: (4, {}), {3}: (5, {})} | custom-call | flops 2415919104 | bytes 3145728 | tf_op jit(solution)/shard_map/pallas_call | solution.py:43
  107.7 0.4 collective-permute-start.13
  108.2 11.2 %shard_map.34 = (f32[2,128,1024]{2,1,0:T(8,128)}, f32[2,128,1024]{2,1,0:T(8,128)}, bf16[2,3,256,2048]{3,2,1,0:T(8,128)(2,1)S(1)}, bf16[2,3,256,2048]{3,2,1,0:T(8,128)(2,1)S(1)}) custom-call(s32[2]{0:T(128)S(1)} %pad_add_fusion.role, f32[2,128,2048]{2,1,0:T(8,128)S(1)} %collective-permute-done.9.raw, ...), custom_call_target="tpu_custom_call", output_to_operand_aliasing={{2}: (4, {}), {3}: (5, {})} | custom-call | flops 6442450944 | bytes 3145728 | tf_op jit(solution)/shard_map/pallas_call | solution.py:43
  119.3 0.1 collective-permute-done.13.refs_1_.refs_5_
  119.4 0.7 copy-done.10
  120.2 2.9 %collective-permute-start.17 = (f32[2,128,1024]{2,1,0:T(8,128)}, f32[2,128,1024]{2,1,0:T(8,128)}, u32[]{:S(2)}, u32[]{:S(2)}) collective-permute-start(f32[2,128,1024]{2,1,0:T(8,128)} %get-tuple-element.189), channel_id=1, source_target_pairs={{0,2},{2,0},{5,7},{7,5},{8,10},{10,8},{13,15},{15,13},{16,18},{18,... | collective-permute-start | bytes 3145736 | tf_op jit(solution)/shard_map/ppermute | solution.py:422
  123.1 3.0 %shard_map.35 = (f32[256,384]{1,0:T(8,128)}, f32[256,384]{1,0:T(8,128)S(1)}, f32[512,128]{1,0:T(8,128)S(1)}) custom-call(s32[2]{0:T(128)S(1)} %pad_add_fusion.role, f32[2,128,384]{2,1,0:T(8,128)} %get-tuple-element.190.refs_0_, f32[2,128,384]{2,1,0:T(8,128)} %copy-done.8, f32[2,128,512]{2,1,0:T(8,128)} %get-tuple-element.184.refs_2_.refs_0_, ...), custom_call_target="tpu_custom_call" | custom-call | flops 98304 | bytes 1179648 | tf_op jit(solution)/shard_map/pallas_call | solution.py:43
  126.1 0.7 copy-done.3
  126.9 0.7 copy-done.4
  127.6 2.9 %collective-permute-start.22 = (f32[256,384]{1,0:T(8,128)}, f32[256,384]{1,0:T(8,128)S(1)}, u32[]{:S(2)}, u32[]{:S(2)}) collective-permute-start(f32[256,384]{1,0:T(8,128)} %get-tuple-element.207), channel_id=1, source_target_pairs={{0,9},{2,11},{4,13},{6,15},{8,17},{9,0},{10,19},{11,2},{12,21},{13... | collective-permute-start | bytes 1179656 | tf_op jit(solution)/shard_map/ppermute | solution.py:422
  130.5 7.1 %collective-permute-start.18 = (f32[256,384]{1,0:T(8,128)}, f32[256,384]{1,0:T(8,128)S(1)}, u32[]{:S(2)}, u32[]{:S(2)}) collective-permute-start(f32[256,384]{1,0:T(8,128)} %copy-done.3), channel_id=1, source_target_pairs={{0,5},{2,7},{5,0},{7,2},{8,13},{10,15},{13,8},{15,10},{16,21},{18,... | collective-permute-start | bytes 1179656 | tf_op jit(solution)/shard_map/ppermute | solution.py:422
  137.6 0.1 constant_dynamic-slice_fusion.stats_rows
  137.7 1.1 shard_map.36
  138.8 2.1 %shard_map.37 = (f32[128,384]{1,0:T(8,128)S(1)}, f32[128,384]{1,0:T(8,128)S(1)}, f32[640,128]{1,0:T(8,128)S(1)}) custom-call(s32[2]{0:T(128)S(1)} %pad_add_fusion.role, f32[2,128,384]{2,1,0:T(8,128)} %get-tuple-element.201.refs_0_.refs_4_, f32[2,128,384]{2,1,0:T(8,128)} %copy-done.10, f32[2,128,1024]{2,1,0:T(8,128)} %get-tuple-element.188.refs_2_.refs_4_, ...), custom_call_target="tpu_custom_call" | custom-call | flops 49152 | bytes 589824 | tf_op jit(solution)/shard_map/pallas_call | solution.py:43
  140.9 6.3 %collective-permute-start.21 = (f32[640,128]{1,0:T(8,128)S(1)}, f32[640,128]{1,0:T(8,128)S(1)}, u32[]{:S(2)}, u32[]{:S(2)}) collective-permute-start(f32[640,128]{1,0:T(8,128)S(1)} %get-tuple-element.204), channel_id=1, source_target_pairs={{0,13},{2,15},{8,21},{10,23},{13,0},{15,2},{16,29},{18,31},{21,8},... | collective-permute-start | bytes 983048 | tf_op jit(solution)/shard_map/ppermute | solution.py:422
  147.2 1.9 %collective-permute-start.19 = (f32[512,128]{1,0:T(8,128)S(1)}, f32[512,128]{1,0:T(8,128)S(1)}, u32[]{:S(2)}, u32[]{:S(2)}) collective-permute-start(f32[512,128]{1,0:T(8,128)S(1)} %copy-done.5), channel_id=1, source_target_pairs={{0,13},{2,15},{8,21},{10,23},{13,0},{15,2},{16,29},{18,31},{21,8},... | collective-permute-start | bytes 786440 | tf_op jit(solution)/shard_map/ppermute | solution.py:422
  149.1 1.9 %collective-permute-start.23 = (f32[128,384]{1,0:T(8,128)S(1)}, f32[128,384]{1,0:T(8,128)S(1)}, u32[]{:S(2)}, u32[]{:S(2)}) collective-permute-start(f32[128,384]{1,0:T(8,128)S(1)} %get-tuple-element.208), channel_id=1, source_target_pairs={{0,9},{2,11},{4,13},{6,15},{8,17},{9,0},{10,19},{11,2},{12,21},{13... | collective-permute-start | bytes 589832 | tf_op jit(solution)/shard_map/ppermute | solution.py:422
  151.1 5.1 %collective-permute-start.20 = (f32[128,384]{1,0:T(8,128)S(1)}, f32[128,384]{1,0:T(8,128)S(1)}, u32[]{:S(2)}, u32[]{:S(2)}) collective-permute-start(f32[128,384]{1,0:T(8,128)S(1)} %get-tuple-element.203), channel_id=1, source_target_pairs={{0,5},{2,7},{5,0},{7,2},{8,13},{10,15},{13,8},{15,10},{16,21},{18,... | collective-permute-start | bytes 589832 | tf_op jit(solution)/shard_map/ppermute | solution.py:422
  156.2 3.4 %shard_map.38 = (f32[384,128]{1,0:T(8,128)S(1)}, f32[384,128]{1,0:T(8,128)S(1)}) custom-call(s32[2]{0:T(128)S(1)} %pad_add_fusion.role, f32[2,128,384]{2,1,0:T(8,128)} %get-tuple-element.190.refs_0_, f32[2,128,384]{2,1,0:T(8,128)} %copy-done.8, f32[2,128,384]{2,1,0:T(8,128)} %get-tuple-element.192.refs_4_.refs_2_, f32[2,128,384]{2,1,0:T(8,128)} %copy-done.9, ...), custom_call_target="tpu_custom_call" | custom-call | flops 226492416 | bytes 2359296 | tf_op jit(solution)/shard_map/pallas_call | solution.py:43
  159.6 4.7 %shard_map.39 = (f32[384,128]{1,0:T(8,128)S(1)}, f32[384,128]{1,0:T(8,128)S(1)}, f32[384,128]{1,0:T(8,128)S(1)}, f32[384,128]{1,0:T(8,128)S(1)}) custom-call(s32[2]{0:T(128)S(1)} %pad_add_fusion.role, f32[2,128,512]{2,1,0:T(8,128)} %get-tuple-element.184.refs_2_.refs_0_, f32[2,128,512]{2,1,0:T(8,128)} %copy-done.7, ...), custom_call_target="tpu_custom_call" | custom-call | flops 226492416 | bytes 2359296 | tf_op jit(solution)/shard_map/pallas_call | solution.py:43
  164.3 4.1 %collective-permute-start.24 = (f32[384,128]{1,0:T(8,128)S(1)}, f32[384,128]{1,0:T(8,128)S(1)}, u32[]{:S(2)}, u32[]{:S(2)}) collective-permute-start(f32[384,128]{1,0:T(8,128)S(1)} %get-tuple-element.212), channel_id=1, source_target_pairs={{0,4},{2,6},{5,3},{7,1},{8,12},{10,14},{13,11},{15,9},{16,20},{18,... | collective-permute-start | bytes 589832 | tf_op jit(solution)/shard_map/ppermute | solution.py:422
  168.5 4.1 %collective-permute-start.25 = (f32[384,128]{1,0:T(8,128)S(1)}, f32[384,128]{1,0:T(8,128)S(1)}, u32[]{:S(2)}, u32[]{:S(2)}) collective-permute-start(f32[384,128]{1,0:T(8,128)S(1)} %get-tuple-element.213), channel_id=1, source_target_pairs={{5,0},{7,2},{13,8},{15,10},{21,16},{23,18},{29,24},{31,26}} | collective-permute-start | bytes 589832 | tf_op jit(solution)/shard_map/ppermute | solution.py:422
  172.6 1.9 %collective-permute-start.26 = (f32[384,128]{1,0:T(8,128)S(1)}, f32[384,128]{1,0:T(8,128)S(1)}, u32[]{:S(2)}, u32[]{:S(2)}) collective-permute-start(f32[384,128]{1,0:T(8,128)S(1)} %get-tuple-element.214), channel_id=1, source_target_pairs={{0,8},{2,10},{4,12},{6,14},{8,16},{9,3},{10,18},{11,1},{12,20},{13... | collective-permute-start | bytes 589832 | tf_op jit(solution)/shard_map/ppermute | solution.py:422
  174.5 0.6 collective-permute-done.25
  175.2 4.7 %collective-permute-done.26 = f32[384,128]{1,0:T(8,128)S(1)} collective-permute-done((f32[384,128]{1,0:T(8,128)S(1)}, f32[384,128]{1,0:T(8,128)S(1)}, u32[]{:S(2)}, u32[]{:S(2)}) %collective-permute-start.26) | collective-permute-done | bytes 196640 | tf_op jit(solution)/shard_map/ppermute | solution.py:422
  180.1 1.3 collective-permute-done.27
  181.3 0.7 fusion
  (59 shorter events, 0.4 us)
Async XLA Ops:
  14.4 9.8 %copy-start.11 = (f32[2,192,768]{2,1,0:T(8,128)S(1)}, f32[2,192,768]{2,1,0:T(8,128)}, u32[]{:S(2)}) copy-start(f32[2,192,768]{2,1,0:T(8,128)} %get-tuple-element.122) | copy-start | bytes 3538948
  17.7 6.6 %collective-permute-start.5 = (f32[2,192,768]{2,1,0:T(8,128)}, f32[2,192,768]{2,1,0:T(8,128)}, u32[]{:S(2)}, u32[]{:S(2)}) collective-permute-start(f32[2,192,768]{2,1,0:T(8,128)} %get-tuple-element.123), channel_id=1, source_target_pairs={{0,1},{1,0},{2,3},{3,2},{4,5},{5,4},{6,7},{7,6},{8,9},{9,8},{10,11... | collective-permute-start | bytes 3538952 | tf_op jit(solution)/shard_map/ppermute | solution.py:422
  18.3 27.4 %collective-permute-start.2 = (f32[2,128,2048]{2,1,0:T(8,128)}, f32[2,128,2048]{2,1,0:T(8,128)S(1)}, u32[]{:S(2)}, u32[]{:S(2)}) collective-permute-start(f32[2,128,2048]{2,1,0:T(8,128)} %slice.13), channel_id=1, source_target_pairs={{1,5},{3,7},{4,0},{6,2},{9,13},{11,15},{12,8},{14,10},{17,21},{19,... | collective-permute-start | bytes 6291464 | tf_op jit(solution)/shard_map/ppermute | solution.py:422
  19.6 27.4 %collective-permute-start.3 = (f32[2,128,2048]{2,1,0:T(8,128)}, f32[2,128,2048]{2,1,0:T(8,128)}, u32[]{:S(2)}, u32[]{:S(2)}) collective-permute-start(f32[2,128,2048]{2,1,0:T(8,128)} %slice.13), channel_id=1, source_target_pairs={{1,9},{3,11},{5,13},{7,15},{8,0},{9,17},{10,2},{11,19},{12,4},{13,... | collective-permute-start | bytes 6291464 | tf_op jit(solution)/shard_map/ppermute | solution.py:422
  22.9 1.3 collective-permute-start.4
  23.4 9.3 %copy-start.12 = (s32[768,128]{1,0:T(8,128)S(1)}, s32[768,128]{1,0:T(8,128)}, u32[]{:S(2)}) copy-start(s32[768,128]{1,0:T(8,128)} %param.3) | copy-start | bytes 1179652
  26.6 6.1 %collective-permute-start.6 = (f32[2,2,768]{2,0,1:T(2,128)S(1)}, f32[2,2,768]{2,0,1:T(2,128)S(1)}, u32[]{:S(2)}, u32[]{:S(2)}) collective-permute-start(f32[2,2,768]{2,0,1:T(2,128)S(1)} %pad_maximum_fusion.2), channel_id=1, source_target_pairs={{0,2},{1,3},{2,0},{3,1},{4,6},{5,7},{6,4},{7,5},{8,10},{9,11},{10,... | collective-permute-start | bytes 36872 | tf_op jit(solution)/shard_map/ppermute | solution.py:422
  26.8 41.4 %collective-permute-start = (f32[2,128,2048]{2,1,0:T(8,128)}, f32[2,128,2048]{2,1,0:T(8,128)}, u32[]{:S(2)}, u32[]{:S(2)}) collective-permute-start(f32[2,128,2048]{2,1,0:T(8,128)} %get-tuple-element.117), channel_id=1, source_target_pairs={{1,5},{3,7},{4,0},{6,2},{9,13},{11,15},{12,8},{14,10},{17,21},{19,... | collective-permute-start | bytes 6291464 | tf_op jit(solution)/shard_map/ppermute | solution.py:422
  28.1 41.4 %collective-permute-start.1 = (f32[2,128,2048]{2,1,0:T(8,128)}, f32[2,128,2048]{2,1,0:T(8,128)}, u32[]{:S(2)}, u32[]{:S(2)}) collective-permute-start(f32[2,128,2048]{2,1,0:T(8,128)} %get-tuple-element.117), channel_id=1, source_target_pairs={{1,9},{3,11},{5,13},{7,15},{8,0},{9,17},{10,2},{11,19},{12,4},{13,... | collective-permute-start | bytes 6291464 | tf_op jit(solution)/shard_map/ppermute | solution.py:422
  47.0 13.0 %collective-permute-start.7 = (f32[192,768]{1,0:T(8,128)}, f32[192,768]{1,0:T(8,128)S(1)}, u32[]{:S(2)}, u32[]{:S(2)}) collective-permute-start(f32[192,768]{1,0:T(8,128)} %get-tuple-element.140), channel_id=1, source_target_pairs={{0,2},{1,3},{2,0},{3,1},{4,6},{5,7},{6,4},{7,5},{8,10},{9,11},{10,... | collective-permute-start | bytes 1769480 | tf_op jit(solution)/shard_map/ppermute | solution.py:422
  60.0 6.9 %copy-start = (f32[192,768]{1,0:T(8,128)}, f32[192,768]{1,0:T(8,128)S(1)}, u32[]{:S(2)}) copy-start(f32[192,768]{1,0:T(8,128)S(1)} %collective-permute-done.7.tile_pair) | copy-start | bytes 1769476
  60.0 8.0 %collective-permute-start.8 = (f32[2,128,384]{2,1,0:T(8,128)}, f32[2,128,384]{2,1,0:T(8,128)S(1)}, u32[]{:S(2)}, u32[]{:S(2)}) collective-permute-start(f32[2,128,384]{2,1,0:T(8,128)} %get-tuple-element.141), channel_id=1, source_target_pairs={{0,2},{1,3},{2,0},{3,1},{4,6},{5,7},{6,4},{7,5},{8,10},{9,11},{10,... | collective-permute-start | bytes 1179656 | tf_op jit(solution)/shard_map/ppermute | solution.py:422
  60.3 9.2 %copy-start.13 = (f32[2,128,2048]{2,1,0:T(8,128)S(1)}, f32[2,128,2048]{2,1,0:T(8,128)}, u32[]{:S(2)}) copy-start(f32[2,128,2048]{2,1,0:T(8,128)} %get-tuple-element.144) | copy-start | bytes 6291460
  68.0 17.6 %copy-start.8 = (f32[2,128,384]{2,1,0:T(8,128)}, f32[2,128,384]{2,1,0:T(8,128)S(1)}, u32[]{:S(2)}) copy-start(f32[2,128,384]{2,1,0:T(8,128)S(1)} %collective-permute-done.8.refs_1_) | copy-start | bytes 1179652
  69.5 31.7 %collective-permute-start.10 = (f32[2,128,2048]{2,1,0:T(8,128)S(1)}, f32[2,128,2048]{2,1,0:T(8,128)S(1)}, u32[]{:S(2)}, u32[]{:S(2)}) collective-permute-start(f32[2,128,2048]{2,1,0:T(8,128)S(1)} %copy-done.13), channel_id=1, source_target_pairs={{1,9},{3,11},{5,13},{7,15},{8,0},{9,17},{10,2},{11,19},{12,4},{13,... | collective-permute-start | bytes 6291464 | tf_op jit(solution)/shard_map/ppermute | solution.py:422
  74.3 27.8 %collective-permute-start.9 = (f32[2,128,2048]{2,1,0:T(8,128)S(1)}, f32[2,128,2048]{2,1,0:T(8,128)S(1)}, u32[]{:S(2)}, u32[]{:S(2)}) collective-permute-start(f32[2,128,2048]{2,1,0:T(8,128)S(1)} %copy-done.13), channel_id=1, source_target_pairs={{1,5},{3,7},{4,0},{6,2},{9,13},{11,15},{12,8},{14,10},{17,21},{19,... | collective-permute-start | bytes 6291464 | tf_op jit(solution)/shard_map/ppermute | solution.py:422
  75.6 43.9 %collective-permute-start.14 = (f32[864,128]{1,0:T(8,128)S(1)}, f32[864,128]{1,0:T(8,128)S(1)}, u32[]{:S(2)}, u32[]{:S(2)}) collective-permute-start(f32[864,128]{1,0:T(8,128)S(1)} %pad_maximum_fusion.refs_8_.refs_10_), channel_id=1, source_target_pairs={{1,5},{3,7},{4,0},{6,2},{9,13},{11,15},{12,8},{14,10},{17,21},{19,... | collective-permute-start | bytes 1327112 | tf_op jit(solution)/shard_map/ppermute | solution.py:422
  76.9 22.0 %collective-permute-start.11 = (f32[2,128,512]{2,1,0:T(8,128)}, f32[2,128,512]{2,1,0:T(8,128)S(1)}, u32[]{:S(2)}, u32[]{:S(2)}) collective-permute-start(f32[2,128,512]{2,1,0:T(8,128)} %get-tuple-element.158), channel_id=1, source_target_pairs={{0,2},{2,0},{5,7},{7,5},{8,10},{10,8},{13,15},{15,13},{16,18},{18,... | collective-permute-start | bytes 1572872 | tf_op jit(solution)/shard_map/ppermute | solution.py:422
  85.6 11.3 %collective-permute-start.12 = (f32[2,128,384]{2,1,0:T(8,128)}, f32[2,128,384]{2,1,0:T(8,128)S(1)}, u32[]{:S(2)}, u32[]{:S(2)}) collective-permute-start(f32[2,128,384]{2,1,0:T(8,128)} %get-tuple-element.161), channel_id=1, source_target_pairs={{0,2},{1,3},{2,0},{3,1},{4,6},{5,7},{6,4},{7,5},{8,10},{9,11},{10,... | collective-permute-start | bytes 1179656 | tf_op jit(solution)/shard_map/ppermute | solution.py:422
  96.9 10.8 %copy-start.9 = (f32[2,128,384]{2,1,0:T(8,128)}, f32[2,128,384]{2,1,0:T(8,128)S(1)}, u32[]{:S(2)}) copy-start(f32[2,128,384]{2,1,0:T(8,128)S(1)} %collective-permute-done.12.refs_5_.refs_3_) | copy-start | bytes 1179652
  96.9 22.5 %collective-permute-start.15 = (f32[864,128]{1,0:T(8,128)S(1)}, f32[864,128]{1,0:T(8,128)S(1)}, u32[]{:S(2)}, u32[]{:S(2)}) collective-permute-start(f32[864,128]{1,0:T(8,128)S(1)} %pad_maximum_fusion.refs_8_.refs_10_), channel_id=1, source_target_pairs={{1,9},{3,11},{5,13},{7,15},{8,0},{9,17},{10,2},{11,19},{12,4},{13,... | collective-permute-start | bytes 1327112 | tf_op jit(solution)/shard_map/ppermute | solution.py:422
  98.9 8.8 %copy-start.7 = (f32[2,128,512]{2,1,0:T(8,128)}, f32[2,128,512]{2,1,0:T(8,128)S(1)}, u32[]{:S(2)}) copy-start(f32[2,128,512]{2,1,0:T(8,128)S(1)} %collective-permute-done.11.refs_3_.refs_1_) | copy-start | bytes 1572868
  98.9 20.5 %collective-permute-start.16 = (f32[2,128,768]{2,1,0:T(8,128)}, f32[2,128,768]{2,1,0:T(8,128)S(1)}, u32[]{:S(2)}, u32[]{:S(2)}) collective-permute-start(f32[2,128,768]{2,1,0:T(8,128)} %get-tuple-element.183), channel_id=1, source_target_pairs={{0,2},{2,0},{5,7},{7,5},{8,10},{10,8},{13,15},{15,13},{16,18},{18,... | collective-permute-start | bytes 2359304 | tf_op jit(solution)/shard_map/ppermute | solution.py:422
  107.7 11.7 %collective-permute-start.13 = (f32[2,128,384]{2,1,0:T(8,128)}, f32[2,128,384]{2,1,0:T(8,128)S(1)}, u32[]{:S(2)}, u32[]{:S(2)}) collective-permute-start(f32[2,128,384]{2,1,0:T(8,128)} %get-tuple-element.173), channel_id=1, source_target_pairs={{0,2},{1,3},{2,0},{3,1},{4,6},{5,7},{6,4},{7,5},{8,10},{9,11},{10,... | collective-permute-start | bytes 1179656 | tf_op jit(solution)/shard_map/ppermute | solution.py:422
  119.3 18.3 %copy-start.2 = (f32[16,768]{1,0:T(8,128)S(1)}, f32[16,768]{1,0:T(8,128)}, u32[]{:S(2)}) copy-start(f32[16,768]{1,0:T(8,128)} %maximum_maximum_fusion.stats) | copy-start | bytes 147460
  119.3 18.4 %copy-start.1 = (f32[192,768]{1,0:T(8,128)S(1)}, f32[192,768]{1,0:T(8,128)}, u32[]{:S(2)}) copy-start(f32[192,768]{1,0:T(8,128)} %copy-done) | copy-start | bytes 1769476
  119.4 0.8 copy-start.10
  120.2 2.9 %copy-start.6 = (f32[2,128,768]{2,1,0:T(8,128)}, f32[2,128,768]{2,1,0:T(8,128)S(1)}, u32[]{:S(2)}) copy-start(f32[2,128,768]{2,1,0:T(8,128)S(1)} %collective-permute-done.16.refs_7_.refs_3_) | copy-start | bytes 2359300
  120.2 18.6 %collective-permute-start.17 = (f32[2,128,1024]{2,1,0:T(8,128)}, f32[2,128,1024]{2,1,0:T(8,128)}, u32[]{:S(2)}, u32[]{:S(2)}) collective-permute-start(f32[2,128,1024]{2,1,0:T(8,128)} %get-tuple-element.189), channel_id=1, source_target_pairs={{0,2},{2,0},{5,7},{7,5},{8,10},{10,8},{13,15},{15,13},{16,18},{18,... | collective-permute-start | bytes 3145736 | tf_op jit(solution)/shard_map/ppermute | solution.py:422
  126.1 0.7 copy-start.3
  126.9 0.7 copy-start.4
  127.6 23.5 %collective-permute-start.22 = (f32[256,384]{1,0:T(8,128)}, f32[256,384]{1,0:T(8,128)S(1)}, u32[]{:S(2)}, u32[]{:S(2)}) collective-permute-start(f32[256,384]{1,0:T(8,128)} %get-tuple-element.207), channel_id=1, source_target_pairs={{0,9},{2,11},{4,13},{6,15},{8,17},{9,0},{10,19},{11,2},{12,21},{13... | collective-permute-start | bytes 1179656 | tf_op jit(solution)/shard_map/ppermute | solution.py:422
  130.5 16.7 %copy-start.5 = (f32[512,128]{1,0:T(8,128)S(1)}, f32[512,128]{1,0:T(8,128)}, u32[]{:S(2)}) copy-start(f32[512,128]{1,0:T(8,128)} %copy-done.4) | copy-start | bytes 786436
  130.5 29.1 %collective-permute-start.18 = (f32[256,384]{1,0:T(8,128)}, f32[256,384]{1,0:T(8,128)S(1)}, u32[]{:S(2)}, u32[]{:S(2)}) collective-permute-start(f32[256,384]{1,0:T(8,128)} %copy-done.3), channel_id=1, source_target_pairs={{0,5},{2,7},{5,0},{7,2},{8,13},{10,15},{13,8},{15,10},{16,21},{18,... | collective-permute-start | bytes 1179656 | tf_op jit(solution)/shard_map/ppermute | solution.py:422
  140.9 18.7 %collective-permute-start.21 = (f32[640,128]{1,0:T(8,128)S(1)}, f32[640,128]{1,0:T(8,128)S(1)}, u32[]{:S(2)}, u32[]{:S(2)}) collective-permute-start(f32[640,128]{1,0:T(8,128)S(1)} %get-tuple-element.204), channel_id=1, source_target_pairs={{0,13},{2,15},{8,21},{10,23},{13,0},{15,2},{16,29},{18,31},{21,8},... | collective-permute-start | bytes 983048 | tf_op jit(solution)/shard_map/ppermute | solution.py:422
  147.2 12.4 %collective-permute-start.19 = (f32[512,128]{1,0:T(8,128)S(1)}, f32[512,128]{1,0:T(8,128)S(1)}, u32[]{:S(2)}, u32[]{:S(2)}) collective-permute-start(f32[512,128]{1,0:T(8,128)S(1)} %copy-done.5), channel_id=1, source_target_pairs={{0,13},{2,15},{8,21},{10,23},{13,0},{15,2},{16,29},{18,31},{21,8},... | collective-permute-start | bytes 786440 | tf_op jit(solution)/shard_map/ppermute | solution.py:422
  149.1 7.0 %collective-permute-start.23 = (f32[128,384]{1,0:T(8,128)S(1)}, f32[128,384]{1,0:T(8,128)S(1)}, u32[]{:S(2)}, u32[]{:S(2)}) collective-permute-start(f32[128,384]{1,0:T(8,128)S(1)} %get-tuple-element.208), channel_id=1, source_target_pairs={{0,9},{2,11},{4,13},{6,15},{8,17},{9,0},{10,19},{11,2},{12,21},{13... | collective-permute-start | bytes 589832 | tf_op jit(solution)/shard_map/ppermute | solution.py:422
  151.1 8.6 %collective-permute-start.20 = (f32[128,384]{1,0:T(8,128)S(1)}, f32[128,384]{1,0:T(8,128)S(1)}, u32[]{:S(2)}, u32[]{:S(2)}) collective-permute-start(f32[128,384]{1,0:T(8,128)S(1)} %get-tuple-element.203), channel_id=1, source_target_pairs={{0,5},{2,7},{5,0},{7,2},{8,13},{10,15},{13,8},{15,10},{16,21},{18,... | collective-permute-start | bytes 589832 | tf_op jit(solution)/shard_map/ppermute | solution.py:422
  164.3 10.2 %collective-permute-start.24 = (f32[384,128]{1,0:T(8,128)S(1)}, f32[384,128]{1,0:T(8,128)S(1)}, u32[]{:S(2)}, u32[]{:S(2)}) collective-permute-start(f32[384,128]{1,0:T(8,128)S(1)} %get-tuple-element.212), channel_id=1, source_target_pairs={{0,4},{2,6},{5,3},{7,1},{8,12},{10,14},{13,11},{15,9},{16,20},{18,... | collective-permute-start | bytes 589832 | tf_op jit(solution)/shard_map/ppermute | solution.py:422
  168.5 6.7 %collective-permute-start.25 = (f32[384,128]{1,0:T(8,128)S(1)}, f32[384,128]{1,0:T(8,128)S(1)}, u32[]{:S(2)}, u32[]{:S(2)}) collective-permute-start(f32[384,128]{1,0:T(8,128)S(1)} %get-tuple-element.213), channel_id=1, source_target_pairs={{5,0},{7,2},{13,8},{15,10},{21,16},{23,18},{29,24},{31,26}} | collective-permute-start | bytes 589832 | tf_op jit(solution)/shard_map/ppermute | solution.py:422
  172.6 7.3 %collective-permute-start.26 = (f32[384,128]{1,0:T(8,128)S(1)}, f32[384,128]{1,0:T(8,128)S(1)}, u32[]{:S(2)}, u32[]{:S(2)}) collective-permute-start(f32[384,128]{1,0:T(8,128)S(1)} %get-tuple-element.214), channel_id=1, source_target_pairs={{0,8},{2,10},{4,12},{6,14},{8,16},{9,3},{10,18},{11,1},{12,20},{13... | collective-permute-start | bytes 589832 | tf_op jit(solution)/shard_map/ppermute | solution.py:422
  180.0 1.4 collective-permute-start.27
